TPU v7x, 512 devices: a whole 4x4x16 slice. The times are simulated.
512 devices in a mesh: head: 8 (over x, core), expert: 64 (over y, z).
Axes of the slice: x: 4, y: 4, z: 16, core: 2. Of those that a mesh axis runs over, the one named last changes fastest.
Arguments:
- out_grad: bfloat16 [16384, 2048], P('expert'), may hold values from -6 to 6
- expert_ids: int32 [16384, 8], P('expert'), may hold values from 0 to 63, all different within a row; in each aligned block of 256 rows (0 to 255, 256 to 511, ...) at most 40 rows name the same one
- chosen_logits: float32 [16384, 8], P('expert'), may hold values from -6 to 6
- down_weight: bfloat16 [64, 768, 2048], P('expert', 'head'), may hold values from -0.21875 to 0.21875
- saved_hidden: bfloat16 [64, 64, 40, 768], P('expert', None, None, 'head'), may hold values from -0.29882812 to 0.29882812
- router_weight: bfloat16 [2048, 64], P('head'), may hold values from -6 to 6
Outputs:
- router_input_grad: bfloat16 [16384, 2048], P('expert', 'head')
- weight_grad: float32 [16384, 8], P('expert')
Inputs may be any that keep to these rules, and one draw needn't show every extreme that they name: `expert_ids`: each row names 8 different experts. Among the 256 rows of one expert index no expert is named more than 40 times, and in every draw some expert index names some expert exactly 40 times.
All inputs are finite; a program needn't handle non-finite values.
Results may differ from a plain program's by a relative error of at most 0.012.
Values may be sent and summed in bfloat16 or wider, within the bound.
No kernel may reach another device: no remote copies, remote signals or barrier semaphores. Data moves between devices by JAX's collectives and lax.ppermute only.
A program may use at most 64 MiB of HBM per device.

v0:
```python
import jax
import jax.numpy as jnp
from jax import lax
from jax.sharding import PartitionSpec as P


def slot_numbers(block_ids, count):
    onehot = (block_ids[:, :, None] == jnp.arange(count, dtype=jnp.int32)[None, None, :]).astype(
        jnp.float32
    )
    hits = jnp.sum(onehot, axis=1)
    rows = block_ids.shape[0]
    lower = (
        jnp.arange(rows, dtype=jnp.int32)[:, None] > jnp.arange(rows, dtype=jnp.int32)[None, :]
    ).astype(jnp.float32)
    before = jnp.dot(lower, hits, precision=lax.Precision.HIGHEST)
    return jnp.sum(before[:, None, :] * onehot, axis=2).astype(jnp.int32)


def body(out_grad, expert_ids, chosen_logits, down_weight, saved_hidden, router_weight):
    experts = lax.axis_size("expert")
    capacity = saved_hidden.shape[2]
    tok_rows = out_grad.shape[0]
    chosen = expert_ids.shape[1]
    model_width = out_grad.shape[1]
    slots = slot_numbers(expert_ids, experts)
    position = (expert_ids * capacity + slots).reshape(-1)
    marks = jnp.arange(tok_rows * chosen, dtype=jnp.int32) // chosen + 1
    owner = jnp.zeros((experts * capacity,), jnp.int32).at[position].set(marks)
    picked = out_grad[jnp.maximum(owner - 1, 0)]
    outgoing = jnp.where((owner > 0)[:, None], picked, jnp.zeros((), out_grad.dtype))
    outgoing = outgoing.reshape(experts, capacity, model_width)
    received = lax.all_to_all(outgoing, "expert", split_axis=0, concat_axis=0, tiled=True)
    inner = jnp.einsum("scd,fd->scf", received, down_weight[0], preferred_element_type=jnp.float32)
    partial_grads = jnp.sum(inner * saved_hidden[0].astype(jnp.float32), axis=2)
    slot_grads = lax.psum(partial_grads, "head")
    returned = lax.all_to_all(slot_grads, "expert", split_axis=0, concat_axis=0, tiled=True)
    weight_grad = returned.reshape(-1)[position].reshape(tok_rows, chosen)
    raised = jnp.exp(chosen_logits)
    probs = raised / jnp.sum(raised, axis=1, keepdims=True)
    logit_grad = probs * (weight_grad - jnp.sum(probs * weight_grad, axis=1, keepdims=True))
    onehot = (expert_ids[:, :, None] == jnp.arange(experts, dtype=jnp.int32)[None, None, :]).astype(
        jnp.float32
    )
    dense_grad = jnp.sum(logit_grad[:, :, None] * onehot, axis=1).astype(jnp.bfloat16)
    router_input_grad = jnp.einsum(
        "te,de->td", dense_grad, router_weight, preferred_element_type=jnp.float32
    ).astype(jnp.bfloat16)
    return (router_input_grad, weight_grad)


def solution(mesh):
    return jax.shard_map(
        body,
        mesh=mesh,
        in_specs=(
            P("expert", None),
            P("expert", None),
            P("expert", None),
            P("expert", "head", None),
            P("expert", None, None, "head"),
            P("head", None),
        ),
        out_specs=(P("expert", "head"), P("expert", None)),
        check_vma=False,
    )
```

profile of v0, /device:TPU:1, one launch (start us, length us, event | category | flops | bytes accessed | tf_op | source)
XLA Modules:
  0.0 576.0 jit_solution(11736479255491204030)
XLA Ops:
  0.6 0.0 copy-start
  0.7 0.8 convert_reduce_fusion
  1.5 0.3 fusion.2
  1.8 0.8 select_reduce_fusion.1
  2.6 0.7 convert_add_fusion
  3.3 0.1 copy.34
  3.4 0.1 reshape.59
  3.5 8.1 %scatter_custom_fusion = s32[2560]{0:T(1024)S(1)} fusion(s32[2048]{0:T(1024)S(1)} %bitcast.16, s32[2048]{0:T(1024)S(1)} %fusion.4, s32[]{:T(128)} %constant.27.clone.1), kind=kCustom, calls=%fused_computation.32 | custom fusion | bytes 10244 | tf_op jit(solution)/shard_map/scatter | solution.py:29
  11.6 0.1 broadcast_in_dim.16
  11.7 0.0 copy-done
  11.8 10.8 %gather_fusion = bf16[2560,2048]{1,0:T(8,128)(2,1)} fusion(bf16[256,2048]{1,0:T(8,128)(2,1)S(1)} %copy-done, s32[3072]{0:T(1024)S(1)} %pad_clamp_fusion), kind=kCustom, calls=%fused_computation | custom fusion | bytes 20981760 | tf_op jit(solution)/shard_map/gather | solution.py:30
  22.6 10.0 %broadcast_select_fusion = bf16[64,40,2048]{2,1,0:T(8,128)(2,1)} fusion(bf16[64,40,2048]{2,1,0:T(8,128)(2,1)} %bitcast.14, pred[64,40]{1,0:T(8,128)(4,1)S(1)} %broadcast_in_dim.16), kind=kLoop, calls=%fused_computation.3 | loop fusion | flops 5242880 | bytes 20974080 | tf_op jit(solution)/shard_map/jit(_where)/select_n | solution.py:31
  32.6 19.6 %all-to-all-start = ((bf16[64,40,2048]{2,1,0:T(8,128)(2,1)}), bf16[64,40,2048]{2,1,0:T(8,128)(2,1)}, u32[]{:S(2)}, u32[]{:S(2)}) async-start(bf16[64,40,2048]{2,1,0:T(8,128)(2,1)} %broadcast_select_fusion), calls=%async_computation | async-start | bytes 20971520 | tf_op jit(solution)/shard_map/all_to_all | solution.py:33
  52.2 0.0 copy-start.3
  52.3 0.0 copy-start.1
  52.3 0.0 copy-start.4
  52.3 455.6 %all-to-all-done = bf16[64,40,2048]{2,1,0:T(8,128)(2,1)} async-done(((bf16[64,40,2048]{2,1,0:T(8,128)(2,1)}), bf16[64,40,2048]{2,1,0:T(8,128)(2,1)}, u32[]{:S(2)}, u32[]{:S(2)}) %all-to-all-start) | async-done | bytes 10485792 | tf_op jit(solution)/shard_map/all_to_all | solution.py:33
  507.8 0.0 copy-done.5
  507.8 0.0 copy-done.6
  507.9 7.1 %fusion = f32[64,40]{1,0:T(8,128)S(1)} fusion(bf16[64,40,2048]{2,1,0:T(8,128)(2,1)} %all-to-all-done, bf16[1,64,40,96]{3,2,1,0:T(8,128)(2,1)S(1)} %copy-done.5, bf16[1,96,2048]{2,1,0:T(8,128)(2,1)S(1)} %copy-done.6), kind=kOutput, calls=%fused_computation.5 | convolution fusion | flops 1007367680 | bytes 11380736 | tf_op jit(solution)/shard_map/scd,fd->scf/dot_general | solution.py:34
  514.9 23.4 %psum.7 = f32[64,1,40]{2,1,0:T(1,128)} all-reduce(f32[64,1,40]{2,1,0:T(1,128)S(1)} %bitcast.15), channel_id=1, replica_groups=mesh['head'=8,'expert'=64] {'head'}, use_global_device_ids=true, to_apply=%region_5.6 | all-reduce | flops 2560 | bytes 20480 | tf_op jit(solution)/shard_map/psum | solution.py:36
  538.3 10.2 %all-to-all-start.1 = ((f32[64,1,40]{2,1,0:T(1,128)}), f32[64,1,40]{2,1,0:T(1,128)S(1)}, u32[]{:S(2)}, u32[]{:S(2)}) async-start(f32[64,1,40]{2,1,0:T(1,128)} %psum.7), calls=%async_computation.1 | async-start | bytes 65536 | tf_op jit(solution)/shard_map/all_to_all | solution.py:37
  548.5 0.0 copy-done.3
  548.5 13.2 %all-to-all-done.1 = f32[64,1,40]{2,1,0:T(1,128)S(1)} async-done(((f32[64,1,40]{2,1,0:T(1,128)}), f32[64,1,40]{2,1,0:T(1,128)S(1)}, u32[]{:S(2)}, u32[]{:S(2)}) %all-to-all-start.1) | async-done | bytes 10272 | tf_op jit(solution)/shard_map/all_to_all | solution.py:37
  561.7 0.5 broadcast.79
  562.2 0.7 reduce.3
  562.9 0.1 reshape.60
  563.0 11.8 %gather_fusion.1 = f32[2048]{0:T(1024)S(1)} fusion(f32[2560]{0:T(1024)S(1)} %reshape.60, s32[2048]{0:T(1024)S(1)} %broadcast_clamp_fusion), kind=kCustom, calls=%fused_computation.1 | custom fusion | bytes 24576 | tf_op jit(solution)/shard_map/gather | solution.py:38
  574.8 0.1 reshape.61
  574.9 0.1 copy.36
  575.1 0.1 select_reduce_fusion
  575.1 0.9 convolution_convert_fusion
  (15 shorter events, 0.1 us)
Async XLA Ops:
  0.6 11.1 %copy-start = (bf16[256,2048]{1,0:T(8,128)(2,1)S(1)}, bf16[256,2048]{1,0:T(8,128)(2,1)}, u32[]{:S(2)}) copy-start(bf16[256,2048]{1,0:T(8,128)(2,1)} %param.6) | copy-start | bytes 3145732
  32.6 475.3 %copy-start.5 = (bf16[1,64,40,96]{3,2,1,0:T(8,128)(2,1)S(1)}, bf16[1,64,40,96]{3,2,1,0:T(8,128)(2,1)}, u32[]{:S(2)}) copy-start(bf16[1,64,40,96]{3,2,1,0:T(8,128)(2,1)} %param.10) | copy-start | bytes 1474564
  32.6 475.3 %copy-start.6 = (bf16[1,96,2048]{2,1,0:T(8,128)(2,1)S(1)}, bf16[1,96,2048]{2,1,0:T(8,128)(2,1)}, u32[]{:S(2)}) copy-start(bf16[1,96,2048]{2,1,0:T(8,128)(2,1)} %param.9) | copy-start | bytes 1179652
  32.6 475.3 %all-to-all-start = ((bf16[64,40,2048]{2,1,0:T(8,128)(2,1)}), bf16[64,40,2048]{2,1,0:T(8,128)(2,1)}, u32[]{:S(2)}, u32[]{:S(2)}) async-start(bf16[64,40,2048]{2,1,0:T(8,128)(2,1)} %broadcast_select_fusion), calls=%async_computation | async-start | bytes 20971520 | tf_op jit(solution)/shard_map/all_to_all | solution.py:33
  52.2 496.2 %copy-start.3 = (f32[256,8]{0,1:T(8,128)S(1)}, f32[256,8]{0,1:T(8,128)}, u32[]{:S(2)}) copy-start(f32[256,8]{0,1:T(8,128)} %param.8) | copy-start | bytes 24580
  52.3 522.8 %copy-start.1 = (s32[256,8]{0,1:T(8,128)S(1)}, s32[256,8]{0,1:T(8,128)}, u32[]{:S(2)}) copy-start(s32[256,8]{0,1:T(8,128)} %param.7) | copy-start | bytes 24580
  52.3 522.9 %copy-start.4 = (bf16[256,64]{0,1:T(8,128)(2,1)S(1)}, bf16[256,64]{0,1:T(8,128)(2,1)}, u32[]{:S(2)}) copy-start(bf16[256,64]{0,1:T(8,128)(2,1)} %param.11) | copy-start | bytes 98308
  538.3 23.4 %all-to-all-start.1 = ((f32[64,1,40]{2,1,0:T(1,128)}), f32[64,1,40]{2,1,0:T(1,128)S(1)}, u32[]{:S(2)}, u32[]{:S(2)}) async-start(f32[64,1,40]{2,1,0:T(1,128)} %psum.7), calls=%async_computation.1 | async-start | bytes 65536 | tf_op jit(solution)/shard_map/all_to_all | solution.py:37
  575.0 1.0 copy-start.2
where the time goes:
time: 579 us; the launch traced here: 576 us
  waiting for transfers between devices  469 us (81%)
  local copies, waits for them, and re-layouts  31.8 us (5%)
  starting transfers between devices  29.9 us (5%)
  blocking collectives  23.4 us (4%)
  other arithmetic  13.2 us (2%)
  matrix products  8.2 us (1%)
    all_to_all x1, waiting for transfers between devices, body(): lax.all_to_all(outgoing, 'expert', split_axis=0, concat_axis=0, tiled=True)  456 us
    psum x1, blocking collectives, body(): slot_grads = lax.psum(partial_grads, 'head')  23.4 us
    all_to_all x1, starting transfers between devices, body(): lax.all_to_all(outgoing, 'expert', split_axis=0, concat_axis=0, tiled=True)  19.6 us
    all_to_all x1, waiting for transfers between devices, body(): lax.all_to_all(slot_grads, 'expert', split_axis=0, concat_axis=0, tiled=T...  13.2 us
    gather x1, local copies, waits for them, and re-layouts, body(): weight_grad = returned.reshape(-1)[position].reshape(tok_rows, chosen)  11.8 us
  transfers between devices with their start and end apart: 2, of which 2 were waited for; matrix products, arithmetic and copies ran while one was open for 0% of the time, Pallas kernels for 0%

commit v1 on v0

v1 whole, which is shorter than its diff:
```python
import jax
import jax.numpy as jnp
from jax import lax
from jax.experimental import pallas as pl
from jax.experimental.pallas import tpu as pltpu
from jax.sharding import Mesh, PartitionSpec as P

X, CORES, Y, ZH, ZL = 4, 2, 4, 4, 4
EXPERT = ("y", "zh", "zl")
HEAD = ("x", "core")
TOK = 256
CAP = 40
TOPK = 8
EXPERTS = 64
DS = 256
NEAR = Y * ZL
F32 = jnp.float32
BF16 = jnp.bfloat16


def select_kernel(zh_ref, blocks_ref, out_ref, picked):
    zh = zh_ref[0]
    j = lax.broadcasted_iota(jnp.int32, (NEAR, TOK), 0)
    expert = ((j // ZL) * (ZH * ZL) + zh * ZL + j % ZL).astype(F32)
    hits = []
    for b in range(ZH):
        ids = blocks_ref[b, TOK : TOK + 16, :].astype(F32)
        hit = jnp.zeros((NEAR, TOK), F32)
        for k in range(TOPK):
            hit = hit + (ids[k : k + 1, :] == expert).astype(F32)
        hits.append(hit)
    hits = jnp.concatenate(hits, axis=0)
    earlier = lax.broadcasted_iota(jnp.int32, (TOK, TOK), 0) < lax.broadcasted_iota(
        jnp.int32, (TOK, TOK), 1
    )
    before = jnp.dot(hits.astype(BF16), earlier.astype(BF16), preferred_element_type=F32)
    key = jnp.where(hits > 0, before, -1.0)
    slot = lax.broadcasted_iota(jnp.int32, (CAP, TOK), 0).astype(F32)
    for b in range(ZH):
        pick = jnp.concatenate(
            [(key[b * NEAR + e : b * NEAR + e + 1, :] == slot).astype(F32) for e in range(NEAR)],
            axis=0,
        )
        picked[b] = jnp.dot(
            pick.astype(BF16), blocks_ref[b, 0:TOK, :], preferred_element_type=F32
        )
    for e in range(NEAR):
        rows = [picked[b, e * CAP : (e + 1) * CAP, :] for b in range(ZH)]
        out_ref[e] = jnp.concatenate(rows, axis=0).astype(BF16)


def select_rows(zh, blocks):
    return pl.pallas_call(
        select_kernel,
        out_shape=jax.ShapeDtypeStruct((NEAR, ZH * CAP, DS), BF16),
        in_specs=[
            pl.BlockSpec(memory_space=pltpu.SMEM),
            pl.BlockSpec(memory_space=pltpu.VMEM),
        ],
        out_specs=pl.BlockSpec(memory_space=pltpu.VMEM),
        scratch_shapes=[pltpu.VMEM((ZH, NEAR * CAP, DS), F32)],
        compiler_params=pltpu.CompilerParams(vmem_limit_bytes=32 << 20),
    )(zh, blocks)


def plan_kernel(ids_ref, logits_ref, key_ref, probs_ref):
    ids = ids_ref[...]
    raised = jnp.exp(logits_ref[...])
    probs = raised / jnp.sum(raised, axis=1, keepdims=True)
    expert = lax.broadcasted_iota(jnp.int32, (TOK, EXPERTS), 1)
    hits = jnp.zeros((TOK, EXPERTS), F32)
    spread = jnp.zeros((TOK, EXPERTS), F32)
    for k in range(TOPK):
        mine = ids[:, k : k + 1] == expert
        hits = hits + mine.astype(F32)
        spread = spread + jnp.where(mine, probs[:, k : k + 1], 0.0)
    earlier = lax.broadcasted_iota(jnp.int32, (TOK, TOK), 0) > lax.broadcasted_iota(
        jnp.int32, (TOK, TOK), 1
    )
    before = jnp.dot(earlier.astype(BF16), hits.astype(BF16), preferred_element_type=F32)
    key_ref[...] = jnp.where(hits > 0, before, -1.0)
    probs_ref[...] = spread


def plan(ids, logits):
    shape = jax.ShapeDtypeStruct((TOK, EXPERTS), F32)
    return pl.pallas_call(plan_kernel, out_shape=(shape, shape))(ids, logits)


def final_kernel(back_ref, key_ref, probs_ref, ids_ref, router_ref, grad_ref, weight_ref):
    key = key_ref[...]
    probs = probs_ref[...]
    dense = jnp.zeros((TOK, EXPERTS), F32)
    for c in range(CAP):
        dense = jnp.where(key == float(c), back_ref[c : c + 1, :], dense)
    mean = jnp.sum(probs * dense, axis=1, keepdims=True)
    logit = (probs * (dense - mean)).astype(BF16)
    grad_ref[...] = lax.dot_general(
        logit, router_ref[...], (((1,), (1,)), ((), ())), preferred_element_type=F32
    ).astype(BF16)
    ids = ids_ref[...]
    expert = lax.broadcasted_iota(jnp.int32, (TOK, EXPERTS), 1)
    cols = [
        jnp.sum(jnp.where(ids[:, k : k + 1] == expert, dense, 0.0), axis=1, keepdims=True)
        for k in range(TOPK)
    ]
    weight_ref[...] = jnp.concatenate(cols, axis=1)


def finish(back, key, probs, ids, router):
    return pl.pallas_call(
        final_kernel,
        out_shape=(
            jax.ShapeDtypeStruct((TOK, DS), BF16),
            jax.ShapeDtypeStruct((TOK, TOPK), F32),
        ),
    )(back, key, probs, ids, router)


def body(out_grad, expert_ids, chosen_logits, down_weight, saved_hidden, router_weight):
    x, core = lax.axis_index("x"), lax.axis_index("core")
    head = x * CORES + core
    width = down_weight.shape[1]
    hidden = saved_hidden[0].reshape(Y, ZH, ZL, CAP, width).transpose(4, 0, 2, 1, 3)
    hidden = hidden.reshape(width, EXPERTS * CAP)
    weight = down_weight[0].reshape(width, X, CORES * DS).transpose(1, 0, 2)
    along = jnp.concatenate(
        [jnp.broadcast_to(hidden[None], (X,) + hidden.shape), weight], axis=2
    )
    along = lax.all_to_all(along, "x", split_axis=0, concat_axis=0, tiled=True)
    mine = along.reshape(X * width, EXPERTS * CAP + CORES * DS)
    slots = EXPERTS * CAP
    weight_mine = lax.dynamic_slice_in_dim(mine, slots + core * DS, DS, axis=1)
    weight_other = lax.dynamic_slice_in_dim(mine, slots + (1 - core) * DS, DS, axis=1)
    theirs = lax.ppermute(
        jnp.concatenate([mine[:, :slots], weight_other], axis=1), "core", [(0, 1), (1, 0)]
    )
    mixed = lax.dot_general(
        mine[:, :slots], weight_mine, (((0,), (0,)), ((), ())), preferred_element_type=F32
    ) + lax.dot_general(
        theirs[:, :slots], theirs[:, slots:], (((0,), (0,)), ((), ())), preferred_element_type=F32
    )
    own = lax.dynamic_slice_in_dim(out_grad, head * DS, DS, axis=1)
    ids_rows = jnp.pad(expert_ids.T.astype(BF16), ((0, 8), (0, 0)))
    blocks = lax.all_gather(jnp.concatenate([own, ids_rows], axis=0), "zh", axis=0, tiled=False)
    outgoing = select_rows(lax.axis_index("zh").reshape(1).astype(jnp.int32), blocks)
    received = lax.all_to_all(outgoing, ("y", "zl"), split_axis=0, concat_axis=0, tiled=True)
    part = jnp.sum(received.reshape(slots, DS).astype(F32) * mixed, axis=1)
    part = part.reshape(EXPERTS, CAP)
    part = jnp.sum(lax.all_gather(part, "core", axis=0, tiled=False), axis=0)
    part = lax.all_to_all(
        jnp.broadcast_to(part[None], (X,) + part.shape), "x", split_axis=0, concat_axis=0, tiled=True
    )
    part = jnp.sum(part, axis=0)
    back = lax.all_to_all(
        part.reshape(EXPERTS, 1, CAP), ("y", "zl", "zh"), split_axis=0, concat_axis=0, tiled=True
    )
    back = back.reshape(Y, ZL, ZH, CAP).transpose(3, 0, 2, 1).reshape(CAP, EXPERTS)
    key, probs = plan(expert_ids, chosen_logits)
    return finish(back, key, probs, expert_ids, router_weight)


def solution(mesh):
    fine = Mesh(
        mesh.devices.reshape(X, CORES, Y, ZH, ZL), ("x", "core", "y", "zh", "zl")
    )
    return jax.shard_map(
        body,
        mesh=fine,
        in_specs=(
            P(EXPERT, None),
            P(EXPERT, None),
            P(EXPERT, None),
            P(EXPERT, HEAD, None),
            P(EXPERT, None, None, HEAD),
            P(HEAD, None),
        ),
        out_specs=(P(EXPERT, HEAD), P(EXPERT, None)),
        check_vma=False,
    )
```

time: 579 us -> 136 us (0.23)
  waiting for transfers between devices: 469 us -> 29.9 us
  blocking collectives: 23.4 us -> 44.1 us
  local copies, waits for them, and re-layouts: 31.8 us -> 12.5 us
  Pallas kernels: 0 us -> 7.23 us
  other arithmetic: 13.2 us -> 7.13 us
    all_to_all x2 -> x3, waiting for transfers between devices: 469 us -> 29.9 us  [the longest x1 21.2 us: body(): lax.all_to_all(outgoing, ('y', 'zl'), split_axis=0, concat_axis=0, tiled=...]
    all_gather x0 -> x2, blocking collectives: none -> 35.5 us  [the longest x1 31.5 us: body(): lax.all_gather(jnp.concatenate([own, ids_rows], axis=0), 'zh', axis=0, ti...]
    psum x1 -> x0, blocking collectives: 23.4 us -> none  [body(): slot_grads = lax.psum(partial_grads, 'head')]
    gather x2 -> x0, local copies, waits for them, and re-layouts: 22.6 us -> none  [the longest x1 11.8 us: body(): weight_grad = returned.reshape(-1)[position].reshape(tok_rows, chosen)]
    all_to_all x2 -> x3, starting transfers between devices: 29.9 us -> 19.8 us  [the longest x1 9.71 us: body(): lax.all_to_all(part.reshape(EXPERTS, 1, CAP), ('y', 'zl', 'zh'), split_ax...]
    select_n x2 -> x0, other arithmetic: 9.98 us -> none  [the longest x1 9.97 us: body(): jnp.where((owner > 0)[:, None], picked, jnp.zeros((), out_grad.dtype))]
    all_to_all x0 -> x1, blocking collectives: none -> 8.6 us  [body(): lax.all_to_all(jnp.broadcast_to(part[None], (X,) + part.shape), 'x', spli...]
    scatter x1 -> x0, local copies, waits for them, and re-layouts: 8.06 us -> none  [body(): owner = jnp.zeros((experts * capacity,), jnp.int32).at[position].set(marks)]
  transfers between devices with their start and end apart: 2 -> 4, of which waited for: 2 -> 2; matrix products, arithmetic and copies ran while one was open for 0% -> 9% of each run, Pallas kernels for 0% -> 3%
where the time goes in v1:
time: 136 us; the launch traced here: 135 us
  blocking collectives  44.1 us (32%)
  waiting for transfers between devices  29.9 us (22%)
  starting transfers between devices  26.4 us (19%)
  local copies, waits for them, and re-layouts  12.5 us (9%)
  Pallas kernels  7.23 us (5%)
  other arithmetic  7.13 us (5%)
  matrix products  6.57 us (5%)
    all_gather x1, blocking collectives, body(): lax.all_gather(jnp.concatenate([own, ids_rows], axis=0), 'zh', axis=0, ti...  31.5 us
    all_to_all x1, waiting for transfers between devices, body(): lax.all_to_all(outgoing, ('y', 'zl'), split_axis=0, concat_axis=0, tiled=...  21.2 us
    all_to_all x1, starting transfers between devices, body(): lax.all_to_all(part.reshape(EXPERTS, 1, CAP), ('y', 'zl', 'zh'), split_ax...  9.71 us
    all_to_all x1, waiting for transfers between devices, body(): lax.all_to_all(part.reshape(EXPERTS, 1, CAP), ('y', 'zl', 'zh'), split_ax...  8.75 us
    all_to_all x1, blocking collectives, body(): lax.all_to_all(jnp.broadcast_to(part[None], (X,) + part.shape), 'x', spli...  8.6 us
    ppermute x1, starting transfers between devices, body(): lax.ppermute(jnp.concatenate([mine[:, :slots], weight_other], axis=1), 'c...  6.63 us
    all_to_all x1, starting transfers between devices, body(): lax.all_to_all(outgoing, ('y', 'zl'), split_axis=0, concat_axis=0, tiled=...  5.12 us
    all_to_all x1, starting transfers between devices, body(): along = lax.all_to_all(along, 'x', split_axis=0, concat_axis=0, tiled=True)  4.97 us
  transfers between devices with their start and end apart: 4, of which 2 were waited for; matrix products, arithmetic and copies ran while one was open for 9% of the time, Pallas kernels for 3%

profile of v1, /device:TPU:1, one launch (start us, length us, event | category | flops | bytes accessed | tf_op | source)
XLA Modules:
  0.0 134.7 jit_solution(480687775844540067)
XLA Ops:
  0.6 1.4 %reshape_squeeze.7 = bf16[96,4,512]{2,1,0:T(4,128)(2,1)S(1)} reshape(bf16[1,96,2048]{2,1,0:T(8,128)(2,1)} %param.9) | data formatting | bytes 786432 | tf_op jit(solution)/shard_map/reshape;squeeze | solution.py:126
  2.1 1.2 copy.38
  3.3 0.2 copy.39
  3.5 0.1 broadcast_in_dim.14
  3.7 1.8 %pad_maximum_fusion = bf16[4,96,3072]{2,1,0:T(8,128)(2,1)} fusion(bf16[4,96,512]{2,1,0:T(8,128)(2,1)S(1)} %copy.40, bf16[4,96,2560]{2,1,0:T(8,128)(2,1)S(1)} %broadcast_in_dim.14), kind=kLoop, calls=%fused_computation.2 | loop fusion | flops 4718592 | bytes 4718592 | tf_op jit(solution)/shard_map/concatenate | solution.py:127
  5.4 5.0 %all-to-all-start.1 = ((bf16[4,96,3072]{2,1,0:T(8,128)(2,1)}), bf16[4,96,3072]{2,1,0:T(8,128)(2,1)S(1)}, u32[]{:S(2)}, u32[]{:S(2)}) async-start(bf16[4,96,3072]{2,1,0:T(8,128)(2,1)} %pad_maximum_fusion), calls=%async_computation.1 | async-start | bytes 4718592 | tf_op jit(solution)/shard_map/all_to_all | solution.py:130
  10.5 31.5 %all-gather = bf16[1088,256]{1,0:T(8,128)(2,1)S(1)} all-gather(bf16[272,256]{1,0:T(8,128)(2,1)S(1)} %fusion.9), channel_id=2, replica_groups=mesh['x'=4,'core'=2,'y'=4,'zh'=4,'zl'=4] {'zh'}, dimensions={0}, use_global_device_ids=true | all-gather | bytes 696320 | tf_op jit(solution)/shard_map/all_gather | solution.py:145
  42.0 1.7 %shard_map.77 = bf16[16,160,256]{2,1,0:T(8,128)(2,1)} custom-call(s32[1]{0:T(128)} %bitcast.zh_ref, bf16[4,272,256]{2,1,0:T(8,128)(2,1)S(1)} %bitcast.22), custom_call_target="tpu_custom_call" | custom-call | tf_op jit(solution)/shard_map/pallas_call | solution.py:53
  43.7 5.1 %all-to-all-start = ((bf16[16,160,256]{2,1,0:T(8,128)(2,1)}), bf16[16,160,256]{2,1,0:T(8,128)(2,1)}, u32[]{:S(2)}, u32[]{:S(2)}) async-start(bf16[16,160,256]{2,1,0:T(8,128)(2,1)} %shard_map.77), calls=%async_computation | async-start | bytes 2621440 | tf_op jit(solution)/shard_map/all_to_all | solution.py:147
  48.8 0.1 slice.13
  49.0 1.6 %pad_maximum_fusion.1 = bf16[384,2816]{1,0:T(8,128)(2,1)} fusion(bf16[384,256]{1,0:T(8,128)(2,1)S(1)} %constant_dynamic-slice_fusion, bf16[384,2560]{1,0:T(8,128)(2,1)S(1)} %slice.13), kind=kLoop, calls=%fused_computation.3 | loop fusion | flops 4325376 | bytes 4325376 | tf_op jit(solution)/shard_map/concatenate | solution.py:136
  50.6 6.6 %collective-permute-start = (bf16[384,2816]{1,0:T(8,128)(2,1)}, bf16[384,2816]{1,0:T(8,128)(2,1)}, u32[]{:S(2)}, u32[]{:S(2)}) collective-permute-start(bf16[384,2816]{1,0:T(8,128)(2,1)} %pad_maximum_fusion.1), channel_id=1, source_target_pairs={{0,64},{64,0},{1,65},{65,1},{2,66},{66,2},{3,67},{67,3},{4,68},{68... | collective-permute-start | bytes 6488072 | tf_op jit(solution)/shard_map/ppermute | solution.py:135
  57.2 2.4 %fusion.7 = f32[2560,256]{0,1:T(8,128)} fusion(bf16[384,3072]{1,0:T(8,128)(2,1)S(1)} %bitcast.25, s32[]{:T(128)S(6)} %select_n.10), kind=kOutput, calls=%fused_computation.10 | convolution fusion | flops 503316480 | bytes 4784132 | tf_op jit(solution)/shard_map/dot_general | solution.py:138
  59.6 21.2 %all-to-all-done = bf16[16,160,256]{2,1,0:T(8,128)(2,1)} async-done(((bf16[16,160,256]{2,1,0:T(8,128)(2,1)}), bf16[16,160,256]{2,1,0:T(8,128)(2,1)}, u32[]{:S(2)}, u32[]{:S(2)}) %all-to-all-start) | async-done | bytes 1310752 | tf_op jit(solution)/shard_map/all_to_all | solution.py:147
  80.8 3.0 %bitcast_convert_fusion = f32[2560,256]{1,0:T(8,128)} fusion(bf16[16,160,256]{2,1,0:T(8,128)(2,1)} %all-to-all-done), kind=kLoop, calls=%fused_computation.6 | loop fusion | flops 655360 | bytes 3932160 | tf_op jit(solution)/shard_map/convert_element_type | solution.py:148
  83.9 3.2 %copy.41 = f32[2560,256]{0,1:T(8,128)} copy(f32[2560,256]{1,0:T(8,128)} %bitcast_convert_fusion) | data formatting | bytes 5242880 | tf_op jit(solution)/shard_map/convert_element_type | solution.py:148
  87.1 4.2 %fusion.2 = f32[2560]{0:T(1024)S(1)} fusion(f32[2560,256]{0,1:T(8,128)} %copy.41, f32[2560,256]{0,1:T(8,128)} %fusion.7, bf16[384,2816]{1,0:T(8,128)(2,1)} %collective-permute-done), kind=kOutput, calls=%fused_computation.5 | convolution fusion | flops 505280000 | bytes 7415808 | tf_op jit(solution)/shard_map/dot_general | solution.py:140
  91.4 3.9 %all_gather.11 = f32[2,64,40]{1,2,0:T(8,128)S(1)} all-gather(f32[1,64,40]{1,2,0:T(8,128)S(1)} %copy.42), channel_id=1, replica_groups=mesh['x'=4,'core'=2,'y'=4,'zh'=4,'zl'=4] {'core'}, dimensions={0}, use_global_device_ids=true | all-gather | bytes 30720 | tf_op jit(solution)/shard_map/all_gather | solution.py:150
  95.4 0.1 reshape.31
  95.5 8.6 %all_to_all.20 = f32[4,1,2560]{2,1,0:T(1,128)S(1)} all-to-all(f32[4,1,2560]{2,1,0:T(1,128)S(1)} %reshape.31), channel_id=1, replica_groups=mesh['x'=4,'core'=2,'y'=4,'zh'=4,'zl'=4] {'x'}, dimensions={0} | all-to-all | bytes 81920 | tf_op jit(solution)/shard_map/all_to_all | solution.py:151
  104.1 0.5 broadcast.7
  104.6 0.8 reduce
  105.5 0.7 copy.43
  106.1 9.7 %all-to-all-start.3 = ((f32[64,1,40]{2,1,0:T(1,128)}), f32[64,1,40]{2,1,0:T(1,128)S(1)}, u32[]{:S(2)}, u32[]{:S(2)}) async-start(f32[64,1,40]{2,1,0:T(1,128)} %copy.43), calls=%async_computation.3 | async-start | bytes 65536 | tf_op jit(solution)/shard_map/all_to_all | solution.py:155
  115.9 0.8 copy.45.ids_ref
  116.6 0.8 copy.46.logits_ref
  117.4 0.7 copy.49.router_ref
  118.1 2.4 %shard_map.78 = (f32[256,64]{1,0:T(8,128)}, f32[256,64]{1,0:T(8,128)}) custom-call(s32[256,8]{1,0:T(8,128)} %copy.45.ids_ref, f32[256,8]{1,0:T(8,128)} %copy.46.logits_ref), custom_call_target="tpu_custom_call" | custom-call | tf_op jit(solution)/shard_map/pallas_call | solution.py:87
  120.6 8.8 %all-to-all-done.3 = f32[64,1,40]{2,1,0:T(1,128)S(1)} async-done(((f32[64,1,40]{2,1,0:T(1,128)}), f32[64,1,40]{2,1,0:T(1,128)S(1)}, u32[]{:S(2)}, u32[]{:S(2)}) %all-to-all-start.3) | async-done | bytes 10272 | tf_op jit(solution)/shard_map/all_to_all | solution.py:155
  129.3 0.7 copy.47.back_ref
  130.0 3.1 %shard_map.79 = (bf16[256,256]{1,0:T(8,128)(2,1)}, f32[256,8]{1,0:T(8,128)}) custom-call(f32[40,64]{1,0:T(8,128)} %copy.47.back_ref, f32[256,64]{1,0:T(8,128)} %get-tuple-element.4.key_ref, f32[256,64]{1,0:T(8,128)} %get-tuple-element.5.probs_ref, s32[256,8]{1,0:T(8,128)} %copy.45.ids_ref, bf16[256,64]{1,0:T(8,128)(2,1)} %copy.49.router_ref), custom_call_target="tpu_custom_call" | custom-call | tf_op jit(solution)/shard_map/pallas_call | solution.py:111
  133.1 1.6 %copy.50 = f32[256,8]{0,1:T(8,128)} copy(f32[256,8]{1,0:T(8,128)} %get-tuple-element.13) | data formatting | bytes 16384 | tf_op jit(solution)/shard_map/pallas_call | solution.py:111
  (22 shorter events, 0.4 us)
Async XLA Ops:
  0.6 9.8 %copy-start = (bf16[256,2048]{1,0:T(8,128)(2,1)S(1)}, bf16[256,2048]{1,0:T(8,128)(2,1)}, u32[]{:S(2)}) copy-start(bf16[256,2048]{1,0:T(8,128)(2,1)} %param.6) | copy-start | bytes 3145732
  5.4 5.0 %copy-start.2 = (s32[256,8]{0,1:T(8,128)S(1)}, s32[256,8]{0,1:T(8,128)}, u32[]{:S(2)}) copy-start(s32[256,8]{0,1:T(8,128)} %param.7) | copy-start | bytes 24580
  5.4 38.3 %all-to-all-start.1 = ((bf16[4,96,3072]{2,1,0:T(8,128)(2,1)}), bf16[4,96,3072]{2,1,0:T(8,128)(2,1)S(1)}, u32[]{:S(2)}, u32[]{:S(2)}) async-start(bf16[4,96,3072]{2,1,0:T(8,128)(2,1)} %pad_maximum_fusion), calls=%async_computation.1 | async-start | bytes 4718592 | tf_op jit(solution)/shard_map/all_to_all | solution.py:130
  43.7 37.1 %all-to-all-start = ((bf16[16,160,256]{2,1,0:T(8,128)(2,1)}), bf16[16,160,256]{2,1,0:T(8,128)(2,1)}, u32[]{:S(2)}, u32[]{:S(2)}) async-start(bf16[16,160,256]{2,1,0:T(8,128)(2,1)} %shard_map.77), calls=%async_computation | async-start | bytes 2621440 | tf_op jit(solution)/shard_map/all_to_all | solution.py:147
  50.6 36.5 %collective-permute-start = (bf16[384,2816]{1,0:T(8,128)(2,1)}, bf16[384,2816]{1,0:T(8,128)(2,1)}, u32[]{:S(2)}, u32[]{:S(2)}) collective-permute-start(bf16[384,2816]{1,0:T(8,128)(2,1)} %pad_maximum_fusion.1), channel_id=1, source_target_pairs={{0,64},{64,0},{1,65},{65,1},{2,66},{66,2},{3,67},{67,3},{4,68},{68... | collective-permute-start | bytes 6488072 | tf_op jit(solution)/shard_map/ppermute | solution.py:135
  87.1 29.5 %copy-start.3 = (f32[256,8]{0,1:T(8,128)S(1)}, f32[256,8]{0,1:T(8,128)}, u32[]{:S(2)}) copy-start(f32[256,8]{0,1:T(8,128)} %param.8) | copy-start | bytes 24580
  87.1 30.3 %copy-start.1 = (bf16[256,64]{0,1:T(8,128)(2,1)S(1)}, bf16[256,64]{0,1:T(8,128)(2,1)}, u32[]{:S(2)}) copy-start(bf16[256,64]{0,1:T(8,128)(2,1)} %param.11) | copy-start | bytes 98308
  106.1 23.2 %all-to-all-start.3 = ((f32[64,1,40]{2,1,0:T(1,128)}), f32[64,1,40]{2,1,0:T(1,128)S(1)}, u32[]{:S(2)}, u32[]{:S(2)}) async-start(f32[64,1,40]{2,1,0:T(1,128)} %copy.43), calls=%async_computation.3 | async-start | bytes 65536 | tf_op jit(solution)/shard_map/all_to_all | solution.py:155

commit v2 on v1

v2 whole, which is shorter than its diff:
```python
import jax
import jax.numpy as jnp
from jax import lax
from jax.experimental import pallas as pl
from jax.experimental.pallas import tpu as pltpu
from jax.sharding import Mesh, PartitionSpec as P

X, CORES, Y, ZH, ZL = 4, 2, 4, 4, 4
EXPERT = ("y", "zh", "zl")
HEAD = ("x", "core")
TOK = 256
CAP = 40
TOPK = 8
EXPERTS = 64
DS = 256
NEAR = Y * ZL
F32 = jnp.float32
BF16 = jnp.bfloat16


def select_kernel(zh_ref, blocks_ref, out_ref, picked):
    zh = zh_ref[0]
    j = lax.broadcasted_iota(jnp.int32, (NEAR, TOK), 0)
    expert = ((j // ZL) * (ZH * ZL) + zh * ZL + j % ZL).astype(F32)
    hits = []
    for b in range(ZH):
        ids = blocks_ref[b, TOK : TOK + 16, :].astype(F32)
        hit = jnp.zeros((NEAR, TOK), F32)
        for k in range(TOPK):
            hit = hit + (ids[k : k + 1, :] == expert).astype(F32)
        hits.append(hit)
    hits = jnp.concatenate(hits, axis=0)
    earlier = lax.broadcasted_iota(jnp.int32, (TOK, TOK), 0) < lax.broadcasted_iota(
        jnp.int32, (TOK, TOK), 1
    )
    before = jnp.dot(hits.astype(BF16), earlier.astype(BF16), preferred_element_type=F32)
    key = jnp.where(hits > 0, before, -1.0)
    slot = lax.broadcasted_iota(jnp.int32, (CAP, TOK), 0).astype(F32)
    for b in range(ZH):
        pick = jnp.concatenate(
            [(key[b * NEAR + e : b * NEAR + e + 1, :] == slot).astype(F32) for e in range(NEAR)],
            axis=0,
        )
        picked[b] = jnp.dot(
            pick.astype(BF16), blocks_ref[b, 0:TOK, :], preferred_element_type=F32
        )
    for e in range(NEAR):
        rows = [picked[b, e * CAP : (e + 1) * CAP, :] for b in range(ZH)]
        out_ref[e] = jnp.concatenate(rows, axis=0).astype(BF16)


def select_rows(zh, blocks):
    return pl.pallas_call(
        select_kernel,
        out_shape=jax.ShapeDtypeStruct((NEAR, ZH * CAP, DS), BF16),
        in_specs=[
            pl.BlockSpec(memory_space=pltpu.SMEM),
            pl.BlockSpec(memory_space=pltpu.VMEM),
        ],
        out_specs=pl.BlockSpec(memory_space=pltpu.VMEM),
        scratch_shapes=[pltpu.VMEM((ZH, NEAR * CAP, DS), F32)],
        compiler_params=pltpu.CompilerParams(vmem_limit_bytes=32 << 20),
    )(zh, blocks)


def exchange_kernel(hidden_ref, weight_ref, out_ref):
    slots = EXPERTS * CAP
    hidden = hidden_ref[...].astype(F32).T.astype(BF16)
    for i in range(X):
        out_ref[i, :, 0:slots] = hidden
        out_ref[i, :, slots:] = weight_ref[:, i * CORES * DS : (i + 1) * CORES * DS]


def exchange_blocks(hidden, weight):
    width = weight.shape[0]
    return pl.pallas_call(
        exchange_kernel,
        out_shape=jax.ShapeDtypeStruct((X, width, EXPERTS * CAP + CORES * DS), BF16),
        compiler_params=pltpu.CompilerParams(vmem_limit_bytes=32 << 20),
    )(hidden, weight)


def mix_kernel(core_ref, mine_ref, theirs_ref, out_ref):
    slots = EXPERTS * CAP
    first = core_ref[0] == 0
    weight = jnp.where(
        first, mine_ref[:, slots : slots + DS], mine_ref[:, slots + DS : slots + 2 * DS]
    )
    group = ZH * ZL * CAP
    contract = (((0,), (0,)), ((), ()))
    for y in range(Y):
        cols = slice(y * group, (y + 1) * group)
        mixed = lax.dot_general(
            mine_ref[:, cols], weight, contract, preferred_element_type=F32
        ) + lax.dot_general(
            theirs_ref[:, cols], theirs_ref[:, slots:], contract, preferred_element_type=F32
        )
        for zh in range(ZH):
            for zl in range(ZL):
                src, dst = (zh * ZL + zl) * CAP, y * group + (zl * ZH + zh) * CAP
                out_ref[dst : dst + CAP, :] = mixed[src : src + CAP, :]


def mix(core, mine, theirs):
    return pl.pallas_call(
        mix_kernel,
        out_shape=jax.ShapeDtypeStruct((EXPERTS * CAP, DS), F32),
        in_specs=[
            pl.BlockSpec(memory_space=pltpu.SMEM),
            pl.BlockSpec(memory_space=pltpu.VMEM),
            pl.BlockSpec(memory_space=pltpu.VMEM),
        ],
        out_specs=pl.BlockSpec(memory_space=pltpu.VMEM),
        compiler_params=pltpu.CompilerParams(vmem_limit_bytes=32 << 20),
    )(core, mine, theirs)


def value_kernel(rows_ref, mixed_ref, out_ref):
    own_lane = lax.broadcasted_iota(jnp.int32, (CAP, 128), 0) == lax.broadcasted_iota(
        jnp.int32, (CAP, 128), 1
    )
    for e in range(NEAR):
        rows = rows_ref[e].astype(F32) * mixed_ref[e * ZH * CAP : (e + 1) * ZH * CAP, :]
        sums = jnp.sum(rows[:, 0:128] + rows[:, 128:256], axis=1, keepdims=True)
        for b in range(ZH):
            lanes = jnp.where(own_lane, sums[b * CAP : (b + 1) * CAP, :], 0.0)
            out_ref[e * ZH + b] = jnp.sum(lanes, axis=0, keepdims=True)


def slot_sums(rows, mixed):
    return pl.pallas_call(
        value_kernel,
        out_shape=jax.ShapeDtypeStruct((EXPERTS, 1, 128), F32),
        compiler_params=pltpu.CompilerParams(vmem_limit_bytes=32 << 20),
    )(rows, mixed)


def plan_kernel(ids_ref, logits_ref, key_ref, probs_ref):
    ids = ids_ref[...]
    raised = jnp.exp(logits_ref[...])
    probs = raised / jnp.sum(raised, axis=0, keepdims=True)
    expert = lax.broadcasted_iota(jnp.int32, (EXPERTS, TOK), 0)
    hits = jnp.zeros((EXPERTS, TOK), F32)
    spread = jnp.zeros((EXPERTS, TOK), F32)
    for k in range(TOPK):
        mine = ids[k : k + 1, :] == expert
        hits = hits + mine.astype(F32)
        spread = spread + jnp.where(mine, probs[k : k + 1, :], 0.0)
    earlier = lax.broadcasted_iota(jnp.int32, (TOK, TOK), 0) < lax.broadcasted_iota(
        jnp.int32, (TOK, TOK), 1
    )
    before = jnp.dot(hits.astype(BF16), earlier.astype(BF16), preferred_element_type=F32)
    key_ref[...] = jnp.where(hits > 0, before, -1.0)
    probs_ref[...] = spread


def plan(ids, logits):
    shape = jax.ShapeDtypeStruct((EXPERTS, TOK), F32)
    return pl.pallas_call(plan_kernel, out_shape=(shape, shape))(ids, logits)


def final_kernel(back_ref, key_ref, probs_ref, ids_ref, router_ref, grad_ref, weight_ref, total):
    parts = back_ref[0, 0]
    for c in range(CORES):
        for i in range(X):
            if c or i:
                parts = parts + back_ref[c, i]
    parts = parts.reshape(EXPERTS, 128)
    for y in range(Y):
        for zh in range(ZH):
            for zl in range(ZL):
                src, dst = (y * ZL + zl) * ZH + zh, (y * ZH + zh) * ZL + zl
                total[dst : dst + 1, :] = parts[src : src + 1, :]
    back = total[...]
    key = key_ref[...]
    probs = probs_ref[...]
    dense = jnp.zeros((EXPERTS, TOK), F32)
    for c in range(CAP):
        dense = jnp.where(key == float(c), back[:, c : c + 1], dense)
    mean = jnp.sum(probs * dense, axis=0, keepdims=True)
    logit = (probs * (dense - mean)).astype(BF16)
    grad_ref[...] = lax.dot_general(
        logit, router_ref[...], (((0,), (0,)), ((), ())), preferred_element_type=F32
    ).astype(BF16)
    ids = ids_ref[...]
    expert = lax.broadcasted_iota(jnp.int32, (EXPERTS, TOK), 0)
    for k in range(TOPK):
        weight_ref[k : k + 1, :] = jnp.sum(
            jnp.where(ids[k : k + 1, :] == expert, dense, 0.0), axis=0, keepdims=True
        )


def finish(back, key, probs, ids, router):
    return pl.pallas_call(
        final_kernel,
        out_shape=(
            jax.ShapeDtypeStruct((TOK, DS), BF16),
            jax.ShapeDtypeStruct((TOPK, TOK), F32),
        ),
        scratch_shapes=[pltpu.VMEM((EXPERTS, 128), F32)],
    )(back, key, probs, ids, router)


def body(out_grad, expert_ids, chosen_logits, down_weight, saved_hidden, router_weight):
    x, core = lax.axis_index("x"), lax.axis_index("core")
    head = x * CORES + core
    width = down_weight.shape[1]
    slots = EXPERTS * CAP
    ids, logits = expert_ids.T, chosen_logits.T
    along = exchange_blocks(saved_hidden[0].reshape(slots, width), down_weight[0])
    along = lax.all_to_all(along, "x", split_axis=0, concat_axis=0, tiled=True)
    mine = along.reshape(X * width, slots + CORES * DS)
    weight_other = lax.dynamic_slice_in_dim(mine, slots + (1 - core) * DS, DS, axis=1)
    theirs = lax.ppermute(
        jnp.concatenate([mine[:, :slots], weight_other], axis=1), "core", [(0, 1), (1, 0)]
    )
    mixed = mix(core.reshape(1).astype(jnp.int32), mine, theirs)
    ids_late, logits, _ = lax.optimization_barrier((ids, logits, theirs))
    key, probs = plan(ids_late, logits)
    own = lax.dynamic_slice_in_dim(out_grad, head * DS, DS, axis=1)
    ids_rows = jnp.pad(ids.astype(BF16), ((0, 8), (0, 0)))
    blocks = lax.all_gather(jnp.concatenate([own, ids_rows], axis=0), "zh", axis=0, tiled=False)
    outgoing = select_rows(lax.axis_index("zh").reshape(1).astype(jnp.int32), blocks)
    received = lax.all_to_all(outgoing, ("y", "zl"), split_axis=0, concat_axis=0, tiled=True)
    received, mixed, key, probs = lax.optimization_barrier((received, mixed, key, probs))
    part = slot_sums(received, mixed)
    part = lax.all_to_all(part, ("y", "zl", "zh"), split_axis=0, concat_axis=0, tiled=True)
    part = lax.all_to_all(
        jnp.broadcast_to(part[None], (X,) + part.shape), "x", split_axis=0, concat_axis=0, tiled=True
    )
    part = lax.all_gather(part, "core", axis=0, tiled=False)
    grad, weight_grad = finish(part, key, probs, ids, router_weight.T)
    return grad, weight_grad.T


def solution(mesh):
    fine = Mesh(
        mesh.devices.reshape(X, CORES, Y, ZH, ZL), ("x", "core", "y", "zh", "zl")
    )
    return jax.shard_map(
        body,
        mesh=fine,
        in_specs=(
            P(EXPERT, None),
            P(EXPERT, None),
            P(EXPERT, None),
            P(EXPERT, HEAD, None),
            P(EXPERT, None, None, HEAD),
            P(HEAD, None),
        ),
        out_specs=(P(EXPERT, HEAD), P(EXPERT, None)),
        check_vma=False,
    )
```

time: 136 us -> 126 us (0.926)
  blocking collectives: 44.1 us -> 70.4 us
  waiting for transfers between devices: 29.9 us -> 17.4 us
  starting transfers between devices: 26.4 us -> 16.7 us
  other arithmetic: 7.13 us -> 0.16 us
  matrix products: 6.57 us -> 0 us
  local copies, waits for them, and re-layouts: 12.5 us -> 11 us
    all_to_all x0 -> x1, blocking collectives: none -> 25.6 us  [body(): lax.all_to_all(part, ('y', 'zl', 'zh'), split_axis=0, concat_axis=0, tile...]
    all_to_all x1 -> x0, starting transfers between devices: 9.71 us -> none  [body(): lax.all_to_all(part.reshape(EXPERTS, 1, CAP), ('y', 'zl', 'zh'), split_ax...]
    all_to_all x1 -> x0, waiting for transfers between devices: 8.75 us -> none  [body(): lax.all_to_all(part.reshape(EXPERTS, 1, CAP), ('y', 'zl', 'zh'), split_ax...]
    unnamed x14 -> x20, local copies, waits for them, and re-layouts: 2.51 us -> 10.9 us
    all_to_all x1, waiting for transfers between devices: 21.2 us -> 13.5 us  [body(): lax.all_to_all(outgoing, ('y', 'zl'), split_axis=0, concat_axis=0, tiled=...]
    dot_general x2 -> x0, matrix products: 6.57 us -> none  [the longest x1 4.16 us: body(): lax.dot_general(theirs[:, :slots], theirs[:, slots:], (((0,), (0,)), ((),...]
    ppermute x1, waiting for transfers between devices: 0.01 us -> 3.86 us  [body(): lax.ppermute(jnp.concatenate([mine[:, :slots], weight_other], axis=1), 'c...]
    pallas_call x0 -> x3, Pallas kernels: none -> 3.57 us  [the longest x1 1.74 us: slot_sums(): pl.pallas_call(value_kernel, out_shape=jax.ShapeDtypeStruct((EXPERTS, 1,...]
  transfers between devices with their start and end apart: 4 -> 3, of which waited for: 2 -> 2; matrix products, arithmetic and copies ran while one was open for 9% -> 0% of each run, Pallas kernels for 3% -> 3%
where the time goes in v2:
time: 126 us; the launch traced here: 125 us
  blocking collectives  70.4 us (56%)
  waiting for transfers between devices  17.4 us (14%)
  starting transfers between devices  16.7 us (13%)
  local copies, waits for them, and re-layouts  11 us (9%)
  Pallas kernels  8.37 us (7%)
    all_gather x1, blocking collectives, body(): lax.all_gather(jnp.concatenate([own, ids_rows], axis=0), 'zh', axis=0, ti...  31.5 us
    all_to_all x1, blocking collectives, body(): lax.all_to_all(part, ('y', 'zl', 'zh'), split_axis=0, concat_axis=0, tile...  25.6 us
    all_to_all x1, waiting for transfers between devices, body(): lax.all_to_all(outgoing, ('y', 'zl'), split_axis=0, concat_axis=0, tiled=...  13.5 us
    unnamed x20, local copies, waits for them, and re-layouts  10.9 us
    all_to_all x1, blocking collectives, body(): lax.all_to_all(jnp.broadcast_to(part[None], (X,) + part.shape), 'x', spli...  7.21 us
    ppermute x1, starting transfers between devices, body(): lax.ppermute(jnp.concatenate([mine[:, :slots], weight_other], axis=1), 'c...  6.64 us
    all_gather x1, blocking collectives, body(): part = lax.all_gather(part, 'core', axis=0, tiled=False)  6.11 us
    all_to_all x1, starting transfers between devices, body(): lax.all_to_all(outgoing, ('y', 'zl'), split_axis=0, concat_axis=0, tiled=...  5.12 us
  transfers between devices with their start and end apart: 3, of which 2 were waited for; matrix products, arithmetic and copies ran while one was open for 0% of the time, Pallas kernels for 3%

profile of v2, /device:TPU:1, one launch (start us, length us, event | category | flops | bytes accessed | tf_op | source)
XLA Modules:
  0.0 124.9 jit_solution(9284733327114026562)
XLA Ops:
  0.6 0.0 copy-start
  0.6 0.0 copy-start.7
  0.7 1.2 copy-done.7
  1.8 1.0 copy-done.8
  2.8 0.3 shard_map.78
  3.1 0.0 copy-start.3
  3.1 1.4 %copy-done.3 = bf16[4,96,3072]{2,1,0:T(8,128)(2,1)} copy-done((bf16[4,96,3072]{2,1,0:T(8,128)(2,1)}, bf16[4,96,3072]{2,1,0:T(8,128)(2,1)S(1)}, u32[]{:S(2)}) %copy-start.3) | copy-done | bytes 2359320
  4.5 5.0 %all-to-all-start.1 = ((bf16[4,96,3072]{2,1,0:T(8,128)(2,1)}), bf16[4,96,3072]{2,1,0:T(8,128)(2,1)S(1)}, u32[]{:S(2)}, u32[]{:S(2)}) async-start(bf16[4,96,3072]{2,1,0:T(8,128)(2,1)} %copy-done.3), calls=%async_computation.1 | async-start | bytes 4718592 | tf_op jit(solution)/shard_map/all_to_all | solution.py:211
  9.5 0.0 copy-done
  9.5 0.0 copy-done.9
  9.6 31.5 %all-gather = bf16[1088,256]{1,0:T(8,128)(2,1)S(1)} all-gather(bf16[272,256]{1,0:T(8,128)(2,1)S(1)} %fusion.1), channel_id=2, replica_groups=mesh['x'=4,'core'=2,'y'=4,'zh'=4,'zl'=4] {'zh'}, dimensions={0}, use_global_device_ids=true | all-gather | bytes 696320 | tf_op jit(solution)/shard_map/all_gather | solution.py:222
  41.1 0.6 shard_map.77
  41.8 0.0 copy-start.4
  41.8 1.1 copy-done.4
  42.8 0.0 all-to-all-done.1
  42.8 5.1 %all-to-all-start = ((bf16[16,160,256]{2,1,0:T(8,128)(2,1)}), bf16[16,160,256]{2,1,0:T(8,128)(2,1)}, u32[]{:S(2)}, u32[]{:S(2)}) async-start(bf16[16,160,256]{2,1,0:T(8,128)(2,1)} %copy-done.4), calls=%async_computation | async-start | bytes 2621440 | tf_op jit(solution)/shard_map/all_to_all | solution.py:224
  48.0 0.1 slice.4
  48.1 0.1 pad_maximum_fusion
  48.3 6.6 %collective-permute-start = (bf16[384,2816]{1,0:T(8,128)(2,1)S(1)}, bf16[384,2816]{1,0:T(8,128)(2,1)S(1)}, u32[]{:S(2)}, u32[]{:S(2)}) collective-permute-start(bf16[384,2816]{1,0:T(8,128)(2,1)S(1)} %pad_maximum_fusion), channel_id=1, source_target_pairs={{0,64},{64,0},{1,65},{65,1},{2,66},{66,2},{3,67},{67,3},{4,68},{68... | collective-permute-start | bytes 6488072 | tf_op jit(solution)/shard_map/ppermute | solution.py:214
  54.9 3.9 %collective-permute-done.theirs_ref = bf16[384,2816]{1,0:T(8,128)(2,1)S(1)} collective-permute-done((bf16[384,2816]{1,0:T(8,128)(2,1)S(1)}, bf16[384,2816]{1,0:T(8,128)(2,1)S(1)}, u32[]{:S(2)}, u32[]{:S(2)}) %collective-permute-start) | collective-permute-done | bytes 2162720 | tf_op jit(solution)/shard_map/ppermute | solution.py:214
  58.8 1.4 %copy-done.5 = bf16[384,2816]{1,0:T(8,128)(2,1)} copy-done((bf16[384,2816]{1,0:T(8,128)(2,1)}, bf16[384,2816]{1,0:T(8,128)(2,1)S(1)}, u32[]{:S(2)}) %copy-start.5) | copy-done | bytes 2162712
  60.1 1.6 %shard_map.80 = (f32[64,256]{1,0:T(8,128)}, f32[64,256]{1,0:T(8,128)}) custom-call(s32[8,256]{1,0:T(8,128)} %bitcast.21, f32[8,256]{1,0:T(8,128)} %bitcast.24), custom_call_target="tpu_custom_call" | custom-call | tf_op jit(solution)/shard_map/pallas_call | solution.py:159
  61.7 1.6 %copy-done.6 = bf16[384,2816]{1,0:T(8,128)(2,1)S(1)} copy-done((bf16[384,2816]{1,0:T(8,128)(2,1)S(1)}, bf16[384,2816]{1,0:T(8,128)(2,1)}, u32[]{:S(2)}) %copy-start.6) | copy-done | bytes 2162712
  63.3 1.6 %shard_map.79.mixed_ref = f32[2560,256]{1,0:T(8,128)S(1)} custom-call(s32[1]{0:T(128)} %bitcast.3.core_ref, bf16[384,3072]{1,0:T(8,128)(2,1)S(1)} %bitcast.15, bf16[384,2816]{1,0:T(8,128)(2,1)S(1)} %copy-done.6), custom_call_target="tpu_custom_call" | custom-call | tf_op jit(solution)/shard_map/pallas_call | solution.py:105
  64.9 1.5 %copy-done.1 = f32[2560,256]{1,0:T(8,128)} copy-done((f32[2560,256]{1,0:T(8,128)}, f32[2560,256]{1,0:T(8,128)S(1)}, u32[]{:S(2)}) %copy-start.1) | copy-done | bytes 2621464
  66.4 13.5 %all-to-all-done.rows_ref = bf16[16,160,256]{2,1,0:T(8,128)(2,1)} async-done(((bf16[16,160,256]{2,1,0:T(8,128)(2,1)}), bf16[16,160,256]{2,1,0:T(8,128)(2,1)}, u32[]{:S(2)}, u32[]{:S(2)}) %all-to-all-start) | async-done | bytes 1310752 | tf_op jit(solution)/shard_map/all_to_all | solution.py:224
  79.9 1.7 %copy-done.2 = f32[2560,256]{1,0:T(8,128)S(1)} copy-done((f32[2560,256]{1,0:T(8,128)S(1)}, f32[2560,256]{1,0:T(8,128)}, u32[]{:S(2)}) %copy-start.2) | copy-done | bytes 2621464
  81.7 1.7 %shard_map.81 = f32[64,1,128]{2,1,0:T(1,128)S(1)} custom-call(bf16[16,160,256]{2,1,0:T(8,128)(2,1)} %all-to-all-done.rows_ref, f32[2560,256]{1,0:T(8,128)S(1)} %copy-done.2), custom_call_target="tpu_custom_call" | custom-call | tf_op jit(solution)/shard_map/pallas_call | solution.py:131
  83.4 25.6 %all_to_all.20 = f32[64,1,128]{2,1,0:T(1,128)S(1)} all-to-all(f32[64,1,128]{2,1,0:T(1,128)S(1)} %shard_map.81), channel_id=1, replica_groups=mesh['x'=4,'core'=2,'y'=4,'zh'=4,'zl'=4] {'y','zl','zh'}, dimensions={0} | all-to-all | bytes 65536 | tf_op jit(solution)/shard_map/all_to_all | solution.py:227
  109.0 7.2 %all_to_all.21 = f32[4,64,1,128]{3,1,2,0:T(8,128)S(1)} all-to-all(f32[4,64,1,128]{3,1,2,0:T(8,128)S(1)} %broadcast_in_dim.9), channel_id=1, replica_groups=mesh['x'=4,'core'=2,'y'=4,'zh'=4,'zl'=4] {'x'}, dimensions={0} | all-to-all | bytes 262144 | tf_op jit(solution)/shard_map/all_to_all | solution.py:228
  116.2 6.1 %all-gather.1 = f32[8,64,1,128]{3,1,2,0:T(8,128)} all-gather(f32[4,64,1,128]{3,1,2,0:T(8,128)S(1)} %all_to_all.21), channel_id=3, replica_groups=mesh['x'=4,'core'=2,'y'=4,'zh'=4,'zl'=4] {'core'}, dimensions={0}, use_global_device_ids=true | all-gather | bytes 393216 | tf_op jit(solution)/shard_map/all_gather | solution.py:231
  122.3 2.6 %shard_map.82 = (bf16[256,256]{1,0:T(8,128)(2,1)}, f32[8,256]{1,0:T(8,128)}) custom-call(f32[2,4,64,1,128]{4,3,2,1,0:T(1,128)} %bitcast.19, f32[64,256]{1,0:T(8,128)} %get-tuple-element.18.key_ref, f32[64,256]{1,0:T(8,128)} %get-tuple-element.19.probs_ref, s32[8,256]{1,0:T(8,128)} %bitcast.22, bf16[64,256]{1,0:T(8,128)(2,1)} %bitcast.23), custom_call_target="tpu_custom_call" | custom-call | tf_op jit(solution)/shard_map/pallas_call | solution.py:194
  (11 shorter events, 0.1 us)
Async XLA Ops:
  0.6 8.9 %copy-start = (bf16[256,2048]{1,0:T(8,128)(2,1)S(1)}, bf16[256,2048]{1,0:T(8,128)(2,1)}, u32[]{:S(2)}) copy-start(bf16[256,2048]{1,0:T(8,128)(2,1)} %param.6) | copy-start | bytes 3145732
  0.6 1.2 copy-start.7
  1.8 1.0 copy-start.8
  3.1 1.4 %copy-start.3 = (bf16[4,96,3072]{2,1,0:T(8,128)(2,1)}, bf16[4,96,3072]{2,1,0:T(8,128)(2,1)S(1)}, u32[]{:S(2)}) copy-start(bf16[4,96,3072]{2,1,0:T(8,128)(2,1)S(1)} %shard_map.78) | copy-start | bytes 7077892
  4.5 5.0 %copy-start.9 = (s32[256,8]{0,1:T(8,128)S(1)}, s32[256,8]{0,1:T(8,128)}, u32[]{:S(2)}) copy-start(s32[256,8]{0,1:T(8,128)} %param.7) | copy-start | bytes 24580
  4.5 38.3 %all-to-all-start.1 = ((bf16[4,96,3072]{2,1,0:T(8,128)(2,1)}), bf16[4,96,3072]{2,1,0:T(8,128)(2,1)S(1)}, u32[]{:S(2)}, u32[]{:S(2)}) async-start(bf16[4,96,3072]{2,1,0:T(8,128)(2,1)} %copy-done.3), calls=%async_computation.1 | async-start | bytes 4718592 | tf_op jit(solution)/shard_map/all_to_all | solution.py:211
  41.8 1.1 copy-start.4
  42.8 37.1 %all-to-all-start = ((bf16[16,160,256]{2,1,0:T(8,128)(2,1)}), bf16[16,160,256]{2,1,0:T(8,128)(2,1)}, u32[]{:S(2)}, u32[]{:S(2)}) async-start(bf16[16,160,256]{2,1,0:T(8,128)(2,1)} %copy-done.4), calls=%async_computation | async-start | bytes 2621440 | tf_op jit(solution)/shard_map/all_to_all | solution.py:224
  48.3 10.5 %collective-permute-start = (bf16[384,2816]{1,0:T(8,128)(2,1)S(1)}, bf16[384,2816]{1,0:T(8,128)(2,1)S(1)}, u32[]{:S(2)}, u32[]{:S(2)}) collective-permute-start(bf16[384,2816]{1,0:T(8,128)(2,1)S(1)} %pad_maximum_fusion), channel_id=1, source_target_pairs={{0,64},{64,0},{1,65},{65,1},{2,66},{66,2},{3,67},{67,3},{4,68},{68... | collective-permute-start | bytes 6488072 | tf_op jit(solution)/shard_map/ppermute | solution.py:214
  58.8 1.4 %copy-start.5 = (bf16[384,2816]{1,0:T(8,128)(2,1)}, bf16[384,2816]{1,0:T(8,128)(2,1)S(1)}, u32[]{:S(2)}) copy-start(bf16[384,2816]{1,0:T(8,128)(2,1)S(1)} %collective-permute-done.theirs_ref) | copy-start | bytes 6488068
  61.7 1.6 %copy-start.6 = (bf16[384,2816]{1,0:T(8,128)(2,1)S(1)}, bf16[384,2816]{1,0:T(8,128)(2,1)}, u32[]{:S(2)}) copy-start(bf16[384,2816]{1,0:T(8,128)(2,1)} %copy-done.5) | copy-start | bytes 6488068
  64.9 1.5 %copy-start.1 = (f32[2560,256]{1,0:T(8,128)}, f32[2560,256]{1,0:T(8,128)S(1)}, u32[]{:S(2)}) copy-start(f32[2560,256]{1,0:T(8,128)S(1)} %shard_map.79.mixed_ref) | copy-start | bytes 7864324
  79.9 1.7 %copy-start.2 = (f32[2560,256]{1,0:T(8,128)S(1)}, f32[2560,256]{1,0:T(8,128)}, u32[]{:S(2)}) copy-start(f32[2560,256]{1,0:T(8,128)} %copy-done.1) | copy-start | bytes 7864324

commit v3 on v2

--- a/solution.py
+++ b/solution.py
@@ -15,13 +15,18 @@
 DS = 256
 NEAR = Y * ZL
 F32 = jnp.float32
+NEAR_GROUPS = [
+    [c * Y * ZH * ZL + y * ZH * ZL + (q * ZL + r + 2 * c) % (ZH * ZL) for y in range(Y) for r in range(ZL)]
+    for c in range(CORES)
+    for q in range(ZH)
+]
 BF16 = jnp.bfloat16
 
 
-def select_kernel(zh_ref, blocks_ref, out_ref, picked):
-    zh = zh_ref[0]
+def select_kernel(base_ref, blocks_ref, out_ref, picked):
+    base = base_ref[0]
     j = lax.broadcasted_iota(jnp.int32, (NEAR, TOK), 0)
-    expert = ((j // ZL) * (ZH * ZL) + zh * ZL + j % ZL).astype(F32)
+    expert = ((j // ZL) * (ZH * ZL) + ((base + j % ZL) & (ZH * ZL - 1))).astype(F32)
     hits = []
     for b in range(ZH):
         ids = blocks_ref[b, TOK : TOK + 16, :].astype(F32)
@@ -49,7 +54,7 @@
         out_ref[e] = jnp.concatenate(rows, axis=0).astype(BF16)
 
 
-def select_rows(zh, blocks):
+def select_rows(base, blocks):
     return pl.pallas_call(
         select_kernel,
         out_shape=jax.ShapeDtypeStruct((NEAR, ZH * CAP, DS), BF16),
@@ -59,16 +64,31 @@
         ],
         out_specs=pl.BlockSpec(memory_space=pltpu.VMEM),
         scratch_shapes=[pltpu.VMEM((ZH, NEAR * CAP, DS), F32)],
-        compiler_params=pltpu.CompilerParams(vmem_limit_bytes=32 << 20),
-    )(zh, blocks)
-
-
-def exchange_kernel(hidden_ref, weight_ref, out_ref):
+        compiler_params=pltpu.CompilerParams(vmem_limit_bytes=16 << 20),
+    )(base, blocks)
+
+
+def exchange_kernel(hidden_hbm, weight_hbm, out_ref, hidden, weight, sems):
     slots = EXPERTS * CAP
-    hidden = hidden_ref[...].astype(F32).T.astype(BF16)
-    for i in range(X):
-        out_ref[i, :, 0:slots] = hidden
-        out_ref[i, :, slots:] = weight_ref[:, i * CORES * DS : (i + 1) * CORES * DS]
+    piece = slots // 4
+    copies = [
+        pltpu.make_async_copy(
+            hidden_hbm.at[pl.ds(i * piece, piece)], hidden.at[pl.ds(i * piece, piece)], sems.at[i]
+        )
+        for i in range(4)
+    ]
+    copies.append(pltpu.make_async_copy(weight_hbm, weight, sems.at[4]))
+    for copy in copies:
+        copy.start()
+    for i in range(4):
+        copies[i].wait()
+        rows = slice(i * piece, (i + 1) * piece)
+        turned = hidden[rows, :].astype(F32).T.astype(BF16)
+        for j in range(X):
+            out_ref[j, :, rows] = turned
+    copies[4].wait()
+    for j in range(X):
+        out_ref[j, :, slots:] = weight[:, j * CORES * DS : (j + 1) * CORES * DS]
 
 
 def exchange_blocks(hidden, weight):
@@ -76,15 +96,25 @@
     return pl.pallas_call(
         exchange_kernel,
         out_shape=jax.ShapeDtypeStruct((X, width, EXPERTS * CAP + CORES * DS), BF16),
-        compiler_params=pltpu.CompilerParams(vmem_limit_bytes=32 << 20),
+        in_specs=[pl.BlockSpec(memory_space=pl.ANY)] * 2,
+        out_specs=pl.BlockSpec(memory_space=pltpu.VMEM),
+        scratch_shapes=[
+            pltpu.VMEM(hidden.shape, BF16),
+            pltpu.VMEM(weight.shape, BF16),
+            pltpu.SemaphoreType.DMA((5,)),
+        ],
+        compiler_params=pltpu.CompilerParams(vmem_limit_bytes=16 << 20),
     )(hidden, weight)
 
 
-def mix_kernel(core_ref, mine_ref, theirs_ref, out_ref):
+def mix_kernel(
+    core_ref, mine_ref, theirs_ref, ids_ref, logits_ref, out_ref, key_ref, probs_ref
+):
+    plan(ids_ref[...], logits_ref[...], key_ref, probs_ref)
     slots = EXPERTS * CAP
-    first = core_ref[0] == 0
+    core = core_ref[0]
     weight = jnp.where(
-        first, mine_ref[:, slots : slots + DS], mine_ref[:, slots + DS : slots + 2 * DS]
+        core == 0, mine_ref[:, slots : slots + DS], mine_ref[:, slots + DS : slots + 2 * DS]
     )
     group = ZH * ZL * CAP
     contract = (((0,), (0,)), ((), ()))
@@ -95,49 +125,16 @@
         ) + lax.dot_general(
             theirs_ref[:, cols], theirs_ref[:, slots:], contract, preferred_element_type=F32
         )
-        for zh in range(ZH):
-            for zl in range(ZL):
-                src, dst = (zh * ZL + zl) * CAP, y * group + (zl * ZH + zh) * CAP
-                out_ref[dst : dst + CAP, :] = mixed[src : src + CAP, :]
-
-
-def mix(core, mine, theirs):
-    return pl.pallas_call(
-        mix_kernel,
-        out_shape=jax.ShapeDtypeStruct((EXPERTS * CAP, DS), F32),
-        in_specs=[
-            pl.BlockSpec(memory_space=pltpu.SMEM),
-            pl.BlockSpec(memory_space=pltpu.VMEM),
-            pl.BlockSpec(memory_space=pltpu.VMEM),
-        ],
-        out_specs=pl.BlockSpec(memory_space=pltpu.VMEM),
-        compiler_params=pltpu.CompilerParams(vmem_limit_bytes=32 << 20),
-    )(core, mine, theirs)
-
-
-def value_kernel(rows_ref, mixed_ref, out_ref):
-    own_lane = lax.broadcasted_iota(jnp.int32, (CAP, 128), 0) == lax.broadcasted_iota(
-        jnp.int32, (CAP, 128), 1
-    )
-    for e in range(NEAR):
-        rows = rows_ref[e].astype(F32) * mixed_ref[e * ZH * CAP : (e + 1) * ZH * CAP, :]
-        sums = jnp.sum(rows[:, 0:128] + rows[:, 128:256], axis=1, keepdims=True)
-        for b in range(ZH):
-            lanes = jnp.where(own_lane, sums[b * CAP : (b + 1) * CAP, :], 0.0)
-            out_ref[e * ZH + b] = jnp.sum(lanes, axis=0, keepdims=True)
-
-
-def slot_sums(rows, mixed):
-    return pl.pallas_call(
-        value_kernel,
-        out_shape=jax.ShapeDtypeStruct((EXPERTS, 1, 128), F32),
-        compiler_params=pltpu.CompilerParams(vmem_limit_bytes=32 << 20),
-    )(rows, mixed)
-
-
-def plan_kernel(ids_ref, logits_ref, key_ref, probs_ref):
-    ids = ids_ref[...]
-    raised = jnp.exp(logits_ref[...])
+        for zl in range(ZL):
+            place = zl ^ (2 * core)
+            for zh in range(ZH):
+                src = (zh * ZL + zl) * CAP
+                dst = pl.multiple_of(y * group + (place * ZH + zh) * CAP, 8)
+                out_ref[pl.ds(dst, CAP), :] = mixed[src : src + CAP, :]
+
+
+def plan(ids, logits, key_ref, probs_ref):
+    raised = jnp.exp(logits)
     probs = raised / jnp.sum(raised, axis=0, keepdims=True)
     expert = lax.broadcasted_iota(jnp.int32, (EXPERTS, TOK), 0)
     hits = jnp.zeros((EXPERTS, TOK), F32)
@@ -154,24 +151,49 @@
     probs_ref[...] = spread
 
 
-def plan(ids, logits):
-    shape = jax.ShapeDtypeStruct((EXPERTS, TOK), F32)
-    return pl.pallas_call(plan_kernel, out_shape=(shape, shape))(ids, logits)
-
-
-def final_kernel(back_ref, key_ref, probs_ref, ids_ref, router_ref, grad_ref, weight_ref, total):
+def mix(core, mine, theirs, ids, logits):
+    table = jax.ShapeDtypeStruct((EXPERTS, TOK), F32)
+    return pl.pallas_call(
+        mix_kernel,
+        out_shape=(jax.ShapeDtypeStruct((EXPERTS * CAP, DS), F32), table, table),
+        in_specs=[pl.BlockSpec(memory_space=pltpu.SMEM)]
+        + [pl.BlockSpec(memory_space=pltpu.VMEM)] * 4,
+        out_specs=(pl.BlockSpec(memory_space=pltpu.VMEM),) * 3,
+        compiler_params=pltpu.CompilerParams(vmem_limit_bytes=16 << 20),
+    )(core, mine, theirs, ids, logits)
+
+
+def value_kernel(core_ref, rows_ref, mixed_ref, out_ref):
+    own_lane = lax.broadcasted_iota(jnp.int32, (CAP, 128), 0) == lax.broadcasted_iota(
+        jnp.int32, (CAP, 128), 1
+    )
+    for e in range(NEAR):
+        rows = rows_ref[e].astype(F32) * mixed_ref[e * ZH * CAP : (e + 1) * ZH * CAP, :]
+        sums = jnp.sum(rows[:, 0:128] + rows[:, 128:256], axis=1, keepdims=True)
+        for b in range(ZH):
+            lanes = jnp.where(own_lane, sums[b * CAP : (b + 1) * CAP, :], 0.0)
+            place = (e // ZL * ZH + b) * ZL + ((e % ZL) ^ (2 * core_ref[0]))
+            out_ref[place] = jnp.sum(lanes, axis=0, keepdims=True)
+
+
+def slot_sums(core, rows, mixed):
+    return pl.pallas_call(
+        value_kernel,
+        out_shape=jax.ShapeDtypeStruct((EXPERTS, 1, 128), F32),
+        in_specs=[pl.BlockSpec(memory_space=pltpu.SMEM)]
+        + [pl.BlockSpec(memory_space=pltpu.VMEM)] * 2,
+        out_specs=pl.BlockSpec(memory_space=pltpu.VMEM),
+        compiler_params=pltpu.CompilerParams(vmem_limit_bytes=16 << 20),
+    )(core, rows, mixed)
+
+
+def final_kernel(back_ref, key_ref, probs_ref, ids_ref, router_ref, grad_ref, weight_ref):
     parts = back_ref[0, 0]
     for c in range(CORES):
         for i in range(X):
             if c or i:
                 parts = parts + back_ref[c, i]
-    parts = parts.reshape(EXPERTS, 128)
-    for y in range(Y):
-        for zh in range(ZH):
-            for zl in range(ZL):
-                src, dst = (y * ZL + zl) * ZH + zh, (y * ZH + zh) * ZL + zl
-                total[dst : dst + 1, :] = parts[src : src + 1, :]
-    back = total[...]
+    back = parts.reshape(EXPERTS, 128)
     key = key_ref[...]
     probs = probs_ref[...]
     dense = jnp.zeros((EXPERTS, TOK), F32)
@@ -197,7 +219,6 @@
             jax.ShapeDtypeStruct((TOK, DS), BF16),
             jax.ShapeDtypeStruct((TOPK, TOK), F32),
         ),
-        scratch_shapes=[pltpu.VMEM((EXPERTS, 128), F32)],
     )(back, key, probs, ids, router)
 
 
@@ -214,17 +235,24 @@
     theirs = lax.ppermute(
         jnp.concatenate([mine[:, :slots], weight_other], axis=1), "core", [(0, 1), (1, 0)]
     )
-    mixed = mix(core.reshape(1).astype(jnp.int32), mine, theirs)
-    ids_late, logits, _ = lax.optimization_barrier((ids, logits, theirs))
-    key, probs = plan(ids_late, logits)
+    core_scalar = core.reshape(1).astype(jnp.int32)
+    mixed, key, probs = mix(core_scalar, mine, theirs, ids, logits)
     own = lax.dynamic_slice_in_dim(out_grad, head * DS, DS, axis=1)
     ids_rows = jnp.pad(ids.astype(BF16), ((0, 8), (0, 0)))
     blocks = lax.all_gather(jnp.concatenate([own, ids_rows], axis=0), "zh", axis=0, tiled=False)
-    outgoing = select_rows(lax.axis_index("zh").reshape(1).astype(jnp.int32), blocks)
-    received = lax.all_to_all(outgoing, ("y", "zl"), split_axis=0, concat_axis=0, tiled=True)
-    received, mixed, key, probs = lax.optimization_barrier((received, mixed, key, probs))
-    part = slot_sums(received, mixed)
-    part = lax.all_to_all(part, ("y", "zl", "zh"), split_axis=0, concat_axis=0, tiled=True)
+    z = lax.axis_index("zh") * ZL + lax.axis_index("zl")
+    base = ((z - 2 * core) & (ZH * ZL - ZL)) + 2 * core
+    outgoing = select_rows(base.reshape(1).astype(jnp.int32), blocks)
+    received = lax.all_to_all(
+        outgoing,
+        ("core", "y", "zh", "zl"),
+        split_axis=0,
+        concat_axis=0,
+        tiled=True,
+        axis_index_groups=NEAR_GROUPS,
+    )
+    part = slot_sums(core_scalar, received, mixed)
+    part = lax.all_to_all(part, EXPERT, split_axis=0, concat_axis=0, tiled=True)
     part = lax.all_to_all(
         jnp.broadcast_to(part[None], (X,) + part.shape), "x", split_axis=0, concat_axis=0, tiled=True
     )

time: 126 us -> 122 us (0.968)
  Pallas kernels: 8.37 us -> 10.5 us
  waiting for transfers between devices: 17.4 us -> 15.4 us
  blocking collectives: 70.4 us -> 68.7 us
  local copies, waits for them, and re-layouts: 11 us -> 9.36 us
    all_to_all x1, starting transfers between devices: 5.12 us -> 9.23 us  [body(): lax.all_to_all(outgoing, ('core', 'y', 'zh', 'zl'), split_axis=0, concat_...]
    ppermute x1, starting transfers between devices: 6.64 us -> 2.54 us  [body(): lax.ppermute(jnp.concatenate([mine[:, :slots], weight_other], axis=1), 'c...]
    pallas_call x1, Pallas kernels: 2.58 us -> 4.87 us  [finish(): pl.pallas_call(final_kernel, out_shape=(jax.ShapeDtypeStruct((TOK, DS), B...]
    all_to_all x1, waiting for transfers between devices: 13.5 us -> 11.5 us  [body(): lax.all_to_all(outgoing, ('core', 'y', 'zh', 'zl'), split_axis=0, concat_...]
    all_gather x1, blocking collectives: 6.11 us -> 4.18 us  [body(): part = lax.all_gather(part, 'core', axis=0, tiled=False)]
    unnamed x20 -> x22, local copies, waits for them, and re-layouts: 10.9 us -> 9.17 us
    pallas_call x2 -> x1, Pallas kernels: 3.15 us -> 1.63 us  [mix(): pl.pallas_call(mix_kernel, out_shape=(jax.ShapeDtypeStruct((EXPERTS * CAP...]
    pallas_call x1, Pallas kernels: 0.27 us -> 1.61 us  [exchange_blocks(): pl.pallas_call(exchange_kernel, out_shape=jax.ShapeDtypeStruct((X, width,...]
  transfers between devices with their start and end apart: 3 -> 3, of which waited for: 2 -> 2; matrix products, arithmetic and copies ran while one was open for 0% -> 0% of each run, Pallas kernels for 3% -> 2%
where the time goes in v3:
time: 122 us
  blocking collectives  68.7 us (56%)
  starting transfers between devices  16.7 us (14%)
  waiting for transfers between devices  15.4 us (13%)
  Pallas kernels  10.5 us (9%)
  local copies, waits for them, and re-layouts  9.36 us (8%)
    all_gather x1, blocking collectives, body(): lax.all_gather(jnp.concatenate([own, ids_rows], axis=0), 'zh', axis=0, ti...  31.5 us
    all_to_all x1, blocking collectives, body(): part = lax.all_to_all(part, EXPERT, split_axis=0, concat_axis=0, tiled=True)  25.8 us
    all_to_all x1, waiting for transfers between devices, body(): lax.all_to_all(outgoing, ('core', 'y', 'zh', 'zl'), split_axis=0, concat_...  11.5 us
    all_to_all x1, starting transfers between devices, body(): lax.all_to_all(outgoing, ('core', 'y', 'zh', 'zl'), split_axis=0, concat_...  9.23 us
    unnamed x22, local copies, waits for them, and re-layouts  9.17 us
    all_to_all x1, blocking collectives, body(): lax.all_to_all(jnp.broadcast_to(part[None], (X,) + part.shape), 'x', spli...  7.21 us
    all_to_all x1, starting transfers between devices, body(): along = lax.all_to_all(along, 'x', split_axis=0, concat_axis=0, tiled=True)  4.97 us
    pallas_call x1, Pallas kernels, finish(): pl.pallas_call(final_kernel, out_shape=(jax.ShapeDtypeStruct((TOK, DS), B...  4.87 us
  transfers between devices with their start and end apart: 3, of which 2 were waited for; matrix products, arithmetic and copies ran while one was open for 0% of the time, Pallas kernels for 2%

profile of v3, /device:TPU:1, one launch (start us, length us, event | category | flops | bytes accessed | tf_op | source)
XLA Modules:
  0.0 121.6 jit_solution(10456621023808948209)
XLA Ops:
  0.6 0.0 copy-start
  0.6 0.0 copy-start.5
  0.7 1.2 copy-done.5
  1.8 1.0 copy-done.6
  2.8 1.6 %shard_map.78 = bf16[4,96,3072]{2,1,0:T(8,128)(2,1)S(1)} custom-call(bf16[2560,96]{1,0:T(8,128)(2,1)S(1)} %bitcast.17, bf16[96,2048]{1,0:T(8,128)(2,1)S(1)} %bitcast.18), custom_call_target="tpu_custom_call" | custom-call | tf_op jit(solution)/shard_map/pallas_call | solution.py:96
  4.4 0.0 copy-start.1
  4.4 1.4 %copy-done.1 = bf16[4,96,3072]{2,1,0:T(8,128)(2,1)} copy-done((bf16[4,96,3072]{2,1,0:T(8,128)(2,1)}, bf16[4,96,3072]{2,1,0:T(8,128)(2,1)S(1)}, u32[]{:S(2)}) %copy-start.1) | copy-done | bytes 2359320
  5.9 5.0 %all-to-all-start.1 = ((bf16[4,96,3072]{2,1,0:T(8,128)(2,1)}), bf16[4,96,3072]{2,1,0:T(8,128)(2,1)S(1)}, u32[]{:S(2)}, u32[]{:S(2)}) async-start(bf16[4,96,3072]{2,1,0:T(8,128)(2,1)} %copy-done.1), calls=%async_computation.1 | async-start | bytes 4718592 | tf_op jit(solution)/shard_map/all_to_all | solution.py:232
  10.8 0.0 copy-done
  10.9 0.0 copy-done.7
  10.9 31.5 %all-gather = bf16[1088,256]{1,0:T(8,128)(2,1)S(1)} all-gather(bf16[272,256]{1,0:T(8,128)(2,1)S(1)} %fusion.1), channel_id=2, replica_groups=mesh['x'=4,'core'=2,'y'=4,'zh'=4,'zl'=4] {'zh'}, dimensions={0}, use_global_device_ids=true | all-gather | bytes 696320 | tf_op jit(solution)/shard_map/all_gather | solution.py:242
  42.5 0.6 shard_map.77
  43.1 0.0 copy-start.2
  43.1 1.1 copy-done.2
  44.2 0.0 all-to-all-done.1
  44.2 9.2 %all-to-all-start = ((bf16[16,160,256]{2,1,0:T(8,128)(2,1)}), bf16[16,160,256]{2,1,0:T(8,128)(2,1)}, u32[]{:S(2)}, u32[]{:S(2)}) async-start(bf16[16,160,256]{2,1,0:T(8,128)(2,1)} %copy-done.2), calls=%async_computation | async-start | bytes 2621440 | tf_op jit(solution)/shard_map/all_to_all | solution.py:246
  53.4 0.1 slice.4
  53.6 0.0 copy-start.10
  53.6 0.1 pad_maximum_fusion
  53.7 2.5 %collective-permute-start = (bf16[384,2816]{1,0:T(8,128)(2,1)S(1)}, bf16[384,2816]{1,0:T(8,128)(2,1)S(1)}, u32[]{:S(2)}, u32[]{:S(2)}) collective-permute-start(bf16[384,2816]{1,0:T(8,128)(2,1)S(1)} %pad_maximum_fusion), channel_id=1, source_target_pairs={{0,64},{64,0},{1,65},{65,1},{2,66},{66,2},{3,67},{67,3},{4,68},{68... | collective-permute-start | bytes 6488072 | tf_op jit(solution)/shard_map/ppermute | solution.py:235
  56.3 3.9 %collective-permute-done.theirs_ref = bf16[384,2816]{1,0:T(8,128)(2,1)S(1)} collective-permute-done((bf16[384,2816]{1,0:T(8,128)(2,1)S(1)}, bf16[384,2816]{1,0:T(8,128)(2,1)S(1)}, u32[]{:S(2)}, u32[]{:S(2)}) %collective-permute-start) | collective-permute-done | bytes 2162720 | tf_op jit(solution)/shard_map/ppermute | solution.py:235
  60.1 1.6 %shard_map.79 = (f32[2560,256]{1,0:T(8,128)S(1)}, f32[64,256]{1,0:T(8,128)S(1)}, f32[64,256]{1,0:T(8,128)S(1)}) custom-call(s32[1]{0:T(128)} %bitcast.core_ref, bf16[384,3072]{1,0:T(8,128)(2,1)S(1)} %bitcast.15, bf16[384,2816]{1,0:T(8,128)(2,1)S(1)} %collective-permute-done.theirs_ref, s32[8,256]{1,0:T(8,128)S(1)} %bitcast.20, f32[8,256]{1,0:T(8,128)S(1)} %bitcast.21), custom_call_target="tpu_custom_call" | custom-call | tf_op jit(solution)/shard_map/pallas_call | solution.py:156
  61.8 1.5 %copy-done.3 = f32[2560,256]{1,0:T(8,128)} copy-done((f32[2560,256]{1,0:T(8,128)}, f32[2560,256]{1,0:T(8,128)S(1)}, u32[]{:S(2)}) %copy-start.3) | copy-done | bytes 2621464
  63.3 0.6 copy-done.8
  63.9 0.6 copy-done.9
  64.6 11.5 %all-to-all-done.rows_ref = bf16[16,160,256]{2,1,0:T(8,128)(2,1)} async-done(((bf16[16,160,256]{2,1,0:T(8,128)(2,1)}), bf16[16,160,256]{2,1,0:T(8,128)(2,1)}, u32[]{:S(2)}, u32[]{:S(2)}) %all-to-all-start) | async-done | bytes 1310752 | tf_op jit(solution)/shard_map/all_to_all | solution.py:246
  76.1 1.7 %copy-done.4 = f32[2560,256]{1,0:T(8,128)S(1)} copy-done((f32[2560,256]{1,0:T(8,128)S(1)}, f32[2560,256]{1,0:T(8,128)}, u32[]{:S(2)}) %copy-start.4) | copy-done | bytes 2621464
  77.8 1.7 %shard_map.80 = f32[64,1,128]{2,1,0:T(1,128)S(1)} custom-call(s32[1]{0:T(128)} %bitcast.core_ref, bf16[16,160,256]{2,1,0:T(8,128)(2,1)} %all-to-all-done.rows_ref, f32[2560,256]{1,0:T(8,128)S(1)} %copy-done.4), custom_call_target="tpu_custom_call" | custom-call | tf_op jit(solution)/shard_map/pallas_call | solution.py:180
  79.5 25.8 %all_to_all.20 = f32[64,1,128]{2,1,0:T(1,128)S(1)} all-to-all(f32[64,1,128]{2,1,0:T(1,128)S(1)} %shard_map.80), channel_id=1, replica_groups=mesh['x'=4,'core'=2,'y'=4,'zh'=4,'zl'=4] {'y','zh','zl'}, dimensions={0} | all-to-all | bytes 65536 | tf_op jit(solution)/shard_map/all_to_all | solution.py:255
  105.3 7.2 %all_to_all.21 = f32[4,64,1,128]{3,1,2,0:T(8,128)S(1)} all-to-all(f32[4,64,1,128]{3,1,2,0:T(8,128)S(1)} %broadcast_in_dim.9), channel_id=1, replica_groups=mesh['x'=4,'core'=2,'y'=4,'zh'=4,'zl'=4] {'x'}, dimensions={0} | all-to-all | bytes 262144 | tf_op jit(solution)/shard_map/all_to_all | solution.py:256
  112.6 4.2 %all-gather.1 = f32[8,64,1,128]{3,1,2,0:T(8,128)} all-gather(f32[4,64,1,128]{3,1,2,0:T(8,128)S(1)} %all_to_all.21), channel_id=3, replica_groups=mesh['x'=4,'core'=2,'y'=4,'zh'=4,'zl'=4] {'core'}, dimensions={0}, use_global_device_ids=true | all-gather | bytes 393216 | tf_op jit(solution)/shard_map/all_gather | solution.py:259
  116.7 4.9 %shard_map.81 = (bf16[256,256]{1,0:T(8,128)(2,1)}, f32[8,256]{1,0:T(8,128)}) custom-call(f32[2,4,64,1,128]{4,3,2,1,0:T(1,128)} %bitcast.22, f32[64,256]{1,0:T(8,128)} %copy-done.8, f32[64,256]{1,0:T(8,128)} %copy-done.9, s32[8,256]{1,0:T(8,128)} %bitcast.19, bf16[64,256]{1,0:T(8,128)(2,1)} %bitcast.24), custom_call_target="tpu_custom_call" | custom-call | tf_op jit(solution)/shard_map/pallas_call | solution.py:216
  (12 shorter events, 0.1 us)
Async XLA Ops:
  0.6 10.2 %copy-start = (bf16[256,2048]{1,0:T(8,128)(2,1)S(1)}, bf16[256,2048]{1,0:T(8,128)(2,1)}, u32[]{:S(2)}) copy-start(bf16[256,2048]{1,0:T(8,128)(2,1)} %param.6) | copy-start | bytes 3145732
  0.6 1.2 copy-start.5
  1.8 1.0 copy-start.6
  4.4 1.4 %copy-start.1 = (bf16[4,96,3072]{2,1,0:T(8,128)(2,1)}, bf16[4,96,3072]{2,1,0:T(8,128)(2,1)S(1)}, u32[]{:S(2)}) copy-start(bf16[4,96,3072]{2,1,0:T(8,128)(2,1)S(1)} %shard_map.78) | copy-start | bytes 7077892
  5.9 5.0 %copy-start.7 = (s32[256,8]{0,1:T(8,128)S(1)}, s32[256,8]{0,1:T(8,128)}, u32[]{:S(2)}) copy-start(s32[256,8]{0,1:T(8,128)} %param.7) | copy-start | bytes 24580
  5.9 38.3 %all-to-all-start.1 = ((bf16[4,96,3072]{2,1,0:T(8,128)(2,1)}), bf16[4,96,3072]{2,1,0:T(8,128)(2,1)S(1)}, u32[]{:S(2)}, u32[]{:S(2)}) async-start(bf16[4,96,3072]{2,1,0:T(8,128)(2,1)} %copy-done.1), calls=%async_computation.1 | async-start | bytes 4718592 | tf_op jit(solution)/shard_map/all_to_all | solution.py:232
  43.1 1.1 copy-start.2
  44.2 31.9 %all-to-all-start = ((bf16[16,160,256]{2,1,0:T(8,128)(2,1)}), bf16[16,160,256]{2,1,0:T(8,128)(2,1)}, u32[]{:S(2)}, u32[]{:S(2)}) async-start(bf16[16,160,256]{2,1,0:T(8,128)(2,1)} %copy-done.2), calls=%async_computation | async-start | bytes 2621440 | tf_op jit(solution)/shard_map/all_to_all | solution.py:246
  53.6 6.6 %copy-start.10 = (f32[256,8]{0,1:T(8,128)S(1)}, f32[256,8]{0,1:T(8,128)}, u32[]{:S(2)}) copy-start(f32[256,8]{0,1:T(8,128)} %param.8) | copy-start | bytes 24580
  53.7 6.4 %collective-permute-start = (bf16[384,2816]{1,0:T(8,128)(2,1)S(1)}, bf16[384,2816]{1,0:T(8,128)(2,1)S(1)}, u32[]{:S(2)}, u32[]{:S(2)}) collective-permute-start(bf16[384,2816]{1,0:T(8,128)(2,1)S(1)} %pad_maximum_fusion), channel_id=1, source_target_pairs={{0,64},{64,0},{1,65},{65,1},{2,66},{66,2},{3,67},{67,3},{4,68},{68... | collective-permute-start | bytes 6488072 | tf_op jit(solution)/shard_map/ppermute | solution.py:235
  61.8 1.5 %copy-start.3 = (f32[2560,256]{1,0:T(8,128)}, f32[2560,256]{1,0:T(8,128)S(1)}, u32[]{:S(2)}) copy-start(f32[2560,256]{1,0:T(8,128)S(1)} %get-tuple-element.7.mixed_ref) | copy-start | bytes 7864324
  63.3 0.6 copy-start.8
  63.9 0.6 copy-start.9
  76.1 1.7 %copy-start.4 = (f32[2560,256]{1,0:T(8,128)S(1)}, f32[2560,256]{1,0:T(8,128)}, u32[]{:S(2)}) copy-start(f32[2560,256]{1,0:T(8,128)} %copy-done.3) | copy-start | bytes 7864324

commit v4 on v3

--- a/solution.py
+++ b/solution.py
@@ -23,7 +23,11 @@
 BF16 = jnp.bfloat16
 
 
-def select_kernel(base_ref, blocks_ref, out_ref, picked):
+def in_hbm(array):
+    return pltpu.with_memory_space_constraint(array, pltpu.HBM)
+
+
+def select_kernel(base_ref, blocks_ref, out_hbm, picked, rows_out, sems):
     base = base_ref[0]
     j = lax.broadcasted_iota(jnp.int32, (NEAR, TOK), 0)
     expert = ((j // ZL) * (ZH * ZL) + ((base + j % ZL) & (ZH * ZL - 1))).astype(F32)
@@ -49,66 +53,107 @@
         picked[b] = jnp.dot(
             pick.astype(BF16), blocks_ref[b, 0:TOK, :], preferred_element_type=F32
         )
-    for e in range(NEAR):
-        rows = [picked[b, e * CAP : (e + 1) * CAP, :] for b in range(ZH)]
-        out_ref[e] = jnp.concatenate(rows, axis=0).astype(BF16)
+    copies = []
+    for y in range(Y):
+        for e in range(y * ZL, (y + 1) * ZL):
+            rows = [picked[b, e * CAP : (e + 1) * CAP, :] for b in range(ZH)]
+            rows_out[e] = jnp.concatenate(rows, axis=0).astype(BF16)
+        near = pl.ds(y * ZL, ZL)
+        copies.append(pltpu.make_async_copy(rows_out.at[near], out_hbm.at[near], sems.at[y]))
+        copies[-1].start()
+    for copy in copies:
+        copy.wait()
 
 
 def select_rows(base, blocks):
     return pl.pallas_call(
         select_kernel,
-        out_shape=jax.ShapeDtypeStruct((NEAR, ZH * CAP, DS), BF16),
+        out_shape=pltpu.HBM((NEAR, ZH * CAP, DS), BF16),
         in_specs=[
             pl.BlockSpec(memory_space=pltpu.SMEM),
             pl.BlockSpec(memory_space=pltpu.VMEM),
         ],
-        out_specs=pl.BlockSpec(memory_space=pltpu.VMEM),
-        scratch_shapes=[pltpu.VMEM((ZH, NEAR * CAP, DS), F32)],
+        out_specs=pl.BlockSpec(memory_space=pltpu.HBM),
+        scratch_shapes=[
+            pltpu.VMEM((ZH, NEAR * CAP, DS), F32),
+            pltpu.VMEM((NEAR, ZH * CAP, DS), BF16),
+            pltpu.SemaphoreType.DMA((Y,)),
+        ],
         compiler_params=pltpu.CompilerParams(vmem_limit_bytes=16 << 20),
     )(base, blocks)
 
 
-def exchange_kernel(hidden_hbm, weight_hbm, out_ref, hidden, weight, sems):
+def exchange_kernel(
+    head_ref, ids_hbm, grad_hbm, hidden_hbm, weight_hbm, out_hbm, block_ref, ids_ref, hidden, turned, sems
+):
     slots = EXPERTS * CAP
     piece = slots // 4
-    copies = [
-        pltpu.make_async_copy(
-            hidden_hbm.at[pl.ds(i * piece, piece)], hidden.at[pl.ds(i * piece, piece)], sems.at[i]
-        )
+    pieces = [pl.ds(i * piece, piece) for i in range(4)]
+    loads = [
+        pltpu.make_async_copy(hidden_hbm.at[pieces[i]], hidden.at[pieces[i]], sems.at[i])
         for i in range(4)
     ]
-    copies.append(pltpu.make_async_copy(weight_hbm, weight, sems.at[4]))
-    for copy in copies:
+    columns = pl.ds(pl.multiple_of(head_ref[0] * DS, DS), DS)
+    others = [
+        pltpu.make_async_copy(
+            weight_hbm.at[:, pl.ds(j * CORES * DS, CORES * DS)],
+            out_hbm.at[j, :, pl.ds(slots, CORES * DS)],
+            sems.at[4 + j],
+        )
+        for j in range(X)
+    ]
+    others.append(
+        pltpu.make_async_copy(grad_hbm.at[:, columns], block_ref.at[pl.ds(0, TOK)], sems.at[8])
+    )
+    load_ids = pltpu.make_async_copy(ids_hbm, ids_ref, sems.at[9])
+    for copy in loads + others + [load_ids]:
         copy.start()
+    load_ids.wait()
+    ids = ids_ref[...].astype(F32)
+    block_ref[TOK : TOK + 16, :] = jnp.concatenate([ids, jnp.zeros_like(ids)], axis=0).astype(BF16)
     for i in range(4):
-        copies[i].wait()
+        loads[i].wait()
         rows = slice(i * piece, (i + 1) * piece)
-        turned = hidden[rows, :].astype(F32).T.astype(BF16)
+        turned[:, rows] = hidden[rows, :].astype(F32).T.astype(BF16)
         for j in range(X):
-            out_ref[j, :, rows] = turned
-    copies[4].wait()
-    for j in range(X):
-        out_ref[j, :, slots:] = weight[:, j * CORES * DS : (j + 1) * CORES * DS]
-
-
-def exchange_blocks(hidden, weight):
+            copy = pltpu.make_async_copy(
+                turned.at[:, pieces[i]], out_hbm.at[j, :, pieces[i]], sems.at[10 + i * X + j]
+            )
+            copy.start()
+            others.append(copy)
+    for copy in others:
+        copy.wait()
+
+
+def exchange_blocks(head, ids, grad, hidden, weight):
     width = weight.shape[0]
+    far = pl.BlockSpec(memory_space=pltpu.HBM)
     return pl.pallas_call(
         exchange_kernel,
-        out_shape=jax.ShapeDtypeStruct((X, width, EXPERTS * CAP + CORES * DS), BF16),
-        in_specs=[pl.BlockSpec(memory_space=pl.ANY)] * 2,
-        out_specs=pl.BlockSpec(memory_space=pltpu.VMEM),
+        out_shape=(
+            pltpu.HBM((X, width, EXPERTS * CAP + CORES * DS), BF16),
+            jax.ShapeDtypeStruct((TOK + 16, DS), BF16),
+        ),
+        in_specs=[
+            pl.BlockSpec(memory_space=pltpu.SMEM),
+            far,
+            far,
+            far,
+            far,
+        ],
+        out_specs=(far, pl.BlockSpec(memory_space=pltpu.VMEM)),
         scratch_shapes=[
+            pltpu.VMEM(ids.shape, jnp.int32),
             pltpu.VMEM(hidden.shape, BF16),
-            pltpu.VMEM(weight.shape, BF16),
-            pltpu.SemaphoreType.DMA((5,)),
-        ],
-        compiler_params=pltpu.CompilerParams(vmem_limit_bytes=16 << 20),
-    )(hidden, weight)
+            pltpu.VMEM((width, EXPERTS * CAP), BF16),
+            pltpu.SemaphoreType.DMA((10 + 4 * X,)),
+        ],
+        compiler_params=pltpu.CompilerParams(vmem_limit_bytes=16 << 20),
+    )(head, in_hbm(ids), in_hbm(grad), in_hbm(hidden), in_hbm(weight))
 
 
 def mix_kernel(
-    core_ref, mine_ref, theirs_ref, ids_ref, logits_ref, out_ref, key_ref, probs_ref
+    core_ref, mine_ref, theirs_ref, ids_ref, logits_ref, out_hbm, key_ref, probs_ref, out_ref, sems
 ):
     plan(ids_ref[...], logits_ref[...], key_ref, probs_ref)
     slots = EXPERTS * CAP
@@ -118,6 +163,7 @@
     )
     group = ZH * ZL * CAP
     contract = (((0,), (0,)), ((), ()))
+    copies = []
     for y in range(Y):
         cols = slice(y * group, (y + 1) * group)
         mixed = lax.dot_general(
@@ -131,6 +177,11 @@
                 src = (zh * ZL + zl) * CAP
                 dst = pl.multiple_of(y * group + (place * ZH + zh) * CAP, 8)
                 out_ref[pl.ds(dst, CAP), :] = mixed[src : src + CAP, :]
+        rows = pl.ds(y * group, group)
+        copies.append(pltpu.make_async_copy(out_ref.at[rows], out_hbm.at[rows], sems.at[y]))
+        copies[-1].start()
+    for copy in copies:
+        copy.wait()
 
 
 def plan(ids, logits, key_ref, probs_ref):
@@ -155,45 +206,85 @@
     table = jax.ShapeDtypeStruct((EXPERTS, TOK), F32)
     return pl.pallas_call(
         mix_kernel,
-        out_shape=(jax.ShapeDtypeStruct((EXPERTS * CAP, DS), F32), table, table),
+        out_shape=(pltpu.HBM((EXPERTS * CAP, DS), F32), table, table),
         in_specs=[pl.BlockSpec(memory_space=pltpu.SMEM)]
         + [pl.BlockSpec(memory_space=pltpu.VMEM)] * 4,
-        out_specs=(pl.BlockSpec(memory_space=pltpu.VMEM),) * 3,
+        out_specs=(pl.BlockSpec(memory_space=pltpu.HBM),) + (pl.BlockSpec(memory_space=pltpu.VMEM),) * 2,
+        scratch_shapes=[pltpu.VMEM((EXPERTS * CAP, DS), F32), pltpu.SemaphoreType.DMA((Y,))],
         compiler_params=pltpu.CompilerParams(vmem_limit_bytes=16 << 20),
     )(core, mine, theirs, ids, logits)
 
 
-def value_kernel(core_ref, rows_ref, mixed_ref, out_ref):
+def value_kernel(core_ref, rows_hbm, mixed_hbm, out_ref, rows_ref, mixed_ref, sems):
+    steps = 8
+    per = NEAR // steps
+    copies = []
+    for i in range(steps):
+        near, slots = pl.ds(i * per, per), pl.ds(i * per * ZH * CAP, per * ZH * CAP)
+        copies.append(
+            (
+                pltpu.make_async_copy(rows_hbm.at[near], rows_ref.at[near], sems.at[0, i]),
+                pltpu.make_async_copy(mixed_hbm.at[slots], mixed_ref.at[slots], sems.at[1, i]),
+            )
+        )
+    for pair in copies:
+        for copy in pair:
+            copy.start()
     own_lane = lax.broadcasted_iota(jnp.int32, (CAP, 128), 0) == lax.broadcasted_iota(
         jnp.int32, (CAP, 128), 1
     )
-    for e in range(NEAR):
-        rows = rows_ref[e].astype(F32) * mixed_ref[e * ZH * CAP : (e + 1) * ZH * CAP, :]
-        sums = jnp.sum(rows[:, 0:128] + rows[:, 128:256], axis=1, keepdims=True)
-        for b in range(ZH):
-            lanes = jnp.where(own_lane, sums[b * CAP : (b + 1) * CAP, :], 0.0)
-            place = (e // ZL * ZH + b) * ZL + ((e % ZL) ^ (2 * core_ref[0]))
-            out_ref[place] = jnp.sum(lanes, axis=0, keepdims=True)
+    for i in range(steps):
+        for copy in copies[i]:
+            copy.wait()
+        for e in range(i * per, (i + 1) * per):
+            rows = rows_ref[e].astype(F32) * mixed_ref[e * ZH * CAP : (e + 1) * ZH * CAP, :]
+            sums = jnp.sum(rows[:, 0:128] + rows[:, 128:256], axis=1, keepdims=True)
+            for b in range(ZH):
+                lanes = jnp.where(own_lane, sums[b * CAP : (b + 1) * CAP, :], 0.0)
+                place = (e // ZL * ZH + b) * ZL + ((e % ZL) ^ (2 * core_ref[0]))
+                out_ref[place] = jnp.sum(lanes, axis=0, keepdims=True)
 
 
 def slot_sums(core, rows, mixed):
     return pl.pallas_call(
         value_kernel,
         out_shape=jax.ShapeDtypeStruct((EXPERTS, 1, 128), F32),
-        in_specs=[pl.BlockSpec(memory_space=pltpu.SMEM)]
-        + [pl.BlockSpec(memory_space=pltpu.VMEM)] * 2,
+        in_specs=[
+            pl.BlockSpec(memory_space=pltpu.SMEM),
+            pl.BlockSpec(memory_space=pltpu.HBM),
+            pl.BlockSpec(memory_space=pltpu.HBM),
+        ],
         out_specs=pl.BlockSpec(memory_space=pltpu.VMEM),
-        compiler_params=pltpu.CompilerParams(vmem_limit_bytes=16 << 20),
-    )(core, rows, mixed)
-
-
-def final_kernel(back_ref, key_ref, probs_ref, ids_ref, router_ref, grad_ref, weight_ref):
-    parts = back_ref[0, 0]
+        scratch_shapes=[
+            pltpu.VMEM(rows.shape, BF16),
+            pltpu.VMEM(mixed.shape, F32),
+            pltpu.SemaphoreType.DMA((2, 8)),
+        ],
+        compiler_params=pltpu.CompilerParams(vmem_limit_bytes=16 << 20),
+    )(core, in_hbm(rows), in_hbm(mixed))
+
+
+def final_kernel(
+    parts_hbm, key_hbm, probs_hbm, ids_ref, router_hbm, grad_ref, weight_ref,
+    parts_ref, key_ref, probs_ref, router_ref, total, sems,
+):
+    copies = [
+        pltpu.make_async_copy(far, near, sems.at[i])
+        for i, (far, near) in enumerate(
+            [(parts_hbm, parts_ref), (key_hbm, key_ref), (probs_hbm, probs_ref), (router_hbm, router_ref)]
+        )
+    ]
+    for copy in copies:
+        copy.start()
+    for copy in copies:
+        copy.wait()
+    parts = parts_ref[0, 0]
     for c in range(CORES):
         for i in range(X):
             if c or i:
-                parts = parts + back_ref[c, i]
-    back = parts.reshape(EXPERTS, 128)
+                parts = parts + parts_ref[c, i]
+    total[...] = parts.reshape(EXPERTS, 128)
+    back = total[...]
     key = key_ref[...]
     probs = probs_ref[...]
     dense = jnp.zeros((EXPERTS, TOK), F32)
@@ -212,14 +303,26 @@
         )
 
 
-def finish(back, key, probs, ids, router):
+def finish(parts, key, probs, ids, router):
+    far, near = pl.BlockSpec(memory_space=pltpu.HBM), pl.BlockSpec(memory_space=pltpu.VMEM)
     return pl.pallas_call(
         final_kernel,
         out_shape=(
             jax.ShapeDtypeStruct((TOK, DS), BF16),
             jax.ShapeDtypeStruct((TOPK, TOK), F32),
         ),
-    )(back, key, probs, ids, router)
+        in_specs=[far, far, far, near, far],
+        out_specs=(near, near),
+        scratch_shapes=[
+            pltpu.VMEM(parts.shape, F32),
+            pltpu.VMEM(key.shape, F32),
+            pltpu.VMEM(probs.shape, F32),
+            pltpu.VMEM(router.shape, BF16),
+            pltpu.VMEM((EXPERTS, 128), F32),
+            pltpu.SemaphoreType.DMA((4,)),
+        ],
+        compiler_params=pltpu.CompilerParams(vmem_limit_bytes=16 << 20),
+    )(in_hbm(parts), in_hbm(key), in_hbm(probs), ids, in_hbm(router))
 
 
 def body(out_grad, expert_ids, chosen_logits, down_weight, saved_hidden, router_weight):
@@ -228,7 +331,13 @@
     width = down_weight.shape[1]
     slots = EXPERTS * CAP
     ids, logits = expert_ids.T, chosen_logits.T
-    along = exchange_blocks(saved_hidden[0].reshape(slots, width), down_weight[0])
+    along, block = exchange_blocks(
+        head.reshape(1).astype(jnp.int32),
+        ids,
+        out_grad,
+        saved_hidden[0].reshape(slots, width),
+        down_weight[0],
+    )
     along = lax.all_to_all(along, "x", split_axis=0, concat_axis=0, tiled=True)
     mine = along.reshape(X * width, slots + CORES * DS)
     weight_other = lax.dynamic_slice_in_dim(mine, slots + (1 - core) * DS, DS, axis=1)
@@ -237,9 +346,7 @@
     )
     core_scalar = core.reshape(1).astype(jnp.int32)
     mixed, key, probs = mix(core_scalar, mine, theirs, ids, logits)
-    own = lax.dynamic_slice_in_dim(out_grad, head * DS, DS, axis=1)
-    ids_rows = jnp.pad(ids.astype(BF16), ((0, 8), (0, 0)))
-    blocks = lax.all_gather(jnp.concatenate([own, ids_rows], axis=0), "zh", axis=0, tiled=False)
+    blocks = lax.all_gather(block, "zh", axis=0, tiled=False)
     z = lax.axis_index("zh") * ZL + lax.axis_index("zl")
     base = ((z - 2 * core) & (ZH * ZL - ZL)) + 2 * core
     outgoing = select_rows(base.reshape(1).astype(jnp.int32), blocks)

time: 122 us -> 127 us (1.041)
  Pallas kernels: 10.5 us -> 22.6 us
  local copies, waits for them, and re-layouts: 9.36 us -> 1.42 us
    pallas_call x3, Pallas kernels: 3.88 us -> 17.5 us  [the longest x1 13.3 us: exchange_blocks(): pl.pallas_call(exchange_kernel, out_shape=(pltpu.HBM((X, width, EXPERTS *...]
    unnamed x22 -> x8, local copies, waits for them, and re-layouts: 9.17 us -> 1.25 us
    pallas_call x1, Pallas kernels: 4.87 us -> 2.65 us  [finish(): pl.pallas_call(final_kernel, out_shape=(jax.ShapeDtypeStruct((TOK, DS), B...]
  transfers between devices with their start and end apart: 3 -> 3, of which waited for: 2 -> 2; matrix products, arithmetic and copies ran while one was open for 0% -> 0% of each run, Pallas kernels for 2% -> 3%
where the time goes in v4:
time: 127 us; the launch traced here: 126 us
  blocking collectives  68.7 us (54%)
  Pallas kernels  22.6 us (18%)
  starting transfers between devices  16.6 us (13%)
  waiting for transfers between devices  16 us (13%)
  local copies, waits for them, and re-layouts  1.42 us (1%)
    all_gather x1, blocking collectives, body(): blocks = lax.all_gather(block, 'zh', axis=0, tiled=False)  31.5 us
    all_to_all x1, blocking collectives, body(): part = lax.all_to_all(part, EXPERT, split_axis=0, concat_axis=0, tiled=True)  25.8 us
    pallas_call x1, Pallas kernels, exchange_blocks(): pl.pallas_call(exchange_kernel, out_shape=(pltpu.HBM((X, width, EXPERTS *...  13.3 us
    all_to_all x1, waiting for transfers between devices, body(): lax.all_to_all(outgoing, ('core', 'y', 'zh', 'zl'), split_axis=0, concat_...  12.2 us
    all_to_all x1, starting transfers between devices, body(): lax.all_to_all(outgoing, ('core', 'y', 'zh', 'zl'), split_axis=0, concat_...  9.41 us
    all_to_all x1, blocking collectives, body(): lax.all_to_all(jnp.broadcast_to(part[None], (X,) + part.shape), 'x', spli...  7.21 us
    all_to_all x1, starting transfers between devices, body(): along = lax.all_to_all(along, 'x', split_axis=0, concat_axis=0, tiled=True)  4.85 us
    all_gather x1, blocking collectives, body(): part = lax.all_gather(part, 'core', axis=0, tiled=False)  4.18 us
  transfers between devices with their start and end apart: 3, of which 2 were waited for; matrix products, arithmetic and copies ran while one was open for 0% of the time, Pallas kernels for 3%

profile of v4, /device:TPU:1, one launch (start us, length us, event | category | flops | bytes accessed | tf_op | source)
XLA Modules:
  0.0 126.2 jit_solution(1356624392715587820)
XLA Ops:
  0.6 13.3 %shard_map.77 = (bf16[4,96,3072]{2,1,0:T(8,128)(2,1)}, bf16[272,256]{1,0:T(8,128)(2,1)S(1)}) custom-call(s32[1]{0:T(128)} %bitcast.2.head_ref, s32[8,256]{1,0:T(8,128)} %bitcast.17, bf16[256,2048]{1,0:T(8,128)(2,1)} %grad_hbm.1, bf16[2560,96]{1,0:T(8,128)(2,1)} %bitcast.22, bf16[96,2048]{1,0:T(8,128)(2,1)} %bitcast.23), custom_call_target="tpu_custom_call" | custom-call | tf_op jit(solution)/shard_map/pallas_call | solution.py:131
  13.9 4.9 %all-to-all-start.1 = ((bf16[4,96,3072]{2,1,0:T(8,128)(2,1)}), bf16[4,96,3072]{2,1,0:T(8,128)(2,1)S(1)}, u32[]{:S(2)}, u32[]{:S(2)}) async-start(bf16[4,96,3072]{2,1,0:T(8,128)(2,1)} %get-tuple-element.10), calls=%async_computation.1 | async-start | bytes 4718592 | tf_op jit(solution)/shard_map/all_to_all | solution.py:341
  18.8 31.5 %all-gather = bf16[1088,256]{1,0:T(8,128)(2,1)S(1)} all-gather(bf16[272,256]{1,0:T(8,128)(2,1)S(1)} %get-tuple-element.9), channel_id=2, replica_groups=mesh['x'=4,'core'=2,'y'=4,'zh'=4,'zl'=4] {'zh'}, dimensions={0}, use_global_device_ids=true | all-gather | bytes 696320 | tf_op jit(solution)/shard_map/all_gather | solution.py:349
  50.3 1.6 %shard_map.78 = bf16[16,160,256]{2,1,0:T(8,128)(2,1)} custom-call(s32[1]{0:T(128)} %bitcast.1.base_ref, bf16[4,272,256]{2,1,0:T(8,128)(2,1)S(1)} %bitcast.16), custom_call_target="tpu_custom_call" | custom-call | tf_op jit(solution)/shard_map/pallas_call | solution.py:69
  51.9 0.0 all-to-all-done.1
  51.9 9.4 %all-to-all-start = ((bf16[16,160,256]{2,1,0:T(8,128)(2,1)}), bf16[16,160,256]{2,1,0:T(8,128)(2,1)}, u32[]{:S(2)}, u32[]{:S(2)}) async-start(bf16[16,160,256]{2,1,0:T(8,128)(2,1)} %shard_map.78), calls=%async_computation | async-start | bytes 2621440 | tf_op jit(solution)/shard_map/all_to_all | solution.py:353
  61.3 0.1 slice.4
  61.5 0.0 copy-start
  61.5 0.0 copy-start.3
  61.5 0.1 pad_maximum_fusion
  61.7 2.4 %collective-permute-start = (bf16[384,2816]{1,0:T(8,128)(2,1)S(1)}, bf16[384,2816]{1,0:T(8,128)(2,1)S(1)}, u32[]{:S(2)}, u32[]{:S(2)}) collective-permute-start(bf16[384,2816]{1,0:T(8,128)(2,1)S(1)} %pad_maximum_fusion), channel_id=1, source_target_pairs={{0,64},{64,0},{1,65},{65,1},{2,66},{66,2},{3,67},{67,3},{4,68},{68... | collective-permute-start | bytes 6488072 | tf_op jit(solution)/shard_map/ppermute | solution.py:344
  64.1 3.9 %collective-permute-done.theirs_ref = bf16[384,2816]{1,0:T(8,128)(2,1)S(1)} collective-permute-done((bf16[384,2816]{1,0:T(8,128)(2,1)S(1)}, bf16[384,2816]{1,0:T(8,128)(2,1)S(1)}, u32[]{:S(2)}, u32[]{:S(2)}) %collective-permute-start) | collective-permute-done | bytes 2162720 | tf_op jit(solution)/shard_map/ppermute | solution.py:344
  67.9 0.0 copy-done
  67.9 0.0 copy-done.3
  67.9 2.7 %shard_map.79 = (f32[2560,256]{1,0:T(8,128)}, f32[64,256]{1,0:T(8,128)S(1)}, f32[64,256]{1,0:T(8,128)S(1)}) custom-call(s32[1]{0:T(128)} %bitcast.core_ref, bf16[384,3072]{1,0:T(8,128)(2,1)S(1)} %bitcast.15, bf16[384,2816]{1,0:T(8,128)(2,1)S(1)} %collective-permute-done.theirs_ref, s32[8,256]{1,0:T(8,128)S(1)} %bitcast.18, f32[8,256]{1,0:T(8,128)S(1)} %bitcast.20), custom_call_target="tpu_custom_call" | custom-call | tf_op jit(solution)/shard_map/pallas_call | solution.py:207
  70.6 0.0 copy-start.1
  70.6 0.6 copy-done.1
  71.2 0.0 copy-start.2
  71.2 0.6 copy-done.2
  71.8 12.2 %all-to-all-done.rows_hbm = bf16[16,160,256]{2,1,0:T(8,128)(2,1)} async-done(((bf16[16,160,256]{2,1,0:T(8,128)(2,1)}), bf16[16,160,256]{2,1,0:T(8,128)(2,1)}, u32[]{:S(2)}, u32[]{:S(2)}) %all-to-all-start) | async-done | bytes 1310752 | tf_op jit(solution)/shard_map/all_to_all | solution.py:353
  84.0 2.4 %shard_map.80 = f32[64,1,128]{2,1,0:T(1,128)S(1)} custom-call(s32[1]{0:T(128)} %bitcast.core_ref, bf16[16,160,256]{2,1,0:T(8,128)(2,1)} %all-to-all-done.rows_hbm, f32[2560,256]{1,0:T(8,128)} %get-tuple-element.11.mixed_hbm), custom_call_target="tpu_custom_call" | custom-call | tf_op jit(solution)/shard_map/pallas_call | solution.py:249
  86.4 25.8 %all_to_all.20 = f32[64,1,128]{2,1,0:T(1,128)S(1)} all-to-all(f32[64,1,128]{2,1,0:T(1,128)S(1)} %shard_map.80), channel_id=1, replica_groups=mesh['x'=4,'core'=2,'y'=4,'zh'=4,'zl'=4] {'y','zh','zl'}, dimensions={0} | all-to-all | bytes 65536 | tf_op jit(solution)/shard_map/all_to_all | solution.py:362
  112.2 7.2 %all_to_all.21 = f32[4,64,1,128]{3,1,2,0:T(8,128)S(1)} all-to-all(f32[4,64,1,128]{3,1,2,0:T(8,128)S(1)} %broadcast_in_dim.9), channel_id=1, replica_groups=mesh['x'=4,'core'=2,'y'=4,'zh'=4,'zl'=4] {'x'}, dimensions={0} | all-to-all | bytes 262144 | tf_op jit(solution)/shard_map/all_to_all | solution.py:363
  119.4 4.2 %all-gather.1 = f32[8,64,1,128]{3,1,2,0:T(8,128)} all-gather(f32[4,64,1,128]{3,1,2,0:T(8,128)S(1)} %all_to_all.21), channel_id=3, replica_groups=mesh['x'=4,'core'=2,'y'=4,'zh'=4,'zl'=4] {'core'}, dimensions={0}, use_global_device_ids=true | all-gather | bytes 393216 | tf_op jit(solution)/shard_map/all_gather | solution.py:366
  123.6 2.6 %shard_map.81 = (bf16[256,256]{1,0:T(8,128)(2,1)}, f32[8,256]{1,0:T(8,128)}) custom-call(f32[2,4,64,1,128]{4,3,2,1,0:T(1,128)} %bitcast.21, f32[64,256]{1,0:T(8,128)} %copy-done.1, f32[64,256]{1,0:T(8,128)} %copy-done.2, s32[8,256]{1,0:T(8,128)S(1)} %bitcast.19, bf16[64,256]{1,0:T(8,128)(2,1)} %bitcast.25), custom_call_target="tpu_custom_call" | custom-call | tf_op jit(solution)/shard_map/pallas_call | solution.py:308
  (2 shorter events, 0.0 us)
Async XLA Ops:
  13.9 38.0 %all-to-all-start.1 = ((bf16[4,96,3072]{2,1,0:T(8,128)(2,1)}), bf16[4,96,3072]{2,1,0:T(8,128)(2,1)S(1)}, u32[]{:S(2)}, u32[]{:S(2)}) async-start(bf16[4,96,3072]{2,1,0:T(8,128)(2,1)} %get-tuple-element.10), calls=%async_computation.1 | async-start | bytes 4718592 | tf_op jit(solution)/shard_map/all_to_all | solution.py:341
  51.9 32.1 %all-to-all-start = ((bf16[16,160,256]{2,1,0:T(8,128)(2,1)}), bf16[16,160,256]{2,1,0:T(8,128)(2,1)}, u32[]{:S(2)}, u32[]{:S(2)}) async-start(bf16[16,160,256]{2,1,0:T(8,128)(2,1)} %shard_map.78), calls=%async_computation | async-start | bytes 2621440 | tf_op jit(solution)/shard_map/all_to_all | solution.py:353
  61.5 6.4 %copy-start = (s32[256,8]{0,1:T(8,128)S(1)}, s32[256,8]{0,1:T(8,128)}, u32[]{:S(2)}) copy-start(s32[256,8]{0,1:T(8,128)} %param.7) | copy-start | bytes 24580
  61.5 6.4 %copy-start.3 = (f32[256,8]{0,1:T(8,128)S(1)}, f32[256,8]{0,1:T(8,128)}, u32[]{:S(2)}) copy-start(f32[256,8]{0,1:T(8,128)} %param.8) | copy-start | bytes 24580
  61.7 6.2 %collective-permute-start = (bf16[384,2816]{1,0:T(8,128)(2,1)S(1)}, bf16[384,2816]{1,0:T(8,128)(2,1)S(1)}, u32[]{:S(2)}, u32[]{:S(2)}) collective-permute-start(bf16[384,2816]{1,0:T(8,128)(2,1)S(1)} %pad_maximum_fusion), channel_id=1, source_target_pairs={{0,64},{64,0},{1,65},{65,1},{2,66},{66,2},{3,67},{67,3},{4,68},{68... | collective-permute-start | bytes 6488072 | tf_op jit(solution)/shard_map/ppermute | solution.py:344
  70.6 0.6 copy-start.1
  71.2 0.6 copy-start.2

commit v5 on v4

--- a/solution.py
+++ b/solution.py
@@ -84,7 +84,7 @@
 
 
 def exchange_kernel(
-    head_ref, ids_hbm, grad_hbm, hidden_hbm, weight_hbm, out_hbm, block_ref, ids_ref, hidden, turned, sems
+    head_ref, ids_hbm, grad_hbm, hidden_hbm, weight_hbm, out_hbm, block_ref, ids_ref, hidden, weight, turned, sems
 ):
     slots = EXPERTS * CAP
     piece = slots // 4
@@ -94,20 +94,14 @@
         for i in range(4)
     ]
     columns = pl.ds(pl.multiple_of(head_ref[0] * DS, DS), DS)
-    others = [
-        pltpu.make_async_copy(
-            weight_hbm.at[:, pl.ds(j * CORES * DS, CORES * DS)],
-            out_hbm.at[j, :, pl.ds(slots, CORES * DS)],
-            sems.at[4 + j],
-        )
-        for j in range(X)
-    ]
-    others.append(
-        pltpu.make_async_copy(grad_hbm.at[:, columns], block_ref.at[pl.ds(0, TOK)], sems.at[8])
-    )
+    load_weight = pltpu.make_async_copy(weight_hbm, weight, sems.at[10])
     load_ids = pltpu.make_async_copy(ids_hbm, ids_ref, sems.at[9])
-    for copy in loads + others + [load_ids]:
+    load_grad = pltpu.make_async_copy(
+        grad_hbm.at[:, columns], block_ref.at[pl.ds(0, TOK)], sems.at[8]
+    )
+    for copy in loads + [load_weight, load_ids, load_grad]:
         copy.start()
+    others = [load_grad]
     load_ids.wait()
     ids = ids_ref[...].astype(F32)
     block_ref[TOK : TOK + 16, :] = jnp.concatenate([ids, jnp.zeros_like(ids)], axis=0).astype(BF16)
@@ -117,10 +111,19 @@
         turned[:, rows] = hidden[rows, :].astype(F32).T.astype(BF16)
         for j in range(X):
             copy = pltpu.make_async_copy(
-                turned.at[:, pieces[i]], out_hbm.at[j, :, pieces[i]], sems.at[10 + i * X + j]
+                turned.at[:, pieces[i]], out_hbm.at[j, :, pieces[i]], sems.at[11 + i * X + j]
             )
             copy.start()
             others.append(copy)
+    load_weight.wait()
+    for j in range(X):
+        copy = pltpu.make_async_copy(
+            weight.at[:, pl.ds(j * CORES * DS, CORES * DS)],
+            out_hbm.at[j, :, pl.ds(slots, CORES * DS)],
+            sems.at[4 + j],
+        )
+        copy.start()
+        others.append(copy)
     for copy in others:
         copy.wait()
 
@@ -145,8 +148,9 @@
         scratch_shapes=[
             pltpu.VMEM(ids.shape, jnp.int32),
             pltpu.VMEM(hidden.shape, BF16),
+            pltpu.VMEM(weight.shape, BF16),
             pltpu.VMEM((width, EXPERTS * CAP), BF16),
-            pltpu.SemaphoreType.DMA((10 + 4 * X,)),
+            pltpu.SemaphoreType.DMA((11 + 4 * X,)),
         ],
         compiler_params=pltpu.CompilerParams(vmem_limit_bytes=16 << 20),
     )(head, in_hbm(ids), in_hbm(grad), in_hbm(hidden), in_hbm(weight))
@@ -278,11 +282,9 @@
         copy.start()
     for copy in copies:
         copy.wait()
-    parts = parts_ref[0, 0]
-    for c in range(CORES):
-        for i in range(X):
-            if c or i:
-                parts = parts + parts_ref[c, i]
+    parts = parts_ref[0]
+    for i in range(1, X):
+        parts = parts + parts_ref[i]
     total[...] = parts.reshape(EXPERTS, 128)
     back = total[...]
     key = key_ref[...]
@@ -359,11 +361,10 @@
         axis_index_groups=NEAR_GROUPS,
     )
     part = slot_sums(core_scalar, received, mixed)
-    part = lax.all_to_all(part, EXPERT, split_axis=0, concat_axis=0, tiled=True)
-    part = lax.all_to_all(
-        jnp.broadcast_to(part[None], (X,) + part.shape), "x", split_axis=0, concat_axis=0, tiled=True
-    )
-    part = lax.all_gather(part, "core", axis=0, tiled=False)
+    part = jnp.sum(lax.all_gather(part, "core", axis=0, tiled=False), axis=0)
+    part = jnp.broadcast_to(part[None], (X,) + part.shape).reshape(X * EXPERTS, 1, 128)
+    part = lax.all_to_all(part, ("x",) + EXPERT, split_axis=0, concat_axis=0, tiled=True)
+    part = part.reshape(X, EXPERTS, 1, 128)
     grad, weight_grad = finish(part, key, probs, ids, router_weight.T)
     return grad, weight_grad.T
 

time: 127 us -> 115 us (0.906)
  Pallas kernels: 22.6 us -> 12.2 us
  blocking collectives: 68.7 us -> 67.2 us
    pallas_call x1, Pallas kernels: 13.3 us -> 2.94 us  [exchange_blocks(): pl.pallas_call(exchange_kernel, out_shape=(pltpu.HBM((X, width, EXPERTS *...]
    all_gather x1, blocking collectives: 4.18 us -> 1.85 us  [body(): part = jnp.sum(lax.all_gather(part, 'core', axis=0, tiled=False), axis=0)]
    all_to_all x2 -> x1, blocking collectives: 33 us -> 33.8 us  [body(): lax.all_to_all(part, ('x',) + EXPERT, split_axis=0, concat_axis=0, tiled=...]
  transfers between devices with their start and end apart: 3 -> 3, of which waited for: 2 -> 2; matrix products, arithmetic and copies ran while one was open for 0% -> 0% of each run, Pallas kernels for 3% -> 4%
where the time goes in v5:
time: 115 us; the launch traced here: 114 us
  blocking collectives  67.2 us (58%)
  starting transfers between devices  16.6 us (14%)
  waiting for transfers between devices  16 us (14%)
  Pallas kernels  12.2 us (11%)
  local copies, waits for them, and re-layouts  1.42 us (1%)
    all_to_all x1, blocking collectives, body(): lax.all_to_all(part, ('x',) + EXPERT, split_axis=0, concat_axis=0, tiled=...  33.8 us
    all_gather x1, blocking collectives, body(): blocks = lax.all_gather(block, 'zh', axis=0, tiled=False)  31.5 us
    all_to_all x1, waiting for transfers between devices, body(): lax.all_to_all(outgoing, ('core', 'y', 'zh', 'zl'), split_axis=0, concat_...  12.2 us
    all_to_all x1, starting transfers between devices, body(): lax.all_to_all(outgoing, ('core', 'y', 'zh', 'zl'), split_axis=0, concat_...  9.4 us
    all_to_all x1, starting transfers between devices, body(): along = lax.all_to_all(along, 'x', split_axis=0, concat_axis=0, tiled=True)  4.85 us
    ppermute x1, waiting for transfers between devices, body(): lax.ppermute(jnp.concatenate([mine[:, :slots], weight_other], axis=1), 'c...  3.86 us
    pallas_call x1, Pallas kernels, exchange_blocks(): pl.pallas_call(exchange_kernel, out_shape=(pltpu.HBM((X, width, EXPERTS *...  2.94 us
    pallas_call x1, Pallas kernels, mix(): pl.pallas_call(mix_kernel, out_shape=(pltpu.HBM((EXPERTS * CAP, DS), F32)...  2.66 us
  transfers between devices with their start and end apart: 3, of which 2 were waited for; matrix products, arithmetic and copies ran while one was open for 0% of the time, Pallas kernels for 4%

profile of v5, /device:TPU:1, one launch (start us, length us, event | category | flops | bytes accessed | tf_op | source)
XLA Modules:
  0.0 114.3 jit_solution(13551260107122880067)
XLA Ops:
  0.6 2.9 %shard_map.77 = (bf16[4,96,3072]{2,1,0:T(8,128)(2,1)}, bf16[272,256]{1,0:T(8,128)(2,1)S(1)}) custom-call(s32[1]{0:T(128)} %bitcast.2.head_ref, s32[8,256]{1,0:T(8,128)} %bitcast.20, bf16[256,2048]{1,0:T(8,128)(2,1)} %grad_hbm.1, bf16[2560,96]{1,0:T(8,128)(2,1)} %bitcast.24, bf16[96,2048]{1,0:T(8,128)(2,1)} %bitcast.27), custom_call_target="tpu_custom_call" | custom-call | tf_op jit(solution)/shard_map/pallas_call | solution.py:134
  3.6 4.9 %all-to-all-start.1 = ((bf16[4,96,3072]{2,1,0:T(8,128)(2,1)}), bf16[4,96,3072]{2,1,0:T(8,128)(2,1)S(1)}, u32[]{:S(2)}, u32[]{:S(2)}) async-start(bf16[4,96,3072]{2,1,0:T(8,128)(2,1)} %get-tuple-element.10), calls=%async_computation.1 | async-start | bytes 4718592 | tf_op jit(solution)/shard_map/all_to_all | solution.py:343
  8.4 31.5 %all-gather = bf16[1088,256]{1,0:T(8,128)(2,1)S(1)} all-gather(bf16[272,256]{1,0:T(8,128)(2,1)S(1)} %get-tuple-element.9), channel_id=2, replica_groups=mesh['x'=4,'core'=2,'y'=4,'zh'=4,'zl'=4] {'zh'}, dimensions={0}, use_global_device_ids=true | all-gather | bytes 696320 | tf_op jit(solution)/shard_map/all_gather | solution.py:351
  40.0 1.6 %shard_map.78 = bf16[16,160,256]{2,1,0:T(8,128)(2,1)} custom-call(s32[1]{0:T(128)} %bitcast.1.base_ref, bf16[4,272,256]{2,1,0:T(8,128)(2,1)S(1)} %bitcast.19), custom_call_target="tpu_custom_call" | custom-call | tf_op jit(solution)/shard_map/pallas_call | solution.py:69
  41.6 0.0 all-to-all-done.1
  41.6 9.4 %all-to-all-start = ((bf16[16,160,256]{2,1,0:T(8,128)(2,1)}), bf16[16,160,256]{2,1,0:T(8,128)(2,1)}, u32[]{:S(2)}, u32[]{:S(2)}) async-start(bf16[16,160,256]{2,1,0:T(8,128)(2,1)} %shard_map.78), calls=%async_computation | async-start | bytes 2621440 | tf_op jit(solution)/shard_map/all_to_all | solution.py:355
  51.0 0.1 slice.4
  51.2 0.0 copy-start
  51.2 0.0 copy-start.3
  51.2 0.1 pad_maximum_fusion
  51.3 2.4 %collective-permute-start = (bf16[384,2816]{1,0:T(8,128)(2,1)S(1)}, bf16[384,2816]{1,0:T(8,128)(2,1)S(1)}, u32[]{:S(2)}, u32[]{:S(2)}) collective-permute-start(bf16[384,2816]{1,0:T(8,128)(2,1)S(1)} %pad_maximum_fusion), channel_id=1, source_target_pairs={{0,64},{64,0},{1,65},{65,1},{2,66},{66,2},{3,67},{67,3},{4,68},{68... | collective-permute-start | bytes 6488072 | tf_op jit(solution)/shard_map/ppermute | solution.py:346
  53.7 3.9 %collective-permute-done.theirs_ref = bf16[384,2816]{1,0:T(8,128)(2,1)S(1)} collective-permute-done((bf16[384,2816]{1,0:T(8,128)(2,1)S(1)}, bf16[384,2816]{1,0:T(8,128)(2,1)S(1)}, u32[]{:S(2)}, u32[]{:S(2)}) %collective-permute-start) | collective-permute-done | bytes 2162720 | tf_op jit(solution)/shard_map/ppermute | solution.py:346
  57.6 0.0 copy-done
  57.6 0.0 copy-done.3
  57.6 2.7 %shard_map.79 = (f32[2560,256]{1,0:T(8,128)}, f32[64,256]{1,0:T(8,128)S(1)}, f32[64,256]{1,0:T(8,128)S(1)}) custom-call(s32[1]{0:T(128)} %bitcast.core_ref, bf16[384,3072]{1,0:T(8,128)(2,1)S(1)} %bitcast.18, bf16[384,2816]{1,0:T(8,128)(2,1)S(1)} %collective-permute-done.theirs_ref, s32[8,256]{1,0:T(8,128)S(1)} %bitcast.21, f32[8,256]{1,0:T(8,128)S(1)} %bitcast.23), custom_call_target="tpu_custom_call" | custom-call | tf_op jit(solution)/shard_map/pallas_call | solution.py:211
  60.3 0.0 copy-start.1
  60.3 0.6 copy-done.1
  60.9 0.0 copy-start.2
  60.9 0.6 copy-done.2
  61.5 12.2 %all-to-all-done.rows_hbm = bf16[16,160,256]{2,1,0:T(8,128)(2,1)} async-done(((bf16[16,160,256]{2,1,0:T(8,128)(2,1)}), bf16[16,160,256]{2,1,0:T(8,128)(2,1)}, u32[]{:S(2)}, u32[]{:S(2)}) %all-to-all-start) | async-done | bytes 1310752 | tf_op jit(solution)/shard_map/all_to_all | solution.py:355
  73.7 2.4 %shard_map.80 = f32[64,1,128]{2,1,0:T(1,128)S(1)} custom-call(s32[1]{0:T(128)} %bitcast.core_ref, bf16[16,160,256]{2,1,0:T(8,128)(2,1)} %all-to-all-done.rows_hbm, f32[2560,256]{1,0:T(8,128)} %get-tuple-element.11.mixed_hbm), custom_call_target="tpu_custom_call" | custom-call | tf_op jit(solution)/shard_map/pallas_call | solution.py:253
  76.1 1.9 %all-gather.1 = f32[128,1,128]{2,1,0:T(1,128)S(1)} all-gather(f32[64,1,128]{2,1,0:T(1,128)S(1)} %shard_map.80), channel_id=3, replica_groups=mesh['x'=4,'core'=2,'y'=4,'zh'=4,'zl'=4] {'core'}, dimensions={0}, use_global_device_ids=true | all-gather | bytes 98304 | tf_op jit(solution)/shard_map/all_gather | solution.py:364
  77.9 33.8 %all_to_all.15 = f32[256,1,128]{2,1,0:T(1,128)} all-to-all(f32[256,1,128]{2,1,0:T(1,128)S(1)} %bitcast.26), channel_id=1, replica_groups=mesh['x'=4,'core'=2,'y'=4,'zh'=4,'zl'=4] {'x','y','zh','zl'}, dimensions={0} | all-to-all | bytes 262144 | tf_op jit(solution)/shard_map/all_to_all | solution.py:366
  111.8 2.6 %shard_map.81 = (bf16[256,256]{1,0:T(8,128)(2,1)}, f32[8,256]{1,0:T(8,128)}) custom-call(f32[4,64,1,128]{3,2,1,0:T(1,128)} %bitcast.25, f32[64,256]{1,0:T(8,128)} %copy-done.1, f32[64,256]{1,0:T(8,128)} %copy-done.2, s32[8,256]{1,0:T(8,128)S(1)} %bitcast.22, bf16[64,256]{1,0:T(8,128)(2,1)} %bitcast.29), custom_call_target="tpu_custom_call" | custom-call | tf_op jit(solution)/shard_map/pallas_call | solution.py:310
  (3 shorter events, 0.1 us)
Async XLA Ops:
  3.6 38.0 %all-to-all-start.1 = ((bf16[4,96,3072]{2,1,0:T(8,128)(2,1)}), bf16[4,96,3072]{2,1,0:T(8,128)(2,1)S(1)}, u32[]{:S(2)}, u32[]{:S(2)}) async-start(bf16[4,96,3072]{2,1,0:T(8,128)(2,1)} %get-tuple-element.10), calls=%async_computation.1 | async-start | bytes 4718592 | tf_op jit(solution)/shard_map/all_to_all | solution.py:343
  41.6 32.1 %all-to-all-start = ((bf16[16,160,256]{2,1,0:T(8,128)(2,1)}), bf16[16,160,256]{2,1,0:T(8,128)(2,1)}, u32[]{:S(2)}, u32[]{:S(2)}) async-start(bf16[16,160,256]{2,1,0:T(8,128)(2,1)} %shard_map.78), calls=%async_computation | async-start | bytes 2621440 | tf_op jit(solution)/shard_map/all_to_all | solution.py:355
  51.2 6.4 %copy-start = (s32[256,8]{0,1:T(8,128)S(1)}, s32[256,8]{0,1:T(8,128)}, u32[]{:S(2)}) copy-start(s32[256,8]{0,1:T(8,128)} %param.7) | copy-start | bytes 24580
  51.2 6.4 %copy-start.3 = (f32[256,8]{0,1:T(8,128)S(1)}, f32[256,8]{0,1:T(8,128)}, u32[]{:S(2)}) copy-start(f32[256,8]{0,1:T(8,128)} %param.8) | copy-start | bytes 24580
  51.3 6.2 %collective-permute-start = (bf16[384,2816]{1,0:T(8,128)(2,1)S(1)}, bf16[384,2816]{1,0:T(8,128)(2,1)S(1)}, u32[]{:S(2)}, u32[]{:S(2)}) collective-permute-start(bf16[384,2816]{1,0:T(8,128)(2,1)S(1)} %pad_maximum_fusion), channel_id=1, source_target_pairs={{0,64},{64,0},{1,65},{65,1},{2,66},{66,2},{3,67},{67,3},{4,68},{68... | collective-permute-start | bytes 6488072 | tf_op jit(solution)/shard_map/ppermute | solution.py:346
  60.3 0.6 copy-start.1
  60.9 0.6 copy-start.2

commit v6 on v5

--- a/solution.py
+++ b/solution.py
@@ -23,6 +23,10 @@
 BF16 = jnp.bfloat16
 
 
+def in_vmem(array):
+    return pltpu.with_memory_space_constraint(array, pltpu.VMEM)
+
+
 def in_hbm(array):
     return pltpu.with_memory_space_constraint(array, pltpu.HBM)
 
@@ -45,19 +49,19 @@
     before = jnp.dot(hits.astype(BF16), earlier.astype(BF16), preferred_element_type=F32)
     key = jnp.where(hits > 0, before, -1.0)
     slot = lax.broadcasted_iota(jnp.int32, (CAP, TOK), 0).astype(F32)
-    for b in range(ZH):
-        pick = jnp.concatenate(
-            [(key[b * NEAR + e : b * NEAR + e + 1, :] == slot).astype(F32) for e in range(NEAR)],
-            axis=0,
-        )
-        picked[b] = jnp.dot(
-            pick.astype(BF16), blocks_ref[b, 0:TOK, :], preferred_element_type=F32
-        )
     copies = []
     for y in range(Y):
-        for e in range(y * ZL, (y + 1) * ZL):
+        for b in range(ZH):
+            first = b * NEAR + y * ZL
+            pick = jnp.concatenate(
+                [(key[e : e + 1, :] == slot).astype(F32) for e in range(first, first + ZL)], axis=0
+            )
+            picked[b] = jnp.dot(
+                pick.astype(BF16), blocks_ref[b, 0:TOK, :], preferred_element_type=F32
+            )
+        for e in range(ZL):
             rows = [picked[b, e * CAP : (e + 1) * CAP, :] for b in range(ZH)]
-            rows_out[e] = jnp.concatenate(rows, axis=0).astype(BF16)
+            rows_out[y * ZL + e] = jnp.concatenate(rows, axis=0).astype(BF16)
         near = pl.ds(y * ZL, ZL)
         copies.append(pltpu.make_async_copy(rows_out.at[near], out_hbm.at[near], sems.at[y]))
         copies[-1].start()
@@ -75,7 +79,7 @@
         ],
         out_specs=pl.BlockSpec(memory_space=pltpu.HBM),
         scratch_shapes=[
-            pltpu.VMEM((ZH, NEAR * CAP, DS), F32),
+            pltpu.VMEM((ZH, ZL * CAP, DS), F32),
             pltpu.VMEM((NEAR, ZH * CAP, DS), BF16),
             pltpu.SemaphoreType.DMA((Y,)),
         ],
@@ -99,12 +103,21 @@
     load_grad = pltpu.make_async_copy(
         grad_hbm.at[:, columns], block_ref.at[pl.ds(0, TOK)], sems.at[8]
     )
-    for copy in loads + [load_weight, load_ids, load_grad]:
+    for copy in [load_weight] + loads + [load_ids, load_grad]:
         copy.start()
     others = [load_grad]
     load_ids.wait()
     ids = ids_ref[...].astype(F32)
     block_ref[TOK : TOK + 16, :] = jnp.concatenate([ids, jnp.zeros_like(ids)], axis=0).astype(BF16)
+    load_weight.wait()
+    for j in range(X):
+        copy = pltpu.make_async_copy(
+            weight.at[:, pl.ds(j * CORES * DS, CORES * DS)],
+            out_hbm.at[j, :, pl.ds(slots, CORES * DS)],
+            sems.at[4 + j],
+        )
+        copy.start()
+        others.append(copy)
     for i in range(4):
         loads[i].wait()
         rows = slice(i * piece, (i + 1) * piece)
@@ -115,15 +128,6 @@
             )
             copy.start()
             others.append(copy)
-    load_weight.wait()
-    for j in range(X):
-        copy = pltpu.make_async_copy(
-            weight.at[:, pl.ds(j * CORES * DS, CORES * DS)],
-            out_hbm.at[j, :, pl.ds(slots, CORES * DS)],
-            sems.at[4 + j],
-        )
-        copy.start()
-        others.append(copy)
     for copy in others:
         copy.wait()
 
@@ -157,7 +161,7 @@
 
 
 def mix_kernel(
-    core_ref, mine_ref, theirs_ref, ids_ref, logits_ref, out_hbm, key_ref, probs_ref, out_ref, sems
+    core_ref, mine_ref, theirs_ref, ids_ref, logits_ref, out_hbm, key_ref, probs_ref, out_ref, rounded, sems
 ):
     plan(ids_ref[...], logits_ref[...], key_ref, probs_ref)
     slots = EXPERTS * CAP
@@ -182,7 +186,8 @@
                 dst = pl.multiple_of(y * group + (place * ZH + zh) * CAP, 8)
                 out_ref[pl.ds(dst, CAP), :] = mixed[src : src + CAP, :]
         rows = pl.ds(y * group, group)
-        copies.append(pltpu.make_async_copy(out_ref.at[rows], out_hbm.at[rows], sems.at[y]))
+        rounded[rows, :] = out_ref[rows, :].astype(BF16)
+        copies.append(pltpu.make_async_copy(rounded.at[rows], out_hbm.at[rows], sems.at[y]))
         copies[-1].start()
     for copy in copies:
         copy.wait()
@@ -207,20 +212,24 @@
 
 
 def mix(core, mine, theirs, ids, logits):
-    table = jax.ShapeDtypeStruct((EXPERTS, TOK), F32)
+    table = pltpu.VMEM((EXPERTS, TOK), F32)
     return pl.pallas_call(
         mix_kernel,
-        out_shape=(pltpu.HBM((EXPERTS * CAP, DS), F32), table, table),
+        out_shape=(pltpu.HBM((EXPERTS * CAP, DS), BF16), table, table),
         in_specs=[pl.BlockSpec(memory_space=pltpu.SMEM)]
         + [pl.BlockSpec(memory_space=pltpu.VMEM)] * 4,
         out_specs=(pl.BlockSpec(memory_space=pltpu.HBM),) + (pl.BlockSpec(memory_space=pltpu.VMEM),) * 2,
-        scratch_shapes=[pltpu.VMEM((EXPERTS * CAP, DS), F32), pltpu.SemaphoreType.DMA((Y,))],
+        scratch_shapes=[
+            pltpu.VMEM((EXPERTS * CAP, DS), F32),
+            pltpu.VMEM((EXPERTS * CAP, DS), BF16),
+            pltpu.SemaphoreType.DMA((Y,)),
+        ],
         compiler_params=pltpu.CompilerParams(vmem_limit_bytes=16 << 20),
     )(core, mine, theirs, ids, logits)
 
 
 def value_kernel(core_ref, rows_hbm, mixed_hbm, out_ref, rows_ref, mixed_ref, sems):
-    steps = 8
+    steps = 4
     per = NEAR // steps
     copies = []
     for i in range(steps):
@@ -241,7 +250,9 @@
         for copy in copies[i]:
             copy.wait()
         for e in range(i * per, (i + 1) * per):
-            rows = rows_ref[e].astype(F32) * mixed_ref[e * ZH * CAP : (e + 1) * ZH * CAP, :]
+            rows = rows_ref[e].astype(F32) * mixed_ref[
+                e * ZH * CAP : (e + 1) * ZH * CAP, :
+            ].astype(F32)
             sums = jnp.sum(rows[:, 0:128] + rows[:, 128:256], axis=1, keepdims=True)
             for b in range(ZH):
                 lanes = jnp.where(own_lane, sums[b * CAP : (b + 1) * CAP, :], 0.0)
@@ -261,21 +272,21 @@
         out_specs=pl.BlockSpec(memory_space=pltpu.VMEM),
         scratch_shapes=[
             pltpu.VMEM(rows.shape, BF16),
-            pltpu.VMEM(mixed.shape, F32),
-            pltpu.SemaphoreType.DMA((2, 8)),
+            pltpu.VMEM(mixed.shape, BF16),
+            pltpu.SemaphoreType.DMA((2, 4)),
         ],
         compiler_params=pltpu.CompilerParams(vmem_limit_bytes=16 << 20),
     )(core, in_hbm(rows), in_hbm(mixed))
 
 
 def final_kernel(
-    parts_hbm, key_hbm, probs_hbm, ids_ref, router_hbm, grad_ref, weight_ref,
-    parts_ref, key_ref, probs_ref, router_ref, total, sems,
+    parts_hbm, key_ref, probs_ref, ids_ref, router_hbm, grad_ref, weight_ref,
+    parts_ref, router_ref, total, sems,
 ):
     copies = [
         pltpu.make_async_copy(far, near, sems.at[i])
         for i, (far, near) in enumerate(
-            [(parts_hbm, parts_ref), (key_hbm, key_ref), (probs_hbm, probs_ref), (router_hbm, router_ref)]
+            [(parts_hbm, parts_ref), (router_hbm, router_ref)]
         )
     ]
     for copy in copies:
@@ -313,18 +324,16 @@
             jax.ShapeDtypeStruct((TOK, DS), BF16),
             jax.ShapeDtypeStruct((TOPK, TOK), F32),
         ),
-        in_specs=[far, far, far, near, far],
+        in_specs=[far, near, near, near, far],
         out_specs=(near, near),
         scratch_shapes=[
             pltpu.VMEM(parts.shape, F32),
-            pltpu.VMEM(key.shape, F32),
-            pltpu.VMEM(probs.shape, F32),
             pltpu.VMEM(router.shape, BF16),
             pltpu.VMEM((EXPERTS, 128), F32),
-            pltpu.SemaphoreType.DMA((4,)),
-        ],
-        compiler_params=pltpu.CompilerParams(vmem_limit_bytes=16 << 20),
-    )(in_hbm(parts), in_hbm(key), in_hbm(probs), ids, in_hbm(router))
+            pltpu.SemaphoreType.DMA((2,)),
+        ],
+        compiler_params=pltpu.CompilerParams(vmem_limit_bytes=16 << 20),
+    )(in_hbm(parts), in_vmem(key), in_vmem(probs), ids, in_hbm(router))
 
 
 def body(out_grad, expert_ids, chosen_logits, down_weight, saved_hidden, router_weight):

time: 115 us -> 114 us (level)
  waiting for transfers between devices: 16 us -> 17.4 us
  local copies, waits for them, and re-layouts: 1.42 us -> 0.19 us
    all_to_all x1, waiting for transfers between devices: 12.2 us -> 13.6 us  [body(): lax.all_to_all(outgoing, ('core', 'y', 'zh', 'zl'), split_axis=0, concat_...]
    unnamed x8 -> x4, local copies, waits for them, and re-layouts: 1.24 us -> 0.01 us
where the time goes in v6:
time: 114 us
  blocking collectives  67.4 us (59%)
  waiting for transfers between devices  17.4 us (15%)
  starting transfers between devices  16.6 us (15%)
  Pallas kernels  11.1 us (10%)
    all_to_all x1, blocking collectives, body(): lax.all_to_all(part, ('x',) + EXPERT, split_axis=0, concat_axis=0, tiled=...  34 us
    all_gather x1, blocking collectives, body(): blocks = lax.all_gather(block, 'zh', axis=0, tiled=False)  31.5 us
    all_to_all x1, waiting for transfers between devices, body(): lax.all_to_all(outgoing, ('core', 'y', 'zh', 'zl'), split_axis=0, concat_...  13.6 us
    all_to_all x1, starting transfers between devices, body(): lax.all_to_all(outgoing, ('core', 'y', 'zh', 'zl'), split_axis=0, concat_...  9.51 us
    all_to_all x1, starting transfers between devices, body(): along = lax.all_to_all(along, 'x', split_axis=0, concat_axis=0, tiled=True)  4.85 us
    ppermute x1, waiting for transfers between devices, body(): lax.ppermute(jnp.concatenate([mine[:, :slots], weight_other], axis=1), 'c...  3.86 us
    pallas_call x1, Pallas kernels, exchange_blocks(): pl.pallas_call(exchange_kernel, out_shape=(pltpu.HBM((X, width, EXPERTS *...  2.73 us
    pallas_call x1, Pallas kernels, mix(): pl.pallas_call(mix_kernel, out_shape=(pltpu.HBM((EXPERTS * CAP, DS), BF16...  2.56 us
  transfers between devices with their start and end apart: 3, of which 2 were waited for; matrix products, arithmetic and copies ran while one was open for 0% of the time, Pallas kernels for 4%

profile of v6, /device:TPU:1, one launch (start us, length us, event | category | flops | bytes accessed | tf_op | source)
XLA Modules:
  0.0 113.6 jit_solution(6888446565360863810)
XLA Ops:
  0.6 2.7 %shard_map.77 = (bf16[4,96,3072]{2,1,0:T(8,128)(2,1)}, bf16[272,256]{1,0:T(8,128)(2,1)S(1)}) custom-call(s32[1]{0:T(128)} %bitcast.2.head_ref, s32[8,256]{1,0:T(8,128)} %bitcast.20, bf16[256,2048]{1,0:T(8,128)(2,1)} %grad_hbm.1, bf16[2560,96]{1,0:T(8,128)(2,1)} %bitcast.24, bf16[96,2048]{1,0:T(8,128)(2,1)} %bitcast.27), custom_call_target="tpu_custom_call" | custom-call | tf_op jit(solution)/shard_map/pallas_call | solution.py:138
  3.4 4.9 %all-to-all-start.1 = ((bf16[4,96,3072]{2,1,0:T(8,128)(2,1)}), bf16[4,96,3072]{2,1,0:T(8,128)(2,1)S(1)}, u32[]{:S(2)}, u32[]{:S(2)}) async-start(bf16[4,96,3072]{2,1,0:T(8,128)(2,1)} %get-tuple-element.10), calls=%async_computation.1 | async-start | bytes 4718592 | tf_op jit(solution)/shard_map/all_to_all | solution.py:352
  8.2 31.5 %all-gather = bf16[1088,256]{1,0:T(8,128)(2,1)S(1)} all-gather(bf16[272,256]{1,0:T(8,128)(2,1)S(1)} %get-tuple-element.9), channel_id=2, replica_groups=mesh['x'=4,'core'=2,'y'=4,'zh'=4,'zl'=4] {'zh'}, dimensions={0}, use_global_device_ids=true | all-gather | bytes 696320 | tf_op jit(solution)/shard_map/all_gather | solution.py:360
  39.8 1.5 %shard_map.78 = bf16[16,160,256]{2,1,0:T(8,128)(2,1)} custom-call(s32[1]{0:T(128)} %bitcast.1.base_ref, bf16[4,272,256]{2,1,0:T(8,128)(2,1)S(1)} %bitcast.19), custom_call_target="tpu_custom_call" | custom-call | tf_op jit(solution)/shard_map/pallas_call | solution.py:73
  41.3 0.0 all-to-all-done.1
  41.3 9.5 %all-to-all-start = ((bf16[16,160,256]{2,1,0:T(8,128)(2,1)}), bf16[16,160,256]{2,1,0:T(8,128)(2,1)}, u32[]{:S(2)}, u32[]{:S(2)}) async-start(bf16[16,160,256]{2,1,0:T(8,128)(2,1)} %shard_map.78), calls=%async_computation | async-start | bytes 2621440 | tf_op jit(solution)/shard_map/all_to_all | solution.py:364
  50.8 0.1 slice.4
  51.0 0.0 copy-start
  51.0 0.0 copy-start.1
  51.0 0.1 pad_maximum_fusion
  51.1 2.3 %collective-permute-start = (bf16[384,2816]{1,0:T(8,128)(2,1)S(1)}, bf16[384,2816]{1,0:T(8,128)(2,1)S(1)}, u32[]{:S(2)}, u32[]{:S(2)}) collective-permute-start(bf16[384,2816]{1,0:T(8,128)(2,1)S(1)} %pad_maximum_fusion), channel_id=1, source_target_pairs={{0,64},{64,0},{1,65},{65,1},{2,66},{66,2},{3,67},{67,3},{4,68},{68... | collective-permute-start | bytes 6488072 | tf_op jit(solution)/shard_map/ppermute | solution.py:355
  53.4 3.9 %collective-permute-done.theirs_ref = bf16[384,2816]{1,0:T(8,128)(2,1)S(1)} collective-permute-done((bf16[384,2816]{1,0:T(8,128)(2,1)S(1)}, bf16[384,2816]{1,0:T(8,128)(2,1)S(1)}, u32[]{:S(2)}, u32[]{:S(2)}) %collective-permute-start) | collective-permute-done | bytes 2162720 | tf_op jit(solution)/shard_map/ppermute | solution.py:355
  57.3 0.0 copy-done
  57.3 0.0 copy-done.1
  57.3 2.6 %shard_map.79 = (bf16[2560,256]{1,0:T(8,128)(2,1)}, f32[64,256]{1,0:T(8,128)S(1)}, f32[64,256]{1,0:T(8,128)S(1)}) custom-call(s32[1]{0:T(128)} %bitcast.core_ref, bf16[384,3072]{1,0:T(8,128)(2,1)S(1)} %bitcast.18, bf16[384,2816]{1,0:T(8,128)(2,1)S(1)} %collective-permute-done.theirs_ref, s32[8,256]{1,0:T(8,128)S(1)} %bitcast.21, f32[8,256]{1,0:T(8,128)S(1)} %bitcast.23), custom_call_target="tpu_custom_call" | custom-call | tf_op jit(solution)/shard_map/pallas_call | solution.py:216
  59.8 13.6 %all-to-all-done.rows_hbm = bf16[16,160,256]{2,1,0:T(8,128)(2,1)} async-done(((bf16[16,160,256]{2,1,0:T(8,128)(2,1)}), bf16[16,160,256]{2,1,0:T(8,128)(2,1)}, u32[]{:S(2)}, u32[]{:S(2)}) %all-to-all-start) | async-done | bytes 1310752 | tf_op jit(solution)/shard_map/all_to_all | solution.py:364
  73.4 1.9 %shard_map.80 = f32[64,1,128]{2,1,0:T(1,128)S(1)} custom-call(s32[1]{0:T(128)} %bitcast.core_ref, bf16[16,160,256]{2,1,0:T(8,128)(2,1)} %all-to-all-done.rows_hbm, bf16[2560,256]{1,0:T(8,128)(2,1)} %get-tuple-element.11.mixed_hbm), custom_call_target="tpu_custom_call" | custom-call | tf_op jit(solution)/shard_map/pallas_call | solution.py:264
  75.3 1.9 %all-gather.1 = f32[128,1,128]{2,1,0:T(1,128)S(1)} all-gather(f32[64,1,128]{2,1,0:T(1,128)S(1)} %shard_map.80), channel_id=3, replica_groups=mesh['x'=4,'core'=2,'y'=4,'zh'=4,'zl'=4] {'core'}, dimensions={0}, use_global_device_ids=true | all-gather | bytes 98304 | tf_op jit(solution)/shard_map/all_gather | solution.py:373
  77.2 34.0 %all_to_all.15 = f32[256,1,128]{2,1,0:T(1,128)} all-to-all(f32[256,1,128]{2,1,0:T(1,128)S(1)} %bitcast.26), channel_id=1, replica_groups=mesh['x'=4,'core'=2,'y'=4,'zh'=4,'zl'=4] {'x','y','zh','zl'}, dimensions={0} | all-to-all | bytes 262144 | tf_op jit(solution)/shard_map/all_to_all | solution.py:375
  111.2 2.4 %shard_map.81 = (bf16[256,256]{1,0:T(8,128)(2,1)}, f32[8,256]{1,0:T(8,128)}) custom-call(f32[4,64,1,128]{3,2,1,0:T(1,128)} %bitcast.25, f32[64,256]{1,0:T(8,128)S(1)} %get-tuple-element.12.key_ref, f32[64,256]{1,0:T(8,128)S(1)} %get-tuple-element.13.probs_ref, s32[8,256]{1,0:T(8,128)S(1)} %bitcast.22, bf16[64,256]{1,0:T(8,128)(2,1)} %bitcast.29), custom_call_target="tpu_custom_call" | custom-call | tf_op jit(solution)/shard_map/pallas_call | solution.py:321
  (3 shorter events, 0.1 us)
Async XLA Ops:
  3.4 37.9 %all-to-all-start.1 = ((bf16[4,96,3072]{2,1,0:T(8,128)(2,1)}), bf16[4,96,3072]{2,1,0:T(8,128)(2,1)S(1)}, u32[]{:S(2)}, u32[]{:S(2)}) async-start(bf16[4,96,3072]{2,1,0:T(8,128)(2,1)} %get-tuple-element.10), calls=%async_computation.1 | async-start | bytes 4718592 | tf_op jit(solution)/shard_map/all_to_all | solution.py:352
  41.3 32.2 %all-to-all-start = ((bf16[16,160,256]{2,1,0:T(8,128)(2,1)}), bf16[16,160,256]{2,1,0:T(8,128)(2,1)}, u32[]{:S(2)}, u32[]{:S(2)}) async-start(bf16[16,160,256]{2,1,0:T(8,128)(2,1)} %shard_map.78), calls=%async_computation | async-start | bytes 2621440 | tf_op jit(solution)/shard_map/all_to_all | solution.py:364
  51.0 6.3 %copy-start = (s32[256,8]{0,1:T(8,128)S(1)}, s32[256,8]{0,1:T(8,128)}, u32[]{:S(2)}) copy-start(s32[256,8]{0,1:T(8,128)} %param.7) | copy-start | bytes 24580
  51.0 6.3 %copy-start.1 = (f32[256,8]{0,1:T(8,128)S(1)}, f32[256,8]{0,1:T(8,128)}, u32[]{:S(2)}) copy-start(f32[256,8]{0,1:T(8,128)} %param.8) | copy-start | bytes 24580
  51.1 6.1 %collective-permute-start = (bf16[384,2816]{1,0:T(8,128)(2,1)S(1)}, bf16[384,2816]{1,0:T(8,128)(2,1)S(1)}, u32[]{:S(2)}, u32[]{:S(2)}) collective-permute-start(bf16[384,2816]{1,0:T(8,128)(2,1)S(1)} %pad_maximum_fusion), channel_id=1, source_target_pairs={{0,64},{64,0},{1,65},{65,1},{2,66},{66,2},{3,67},{67,3},{4,68},{68... | collective-permute-start | bytes 6488072 | tf_op jit(solution)/shard_map/ppermute | solution.py:355

commit v7 on v6

--- a/solution.py
+++ b/solution.py
@@ -15,6 +15,7 @@
 DS = 256
 NEAR = Y * ZL
 F32 = jnp.float32
+FAR_GROUPS = [[c * ZH + (b + c) % ZH for b in range(ZH)] for c in range(CORES)]
 NEAR_GROUPS = [
     [c * Y * ZH * ZL + y * ZH * ZL + (q * ZL + r + 2 * c) % (ZH * ZL) for y in range(Y) for r in range(ZL)]
     for c in range(CORES)
@@ -32,7 +33,7 @@
 
 
 def select_kernel(base_ref, blocks_ref, out_hbm, picked, rows_out, sems):
-    base = base_ref[0]
+    base, core = base_ref[0], base_ref[1]
     j = lax.broadcasted_iota(jnp.int32, (NEAR, TOK), 0)
     expert = ((j // ZL) * (ZH * ZL) + ((base + j % ZL) & (ZH * ZL - 1))).astype(F32)
     hits = []
@@ -56,7 +57,7 @@
             pick = jnp.concatenate(
                 [(key[e : e + 1, :] == slot).astype(F32) for e in range(first, first + ZL)], axis=0
             )
-            picked[b] = jnp.dot(
+            picked[(b + core) & (ZH - 1)] = jnp.dot(
                 pick.astype(BF16), blocks_ref[b, 0:TOK, :], preferred_element_type=F32
             )
         for e in range(ZL):
@@ -280,19 +281,11 @@
 
 
 def final_kernel(
-    parts_hbm, key_ref, probs_ref, ids_ref, router_hbm, grad_ref, weight_ref,
-    parts_ref, router_ref, total, sems,
+    parts_ref, key_ref, probs_ref, ids_ref, router_hbm, grad_ref, weight_ref,
+    router_ref, total, sem,
 ):
-    copies = [
-        pltpu.make_async_copy(far, near, sems.at[i])
-        for i, (far, near) in enumerate(
-            [(parts_hbm, parts_ref), (router_hbm, router_ref)]
-        )
-    ]
-    for copy in copies:
-        copy.start()
-    for copy in copies:
-        copy.wait()
+    load_router = pltpu.make_async_copy(router_hbm, router_ref, sem)
+    load_router.start()
     parts = parts_ref[0]
     for i in range(1, X):
         parts = parts + parts_ref[i]
@@ -305,6 +298,7 @@
         dense = jnp.where(key == float(c), back[:, c : c + 1], dense)
     mean = jnp.sum(probs * dense, axis=0, keepdims=True)
     logit = (probs * (dense - mean)).astype(BF16)
+    load_router.wait()
     grad_ref[...] = lax.dot_general(
         logit, router_ref[...], (((0,), (0,)), ((), ())), preferred_element_type=F32
     ).astype(BF16)
@@ -324,16 +318,15 @@
             jax.ShapeDtypeStruct((TOK, DS), BF16),
             jax.ShapeDtypeStruct((TOPK, TOK), F32),
         ),
-        in_specs=[far, near, near, near, far],
+        in_specs=[near, near, near, near, far],
         out_specs=(near, near),
         scratch_shapes=[
-            pltpu.VMEM(parts.shape, F32),
             pltpu.VMEM(router.shape, BF16),
             pltpu.VMEM((EXPERTS, 128), F32),
-            pltpu.SemaphoreType.DMA((2,)),
-        ],
-        compiler_params=pltpu.CompilerParams(vmem_limit_bytes=16 << 20),
-    )(in_hbm(parts), in_vmem(key), in_vmem(probs), ids, in_hbm(router))
+            pltpu.SemaphoreType.DMA(()),
+        ],
+        compiler_params=pltpu.CompilerParams(vmem_limit_bytes=16 << 20),
+    )(in_vmem(parts), in_vmem(key), in_vmem(probs), ids, in_hbm(router))
 
 
 def body(out_grad, expert_ids, chosen_logits, down_weight, saved_hidden, router_weight):
@@ -357,10 +350,12 @@
     )
     core_scalar = core.reshape(1).astype(jnp.int32)
     mixed, key, probs = mix(core_scalar, mine, theirs, ids, logits)
-    blocks = lax.all_gather(block, "zh", axis=0, tiled=False)
+    blocks = lax.all_gather(
+        block, ("core", "zh"), axis=0, tiled=False, axis_index_groups=FAR_GROUPS
+    )
     z = lax.axis_index("zh") * ZL + lax.axis_index("zl")
     base = ((z - 2 * core) & (ZH * ZL - ZL)) + 2 * core
-    outgoing = select_rows(base.reshape(1).astype(jnp.int32), blocks)
+    outgoing = select_rows(jnp.stack([base, core]).astype(jnp.int32), blocks)
     received = lax.all_to_all(
         outgoing,
         ("core", "y", "zh", "zl"),

time: 114 us -> 114 us (level)
  no operation moved by 1% of the time
where the time goes in v7:
time: 114 us
  blocking collectives  67.3 us (59%)
  waiting for transfers between devices  16.9 us (15%)
  starting transfers between devices  16.6 us (15%)
  Pallas kernels  11.7 us (10%)
    all_to_all x1, blocking collectives, body(): lax.all_to_all(part, ('x',) + EXPERT, split_axis=0, concat_axis=0, tiled=...  33.9 us
    all_gather x1, blocking collectives, body(): lax.all_gather(block, ('core', 'zh'), axis=0, tiled=False, axis_index_gro...  31.5 us
    all_to_all x1, waiting for transfers between devices, body(): lax.all_to_all(outgoing, ('core', 'y', 'zh', 'zl'), split_axis=0, concat_...  13 us
    all_to_all x1, starting transfers between devices, body(): lax.all_to_all(outgoing, ('core', 'y', 'zh', 'zl'), split_axis=0, concat_...  8.54 us
    all_to_all x1, starting transfers between devices, body(): along = lax.all_to_all(along, 'x', split_axis=0, concat_axis=0, tiled=True)  4.85 us
    ppermute x1, waiting for transfers between devices, body(): lax.ppermute(jnp.concatenate([mine[:, :slots], weight_other], axis=1), 'c...  3.86 us
    ppermute x1, starting transfers between devices, body(): lax.ppermute(jnp.concatenate([mine[:, :slots], weight_other], axis=1), 'c...  3.24 us
    pallas_call x1, Pallas kernels, exchange_blocks(): pl.pallas_call(exchange_kernel, out_shape=(pltpu.HBM((X, width, EXPERTS *...  2.73 us
  transfers between devices with their start and end apart: 3, of which 2 were waited for; matrix products, arithmetic and copies ran while one was open for 0% of the time, Pallas kernels for 4%

profile of v7, /device:TPU:1, one launch (start us, length us, event | category | flops | bytes accessed | tf_op | source)
XLA Modules:
  0.0 113.6 jit_solution(2617256015974161845)
XLA Ops:
  0.6 2.7 %shard_map.77 = (bf16[4,96,3072]{2,1,0:T(8,128)(2,1)}, bf16[272,256]{1,0:T(8,128)(2,1)S(1)}) custom-call(s32[1]{0:T(128)} %bitcast.2.head_ref, s32[8,256]{1,0:T(8,128)} %bitcast.21, bf16[256,2048]{1,0:T(8,128)(2,1)} %grad_hbm.1, bf16[2560,96]{1,0:T(8,128)(2,1)} %bitcast.25, bf16[96,2048]{1,0:T(8,128)(2,1)} %bitcast.27), custom_call_target="tpu_custom_call" | custom-call | tf_op jit(solution)/shard_map/pallas_call | solution.py:139
  3.4 4.9 %all-to-all-start.1 = ((bf16[4,96,3072]{2,1,0:T(8,128)(2,1)}), bf16[4,96,3072]{2,1,0:T(8,128)(2,1)S(1)}, u32[]{:S(2)}, u32[]{:S(2)}) async-start(bf16[4,96,3072]{2,1,0:T(8,128)(2,1)} %get-tuple-element.10), calls=%async_computation.1 | async-start | bytes 4718592 | tf_op jit(solution)/shard_map/all_to_all | solution.py:345
  8.2 0.1 pad_add_fusion.base_ref
  8.3 31.5 %all-gather = bf16[1088,256]{1,0:T(8,128)(2,1)S(1)} all-gather(bf16[272,256]{1,0:T(8,128)(2,1)S(1)} %get-tuple-element.9), channel_id=2, replica_groups={{0,4,8,12},{68,72,76,64},{1,5,9,13},{69,73,77,65},{2,6,10,14},{70,74,78..., dimensions={0}, use_global_device_ids=true | all-gather | bytes 696320 | tf_op jit(solution)/shard_map/all_gather | solution.py:353
  39.8 2.4 %shard_map.78 = bf16[16,160,256]{2,1,0:T(8,128)(2,1)} custom-call(s32[2]{0:T(128)S(1)} %pad_add_fusion.base_ref, bf16[4,272,256]{2,1,0:T(8,128)(2,1)S(1)} %bitcast.19), custom_call_target="tpu_custom_call" | custom-call | tf_op jit(solution)/shard_map/pallas_call | solution.py:74
  42.2 0.0 all-to-all-done.1
  42.2 8.5 %all-to-all-start = ((bf16[16,160,256]{2,1,0:T(8,128)(2,1)}), bf16[16,160,256]{2,1,0:T(8,128)(2,1)}, u32[]{:S(2)}, u32[]{:S(2)}) async-start(bf16[16,160,256]{2,1,0:T(8,128)(2,1)} %shard_map.78), calls=%async_computation | async-start | bytes 2621440 | tf_op jit(solution)/shard_map/all_to_all | solution.py:359
  50.8 0.1 slice.4
  51.0 0.0 copy-start
  51.0 0.0 copy-start.1
  51.0 0.1 pad_maximum_fusion
  51.1 3.2 %collective-permute-start = (bf16[384,2816]{1,0:T(8,128)(2,1)S(1)}, bf16[384,2816]{1,0:T(8,128)(2,1)S(1)}, u32[]{:S(2)}, u32[]{:S(2)}) collective-permute-start(bf16[384,2816]{1,0:T(8,128)(2,1)S(1)} %pad_maximum_fusion), channel_id=1, source_target_pairs={{0,64},{64,0},{1,65},{65,1},{2,66},{66,2},{3,67},{67,3},{4,68},{68... | collective-permute-start | bytes 6488072 | tf_op jit(solution)/shard_map/ppermute | solution.py:348
  54.4 3.9 %collective-permute-done.theirs_ref = bf16[384,2816]{1,0:T(8,128)(2,1)S(1)} collective-permute-done((bf16[384,2816]{1,0:T(8,128)(2,1)S(1)}, bf16[384,2816]{1,0:T(8,128)(2,1)S(1)}, u32[]{:S(2)}, u32[]{:S(2)}) %collective-permute-start) | collective-permute-done | bytes 2162720 | tf_op jit(solution)/shard_map/ppermute | solution.py:348
  58.2 0.0 copy-done
  58.2 0.0 copy-done.1
  58.2 2.6 %shard_map.79 = (bf16[2560,256]{1,0:T(8,128)(2,1)}, f32[64,256]{1,0:T(8,128)S(1)}, f32[64,256]{1,0:T(8,128)S(1)}) custom-call(s32[1]{0:T(128)} %bitcast.core_ref, bf16[384,3072]{1,0:T(8,128)(2,1)S(1)} %bitcast.18, bf16[384,2816]{1,0:T(8,128)(2,1)S(1)} %collective-permute-done.theirs_ref, s32[8,256]{1,0:T(8,128)S(1)} %bitcast.22, f32[8,256]{1,0:T(8,128)S(1)} %bitcast.24), custom_call_target="tpu_custom_call" | custom-call | tf_op jit(solution)/shard_map/pallas_call | solution.py:217
  60.8 13.0 %all-to-all-done.rows_hbm = bf16[16,160,256]{2,1,0:T(8,128)(2,1)} async-done(((bf16[16,160,256]{2,1,0:T(8,128)(2,1)}), bf16[16,160,256]{2,1,0:T(8,128)(2,1)}, u32[]{:S(2)}, u32[]{:S(2)}) %all-to-all-start) | async-done | bytes 1310752 | tf_op jit(solution)/shard_map/all_to_all | solution.py:359
  73.8 1.9 %shard_map.80 = f32[64,1,128]{2,1,0:T(1,128)S(1)} custom-call(s32[1]{0:T(128)} %bitcast.core_ref, bf16[16,160,256]{2,1,0:T(8,128)(2,1)} %all-to-all-done.rows_hbm, bf16[2560,256]{1,0:T(8,128)(2,1)} %get-tuple-element.11.mixed_hbm), custom_call_target="tpu_custom_call" | custom-call | tf_op jit(solution)/shard_map/pallas_call | solution.py:265
  75.7 1.9 %all-gather.1 = f32[128,1,128]{2,1,0:T(1,128)S(1)} all-gather(f32[64,1,128]{2,1,0:T(1,128)S(1)} %shard_map.80), channel_id=3, replica_groups=mesh['x'=4,'core'=2,'y'=4,'zh'=4,'zl'=4] {'core'}, dimensions={0}, use_global_device_ids=true | all-gather | bytes 98304 | tf_op jit(solution)/shard_map/all_gather | solution.py:368
  77.6 33.9 %all_to_all.15 = f32[256,1,128]{2,1,0:T(1,128)S(1)} all-to-all(f32[256,1,128]{2,1,0:T(1,128)S(1)} %bitcast.26), channel_id=1, replica_groups=mesh['x'=4,'core'=2,'y'=4,'zh'=4,'zl'=4] {'x','y','zh','zl'}, dimensions={0} | all-to-all | bytes 262144 | tf_op jit(solution)/shard_map/all_to_all | solution.py:370
  111.5 2.1 %shard_map.81 = (bf16[256,256]{1,0:T(8,128)(2,1)}, f32[8,256]{1,0:T(8,128)}) custom-call(f32[4,64,1,128]{3,2,1,0:T(1,128)S(1)} %bitcast.20, f32[64,256]{1,0:T(8,128)S(1)} %get-tuple-element.12.key_ref, f32[64,256]{1,0:T(8,128)S(1)} %get-tuple-element.13.probs_ref, s32[8,256]{1,0:T(8,128)S(1)} %bitcast.23, bf16[64,256]{1,0:T(8,128)(2,1)} %bitcast.29), custom_call_target="tpu_custom_call" | custom-call | tf_op jit(solution)/shard_map/pallas_call | solution.py:315
  (3 shorter events, 0.1 us)
Async XLA Ops:
  3.4 38.9 %all-to-all-start.1 = ((bf16[4,96,3072]{2,1,0:T(8,128)(2,1)}), bf16[4,96,3072]{2,1,0:T(8,128)(2,1)S(1)}, u32[]{:S(2)}, u32[]{:S(2)}) async-start(bf16[4,96,3072]{2,1,0:T(8,128)(2,1)} %get-tuple-element.10), calls=%async_computation.1 | async-start | bytes 4718592 | tf_op jit(solution)/shard_map/all_to_all | solution.py:345
  42.2 31.6 %all-to-all-start = ((bf16[16,160,256]{2,1,0:T(8,128)(2,1)}), bf16[16,160,256]{2,1,0:T(8,128)(2,1)}, u32[]{:S(2)}, u32[]{:S(2)}) async-start(bf16[16,160,256]{2,1,0:T(8,128)(2,1)} %shard_map.78), calls=%async_computation | async-start | bytes 2621440 | tf_op jit(solution)/shard_map/all_to_all | solution.py:359
  51.0 7.3 %copy-start = (s32[256,8]{0,1:T(8,128)S(1)}, s32[256,8]{0,1:T(8,128)}, u32[]{:S(2)}) copy-start(s32[256,8]{0,1:T(8,128)} %param.7) | copy-start | bytes 24580
  51.0 7.3 %copy-start.1 = (f32[256,8]{0,1:T(8,128)S(1)}, f32[256,8]{0,1:T(8,128)}, u32[]{:S(2)}) copy-start(f32[256,8]{0,1:T(8,128)} %param.8) | copy-start | bytes 24580
  51.1 7.1 %collective-permute-start = (bf16[384,2816]{1,0:T(8,128)(2,1)S(1)}, bf16[384,2816]{1,0:T(8,128)(2,1)S(1)}, u32[]{:S(2)}, u32[]{:S(2)}) collective-permute-start(bf16[384,2816]{1,0:T(8,128)(2,1)S(1)} %pad_maximum_fusion), channel_id=1, source_target_pairs={{0,64},{64,0},{1,65},{65,1},{2,66},{66,2},{3,67},{67,3},{4,68},{68... | collective-permute-start | bytes 6488072 | tf_op jit(solution)/shard_map/ppermute | solution.py:348

commit v8 on v7

--- a/solution.py
+++ b/solution.py
@@ -15,7 +15,6 @@
 DS = 256
 NEAR = Y * ZL
 F32 = jnp.float32
-FAR_GROUPS = [[c * ZH + (b + c) % ZH for b in range(ZH)] for c in range(CORES)]
 NEAR_GROUPS = [
     [c * Y * ZH * ZL + y * ZH * ZL + (q * ZL + r + 2 * c) % (ZH * ZL) for y in range(Y) for r in range(ZL)]
     for c in range(CORES)
@@ -33,7 +32,7 @@
 
 
 def select_kernel(base_ref, blocks_ref, out_hbm, picked, rows_out, sems):
-    base, core = base_ref[0], base_ref[1]
+    base = base_ref[0]
     j = lax.broadcasted_iota(jnp.int32, (NEAR, TOK), 0)
     expert = ((j // ZL) * (ZH * ZL) + ((base + j % ZL) & (ZH * ZL - 1))).astype(F32)
     hits = []
@@ -57,7 +56,7 @@
             pick = jnp.concatenate(
                 [(key[e : e + 1, :] == slot).astype(F32) for e in range(first, first + ZL)], axis=0
             )
-            picked[(b + core) & (ZH - 1)] = jnp.dot(
+            picked[b] = jnp.dot(
                 pick.astype(BF16), blocks_ref[b, 0:TOK, :], preferred_element_type=F32
             )
         for e in range(ZL):
@@ -280,16 +279,30 @@
     )(core, in_hbm(rows), in_hbm(mixed))
 
 
+def head_sum_kernel(parts_ref, out_ref):
+    for y in range(Y):
+        total = parts_ref[0, y]
+        for i in range(1, X * CORES):
+            total = total + parts_ref[i, y]
+        for z in range(ZH * ZL):
+            out_ref[z, :, y * 128 : (y + 1) * 128] = total[z : z + 1, :]
+
+
+def head_sums(parts):
+    return pl.pallas_call(
+        head_sum_kernel,
+        out_shape=jax.ShapeDtypeStruct((ZH * ZL, 1, Y * 128), F32),
+    )(in_vmem(parts))
+
+
 def final_kernel(
     parts_ref, key_ref, probs_ref, ids_ref, router_hbm, grad_ref, weight_ref,
     router_ref, total, sem,
 ):
     load_router = pltpu.make_async_copy(router_hbm, router_ref, sem)
     load_router.start()
-    parts = parts_ref[0]
-    for i in range(1, X):
-        parts = parts + parts_ref[i]
-    total[...] = parts.reshape(EXPERTS, 128)
+    for y in range(Y):
+        total[y * ZH * ZL : (y + 1) * ZH * ZL, :] = parts_ref[:, 0, y * 128 : (y + 1) * 128]
     back = total[...]
     key = key_ref[...]
     probs = probs_ref[...]
@@ -350,12 +363,10 @@
     )
     core_scalar = core.reshape(1).astype(jnp.int32)
     mixed, key, probs = mix(core_scalar, mine, theirs, ids, logits)
-    blocks = lax.all_gather(
-        block, ("core", "zh"), axis=0, tiled=False, axis_index_groups=FAR_GROUPS
-    )
+    blocks = lax.all_gather(block, "zh", axis=0, tiled=False)
     z = lax.axis_index("zh") * ZL + lax.axis_index("zl")
     base = ((z - 2 * core) & (ZH * ZL - ZL)) + 2 * core
-    outgoing = select_rows(jnp.stack([base, core]).astype(jnp.int32), blocks)
+    outgoing = select_rows(base.reshape(1).astype(jnp.int32), blocks)
     received = lax.all_to_all(
         outgoing,
         ("core", "y", "zh", "zl"),
@@ -365,10 +376,17 @@
         axis_index_groups=NEAR_GROUPS,
     )
     part = slot_sums(core_scalar, received, mixed)
-    part = jnp.sum(lax.all_gather(part, "core", axis=0, tiled=False), axis=0)
-    part = jnp.broadcast_to(part[None], (X,) + part.shape).reshape(X * EXPERTS, 1, 128)
-    part = lax.all_to_all(part, ("x",) + EXPERT, split_axis=0, concat_axis=0, tiled=True)
-    part = part.reshape(X, EXPERTS, 1, 128)
+    part = part.reshape(1, Y, ZH * ZL, 128)
+    part = jnp.broadcast_to(part, (X * CORES,) + part.shape[1:])
+    part = lax.all_to_all(
+        part.reshape(X * CORES * Y, ZH * ZL, 128),
+        ("x", "core", "y"),
+        split_axis=0,
+        concat_axis=0,
+        tiled=True,
+    )
+    part = head_sums(part.reshape(X * CORES, Y, ZH * ZL, 128))
+    part = lax.all_to_all(part, ("zh", "zl"), split_axis=0, concat_axis=0, tiled=True)
     grad, weight_grad = finish(part, key, probs, ids, router_weight.T)
     return grad, weight_grad.T
 

time: 114 us -> 113 us (level)
    all_gather x2 -> x1, blocking collectives: 33.4 us -> 31.5 us  [body(): blocks = lax.all_gather(block, 'zh', axis=0, tiled=False)]
    all_to_all x1 -> x2, blocking collectives: 33.9 us -> 34.6 us  [the longest x1 20.2 us: body(): lax.all_to_all(part, ('zh', 'zl'), split_axis=0, concat_axis=0, tiled=True)]
where the time goes in v8:
time: 113 us
  blocking collectives  66.2 us (59%)
  waiting for transfers between devices  17.4 us (15%)
  starting transfers between devices  16.6 us (15%)
  Pallas kernels  11.5 us (10%)
    all_gather x1, blocking collectives, body(): blocks = lax.all_gather(block, 'zh', axis=0, tiled=False)  31.5 us
    all_to_all x1, blocking collectives, body(): lax.all_to_all(part, ('zh', 'zl'), split_axis=0, concat_axis=0, tiled=True)  20.2 us
    all_to_all x1, blocking collectives, body(): lax.all_to_all(part.reshape(X * CORES * Y, ZH * ZL, 128), ('x', 'core', '...  14.4 us
    all_to_all x1, waiting for transfers between devices, body(): lax.all_to_all(outgoing, ('core', 'y', 'zh', 'zl'), split_axis=0, concat_...  13.6 us
    all_to_all x1, starting transfers between devices, body(): lax.all_to_all(outgoing, ('core', 'y', 'zh', 'zl'), split_axis=0, concat_...  9.5 us
    all_to_all x1, starting transfers between devices, body(): along = lax.all_to_all(along, 'x', split_axis=0, concat_axis=0, tiled=True)  4.85 us
    ppermute x1, waiting for transfers between devices, body(): lax.ppermute(jnp.concatenate([mine[:, :slots], weight_other], axis=1), 'c...  3.86 us
    pallas_call x1, Pallas kernels, exchange_blocks(): pl.pallas_call(exchange_kernel, out_shape=(pltpu.HBM((X, width, EXPERTS *...  2.78 us
  transfers between devices with their start and end apart: 3, of which 2 were waited for; matrix products, arithmetic and copies ran while one was open for 0% of the time, Pallas kernels for 4%

profile of v8, /device:TPU:1, one launch (start us, length us, event | category | flops | bytes accessed | tf_op | source)
XLA Modules:
  0.0 112.8 jit_solution(10499912550166258244)
XLA Ops:
  0.6 2.8 %shard_map.77 = (bf16[4,96,3072]{2,1,0:T(8,128)(2,1)}, bf16[272,256]{1,0:T(8,128)(2,1)S(1)}) custom-call(s32[1]{0:T(128)} %bitcast.2.head_ref, s32[8,256]{1,0:T(8,128)} %bitcast.20, bf16[256,2048]{1,0:T(8,128)(2,1)} %grad_hbm.1, bf16[2560,96]{1,0:T(8,128)(2,1)} %bitcast.25, bf16[96,2048]{1,0:T(8,128)(2,1)} %bitcast.26), custom_call_target="tpu_custom_call" | custom-call | tf_op jit(solution)/shard_map/pallas_call | solution.py:138
  3.4 4.9 %all-to-all-start.1 = ((bf16[4,96,3072]{2,1,0:T(8,128)(2,1)}), bf16[4,96,3072]{2,1,0:T(8,128)(2,1)S(1)}, u32[]{:S(2)}, u32[]{:S(2)}) async-start(bf16[4,96,3072]{2,1,0:T(8,128)(2,1)} %get-tuple-element.10), calls=%async_computation.1 | async-start | bytes 4718592 | tf_op jit(solution)/shard_map/all_to_all | solution.py:358
  8.3 31.5 %all-gather = bf16[1088,256]{1,0:T(8,128)(2,1)S(1)} all-gather(bf16[272,256]{1,0:T(8,128)(2,1)S(1)} %get-tuple-element.9), channel_id=2, replica_groups=mesh['x'=4,'core'=2,'y'=4,'zh'=4,'zl'=4] {'zh'}, dimensions={0}, use_global_device_ids=true | all-gather | bytes 696320 | tf_op jit(solution)/shard_map/all_gather | solution.py:366
  39.8 1.5 %shard_map.78 = bf16[16,160,256]{2,1,0:T(8,128)(2,1)} custom-call(s32[1]{0:T(128)} %bitcast.1.base_ref, bf16[4,272,256]{2,1,0:T(8,128)(2,1)S(1)} %bitcast.17), custom_call_target="tpu_custom_call" | custom-call | tf_op jit(solution)/shard_map/pallas_call | solution.py:73
  41.3 0.0 all-to-all-done.1
  41.3 9.5 %all-to-all-start = ((bf16[16,160,256]{2,1,0:T(8,128)(2,1)}), bf16[16,160,256]{2,1,0:T(8,128)(2,1)}, u32[]{:S(2)}, u32[]{:S(2)}) async-start(bf16[16,160,256]{2,1,0:T(8,128)(2,1)} %shard_map.78), calls=%async_computation | async-start | bytes 2621440 | tf_op jit(solution)/shard_map/all_to_all | solution.py:370
  50.8 0.1 slice.4
  51.0 0.0 copy-start
  51.0 0.0 copy-start.1
  51.0 0.1 pad_maximum_fusion
  51.2 2.3 %collective-permute-start = (bf16[384,2816]{1,0:T(8,128)(2,1)S(1)}, bf16[384,2816]{1,0:T(8,128)(2,1)S(1)}, u32[]{:S(2)}, u32[]{:S(2)}) collective-permute-start(bf16[384,2816]{1,0:T(8,128)(2,1)S(1)} %pad_maximum_fusion), channel_id=1, source_target_pairs={{0,64},{64,0},{1,65},{65,1},{2,66},{66,2},{3,67},{67,3},{4,68},{68... | collective-permute-start | bytes 6488072 | tf_op jit(solution)/shard_map/ppermute | solution.py:361
  53.5 3.9 %collective-permute-done.theirs_ref = bf16[384,2816]{1,0:T(8,128)(2,1)S(1)} collective-permute-done((bf16[384,2816]{1,0:T(8,128)(2,1)S(1)}, bf16[384,2816]{1,0:T(8,128)(2,1)S(1)}, u32[]{:S(2)}, u32[]{:S(2)}) %collective-permute-start) | collective-permute-done | bytes 2162720 | tf_op jit(solution)/shard_map/ppermute | solution.py:361
  57.3 0.0 copy-done
  57.3 0.0 copy-done.1
  57.3 2.6 %shard_map.79 = (bf16[2560,256]{1,0:T(8,128)(2,1)}, f32[64,256]{1,0:T(8,128)S(1)}, f32[64,256]{1,0:T(8,128)S(1)}) custom-call(s32[1]{0:T(128)} %bitcast.core_ref, bf16[384,3072]{1,0:T(8,128)(2,1)S(1)} %bitcast.16, bf16[384,2816]{1,0:T(8,128)(2,1)S(1)} %collective-permute-done.theirs_ref, s32[8,256]{1,0:T(8,128)S(1)} %bitcast.21, f32[8,256]{1,0:T(8,128)S(1)} %bitcast.23), custom_call_target="tpu_custom_call" | custom-call | tf_op jit(solution)/shard_map/pallas_call | solution.py:216
  59.9 13.6 %all-to-all-done.rows_hbm = bf16[16,160,256]{2,1,0:T(8,128)(2,1)} async-done(((bf16[16,160,256]{2,1,0:T(8,128)(2,1)}), bf16[16,160,256]{2,1,0:T(8,128)(2,1)}, u32[]{:S(2)}, u32[]{:S(2)}) %all-to-all-start) | async-done | bytes 1310752 | tf_op jit(solution)/shard_map/all_to_all | solution.py:370
  73.5 1.9 %shard_map.80 = f32[64,1,128]{2,1,0:T(1,128)S(1)} custom-call(s32[1]{0:T(128)} %bitcast.core_ref, bf16[16,160,256]{2,1,0:T(8,128)(2,1)} %all-to-all-done.rows_hbm, bf16[2560,256]{1,0:T(8,128)(2,1)} %get-tuple-element.11.mixed_hbm), custom_call_target="tpu_custom_call" | custom-call | tf_op jit(solution)/shard_map/pallas_call | solution.py:264
  75.4 14.4 %all_to_all.20 = f32[32,16,128]{2,1,0:T(8,128)S(1)} all-to-all(f32[32,16,128]{2,1,0:T(8,128)S(1)} %bitcast.24), channel_id=1, replica_groups=mesh['x'=4,'core'=2,'y'=4,'zh'=4,'zl'=4] {'x','core','y'}, dimensions={0} | all-to-all | bytes 524288 | tf_op jit(solution)/shard_map/all_to_all | solution.py:381
  89.9 0.6 shard_map.81
  90.5 20.2 %all_to_all.21.parts_ref = f32[16,1,512]{2,1,0:T(1,128)S(1)} all-to-all(f32[16,1,512]{2,1,0:T(1,128)} %shard_map.81), channel_id=1, replica_groups=mesh['x'=4,'core'=2,'y'=4,'zh'=4,'zl'=4] {'zh','zl'}, dimensions={0} | all-to-all | bytes 65536 | tf_op jit(solution)/shard_map/all_to_all | solution.py:389
  110.7 2.1 %shard_map.82 = (bf16[256,256]{1,0:T(8,128)(2,1)}, f32[8,256]{1,0:T(8,128)}) custom-call(f32[16,1,512]{2,1,0:T(1,128)S(1)} %all_to_all.21.parts_ref, f32[64,256]{1,0:T(8,128)S(1)} %get-tuple-element.12.key_ref, f32[64,256]{1,0:T(8,128)S(1)} %get-tuple-element.13.probs_ref, s32[8,256]{1,0:T(8,128)S(1)} %bitcast.22, bf16[64,256]{1,0:T(8,128)(2,1)} %bitcast.27), custom_call_target="tpu_custom_call" | custom-call | tf_op jit(solution)/shard_map/pallas_call | solution.py:328
  (2 shorter events, 0.1 us)
Async XLA Ops:
  3.4 37.9 %all-to-all-start.1 = ((bf16[4,96,3072]{2,1,0:T(8,128)(2,1)}), bf16[4,96,3072]{2,1,0:T(8,128)(2,1)S(1)}, u32[]{:S(2)}, u32[]{:S(2)}) async-start(bf16[4,96,3072]{2,1,0:T(8,128)(2,1)} %get-tuple-element.10), calls=%async_computation.1 | async-start | bytes 4718592 | tf_op jit(solution)/shard_map/all_to_all | solution.py:358
  41.3 32.2 %all-to-all-start = ((bf16[16,160,256]{2,1,0:T(8,128)(2,1)}), bf16[16,160,256]{2,1,0:T(8,128)(2,1)}, u32[]{:S(2)}, u32[]{:S(2)}) async-start(bf16[16,160,256]{2,1,0:T(8,128)(2,1)} %shard_map.78), calls=%async_computation | async-start | bytes 2621440 | tf_op jit(solution)/shard_map/all_to_all | solution.py:370
  51.0 6.3 %copy-start = (s32[256,8]{0,1:T(8,128)S(1)}, s32[256,8]{0,1:T(8,128)}, u32[]{:S(2)}) copy-start(s32[256,8]{0,1:T(8,128)} %param.7) | copy-start | bytes 24580
  51.0 6.3 %copy-start.1 = (f32[256,8]{0,1:T(8,128)S(1)}, f32[256,8]{0,1:T(8,128)}, u32[]{:S(2)}) copy-start(f32[256,8]{0,1:T(8,128)} %param.8) | copy-start | bytes 24580
  51.2 6.2 %collective-permute-start = (bf16[384,2816]{1,0:T(8,128)(2,1)S(1)}, bf16[384,2816]{1,0:T(8,128)(2,1)S(1)}, u32[]{:S(2)}, u32[]{:S(2)}) collective-permute-start(bf16[384,2816]{1,0:T(8,128)(2,1)S(1)} %pad_maximum_fusion), channel_id=1, source_target_pairs={{0,64},{64,0},{1,65},{65,1},{2,66},{66,2},{3,67},{67,3},{4,68},{68... | collective-permute-start | bytes 6488072 | tf_op jit(solution)/shard_map/ppermute | solution.py:361

commit v9 on v8

--- a/solution.py
+++ b/solution.py
@@ -243,27 +243,32 @@
     for pair in copies:
         for copy in pair:
             copy.start()
-    own_lane = lax.broadcasted_iota(jnp.int32, (CAP, 128), 0) == lax.broadcasted_iota(
-        jnp.int32, (CAP, 128), 1
-    )
+    slot = lax.broadcasted_iota(jnp.int32, (CAP, 128), 0)
+    lane = lax.broadcasted_iota(jnp.int32, (CAP, 128), 1)
+    own_lane = (lane == slot, lane == slot + 64)
     for i in range(steps):
         for copy in copies[i]:
             copy.wait()
-        for e in range(i * per, (i + 1) * per):
-            rows = rows_ref[e].astype(F32) * mixed_ref[
-                e * ZH * CAP : (e + 1) * ZH * CAP, :
-            ].astype(F32)
-            sums = jnp.sum(rows[:, 0:128] + rows[:, 128:256], axis=1, keepdims=True)
+        for e in range(i * per, (i + 1) * per, 2):
+            sums = []
+            for odd in range(2):
+                rows = rows_ref[e + odd].astype(F32) * mixed_ref[
+                    (e + odd) * ZH * CAP : (e + odd + 1) * ZH * CAP, :
+                ].astype(F32)
+                sums.append(jnp.sum(rows[:, 0:128] + rows[:, 128:256], axis=1, keepdims=True))
             for b in range(ZH):
-                lanes = jnp.where(own_lane, sums[b * CAP : (b + 1) * CAP, :], 0.0)
-                place = (e // ZL * ZH + b) * ZL + ((e % ZL) ^ (2 * core_ref[0]))
+                slots = slice(b * CAP, (b + 1) * CAP)
+                lanes = jnp.where(own_lane[0], sums[0][slots, :], 0.0) + jnp.where(
+                    own_lane[1], sums[1][slots, :], 0.0
+                )
+                place = (e // ZL * ZH + b) * 2 + ((e % ZL // 2) ^ core_ref[0])
                 out_ref[place] = jnp.sum(lanes, axis=0, keepdims=True)
 
 
 def slot_sums(core, rows, mixed):
     return pl.pallas_call(
         value_kernel,
-        out_shape=jax.ShapeDtypeStruct((EXPERTS, 1, 128), F32),
+        out_shape=jax.ShapeDtypeStruct((EXPERTS // 2, 1, 128), F32),
         in_specs=[
             pl.BlockSpec(memory_space=pltpu.SMEM),
             pl.BlockSpec(memory_space=pltpu.HBM),
@@ -284,8 +289,10 @@
         total = parts_ref[0, y]
         for i in range(1, X * CORES):
             total = total + parts_ref[i, y]
-        for z in range(ZH * ZL):
-            out_ref[z, :, y * 128 : (y + 1) * 128] = total[z : z + 1, :]
+        turned = pltpu.roll(total, 64, 1)
+        for z in range(0, ZH * ZL, 2):
+            out_ref[z, :, y * 128 : (y + 1) * 128] = total[z // 2 : z // 2 + 1, :]
+            out_ref[z + 1, :, y * 128 : (y + 1) * 128] = turned[z // 2 : z // 2 + 1, :]
 
 
 def head_sums(parts):
@@ -376,16 +383,16 @@
         axis_index_groups=NEAR_GROUPS,
     )
     part = slot_sums(core_scalar, received, mixed)
-    part = part.reshape(1, Y, ZH * ZL, 128)
-    part = jnp.broadcast_to(part, (X * CORES,) + part.shape[1:])
+    rows = ZH * ZL // 2
+    part = jnp.broadcast_to(part.reshape(1, Y, rows, 128), (X * CORES, Y, rows, 128))
     part = lax.all_to_all(
-        part.reshape(X * CORES * Y, ZH * ZL, 128),
+        part.reshape(X * CORES * Y, rows, 128),
         ("x", "core", "y"),
         split_axis=0,
         concat_axis=0,
         tiled=True,
     )
-    part = head_sums(part.reshape(X * CORES, Y, ZH * ZL, 128))
+    part = head_sums(part.reshape(X * CORES, Y, rows, 128))
     part = lax.all_to_all(part, ("zh", "zl"), split_axis=0, concat_axis=0, tiled=True)
     grad, weight_grad = finish(part, key, probs, ids, router_weight.T)
     return grad, weight_grad.T

time: 113 us -> 112 us (level)
  blocking collectives: 66.2 us -> 64.9 us
    all_to_all x1, blocking collectives: 14.4 us -> 13.2 us  [body(): lax.all_to_all(part.reshape(X * CORES * Y, rows, 128), ('x', 'core', 'y')...]
where the time goes in v9:
time: 112 us
  blocking collectives  64.9 us (58%)
  waiting for transfers between devices  17.4 us (16%)
  starting transfers between devices  16.6 us (15%)
  Pallas kernels  11.6 us (10%)
    all_gather x1, blocking collectives, body(): blocks = lax.all_gather(block, 'zh', axis=0, tiled=False)  31.5 us
    all_to_all x1, blocking collectives, body(): lax.all_to_all(part, ('zh', 'zl'), split_axis=0, concat_axis=0, tiled=True)  20.2 us
    all_to_all x1, waiting for transfers between devices, body(): lax.all_to_all(outgoing, ('core', 'y', 'zh', 'zl'), split_axis=0, concat_...  13.6 us
    all_to_all x1, blocking collectives, body(): lax.all_to_all(part.reshape(X * CORES * Y, rows, 128), ('x', 'core', 'y')...  13.2 us
    all_to_all x1, starting transfers between devices, body(): lax.all_to_all(outgoing, ('core', 'y', 'zh', 'zl'), split_axis=0, concat_...  9.5 us
    all_to_all x1, starting transfers between devices, body(): along = lax.all_to_all(along, 'x', split_axis=0, concat_axis=0, tiled=True)  4.85 us
    ppermute x1, waiting for transfers between devices, body(): lax.ppermute(jnp.concatenate([mine[:, :slots], weight_other], axis=1), 'c...  3.86 us
    pallas_call x1, Pallas kernels, exchange_blocks(): pl.pallas_call(exchange_kernel, out_shape=(pltpu.HBM((X, width, EXPERTS *...  2.78 us
  transfers between devices with their start and end apart: 3, of which 2 were waited for; matrix products, arithmetic and copies ran while one was open for 0% of the time, Pallas kernels for 4%

profile of v9, /device:TPU:1, one launch (start us, length us, event | category | flops | bytes accessed | tf_op | source)
XLA Modules:
  0.0 111.6 jit_solution(13353425395435586139)
XLA Ops:
  0.6 2.8 %shard_map.77 = (bf16[4,96,3072]{2,1,0:T(8,128)(2,1)}, bf16[272,256]{1,0:T(8,128)(2,1)S(1)}) custom-call(s32[1]{0:T(128)} %bitcast.2.head_ref, s32[8,256]{1,0:T(8,128)} %bitcast.19, bf16[256,2048]{1,0:T(8,128)(2,1)} %grad_hbm.1, bf16[2560,96]{1,0:T(8,128)(2,1)} %bitcast.24, bf16[96,2048]{1,0:T(8,128)(2,1)} %bitcast.26), custom_call_target="tpu_custom_call" | custom-call | tf_op jit(solution)/shard_map/pallas_call | solution.py:138
  3.4 4.9 %all-to-all-start.1 = ((bf16[4,96,3072]{2,1,0:T(8,128)(2,1)}), bf16[4,96,3072]{2,1,0:T(8,128)(2,1)S(1)}, u32[]{:S(2)}, u32[]{:S(2)}) async-start(bf16[4,96,3072]{2,1,0:T(8,128)(2,1)} %get-tuple-element.10), calls=%async_computation.1 | async-start | bytes 4718592 | tf_op jit(solution)/shard_map/all_to_all | solution.py:365
  8.3 31.5 %all-gather = bf16[1088,256]{1,0:T(8,128)(2,1)S(1)} all-gather(bf16[272,256]{1,0:T(8,128)(2,1)S(1)} %get-tuple-element.9), channel_id=2, replica_groups=mesh['x'=4,'core'=2,'y'=4,'zh'=4,'zl'=4] {'zh'}, dimensions={0}, use_global_device_ids=true | all-gather | bytes 696320 | tf_op jit(solution)/shard_map/all_gather | solution.py:373
  39.8 1.5 %shard_map.78 = bf16[16,160,256]{2,1,0:T(8,128)(2,1)} custom-call(s32[1]{0:T(128)} %bitcast.1.base_ref, bf16[4,272,256]{2,1,0:T(8,128)(2,1)S(1)} %bitcast.17), custom_call_target="tpu_custom_call" | custom-call | tf_op jit(solution)/shard_map/pallas_call | solution.py:73
  41.3 0.0 all-to-all-done.1
  41.3 9.5 %all-to-all-start = ((bf16[16,160,256]{2,1,0:T(8,128)(2,1)}), bf16[16,160,256]{2,1,0:T(8,128)(2,1)}, u32[]{:S(2)}, u32[]{:S(2)}) async-start(bf16[16,160,256]{2,1,0:T(8,128)(2,1)} %shard_map.78), calls=%async_computation | async-start | bytes 2621440 | tf_op jit(solution)/shard_map/all_to_all | solution.py:377
  50.8 0.1 slice.4
  51.0 0.0 copy-start
  51.0 0.0 copy-start.1
  51.0 0.1 pad_maximum_fusion
  51.2 2.3 %collective-permute-start = (bf16[384,2816]{1,0:T(8,128)(2,1)S(1)}, bf16[384,2816]{1,0:T(8,128)(2,1)S(1)}, u32[]{:S(2)}, u32[]{:S(2)}) collective-permute-start(bf16[384,2816]{1,0:T(8,128)(2,1)S(1)} %pad_maximum_fusion), channel_id=1, source_target_pairs={{0,64},{64,0},{1,65},{65,1},{2,66},{66,2},{3,67},{67,3},{4,68},{68... | collective-permute-start | bytes 6488072 | tf_op jit(solution)/shard_map/ppermute | solution.py:368
  53.5 3.9 %collective-permute-done.theirs_ref = bf16[384,2816]{1,0:T(8,128)(2,1)S(1)} collective-permute-done((bf16[384,2816]{1,0:T(8,128)(2,1)S(1)}, bf16[384,2816]{1,0:T(8,128)(2,1)S(1)}, u32[]{:S(2)}, u32[]{:S(2)}) %collective-permute-start) | collective-permute-done | bytes 2162720 | tf_op jit(solution)/shard_map/ppermute | solution.py:368
  57.3 0.0 copy-done
  57.3 0.0 copy-done.1
  57.3 2.6 %shard_map.79 = (bf16[2560,256]{1,0:T(8,128)(2,1)}, f32[64,256]{1,0:T(8,128)S(1)}, f32[64,256]{1,0:T(8,128)S(1)}) custom-call(s32[1]{0:T(128)} %bitcast.core_ref, bf16[384,3072]{1,0:T(8,128)(2,1)S(1)} %bitcast.16, bf16[384,2816]{1,0:T(8,128)(2,1)S(1)} %collective-permute-done.theirs_ref, s32[8,256]{1,0:T(8,128)S(1)} %bitcast.20, f32[8,256]{1,0:T(8,128)S(1)} %bitcast.23), custom_call_target="tpu_custom_call" | custom-call | tf_op jit(solution)/shard_map/pallas_call | solution.py:216
  59.9 13.6 %all-to-all-done.rows_hbm = bf16[16,160,256]{2,1,0:T(8,128)(2,1)} async-done(((bf16[16,160,256]{2,1,0:T(8,128)(2,1)}), bf16[16,160,256]{2,1,0:T(8,128)(2,1)}, u32[]{:S(2)}, u32[]{:S(2)}) %all-to-all-start) | async-done | bytes 1310752 | tf_op jit(solution)/shard_map/all_to_all | solution.py:377
  73.5 1.9 %shard_map.80 = f32[32,1,128]{2,1,0:T(1,128)S(1)} custom-call(s32[1]{0:T(128)} %bitcast.core_ref, bf16[16,160,256]{2,1,0:T(8,128)(2,1)} %all-to-all-done.rows_hbm, bf16[2560,256]{1,0:T(8,128)(2,1)} %get-tuple-element.11.mixed_hbm), custom_call_target="tpu_custom_call" | custom-call | tf_op jit(solution)/shard_map/pallas_call | solution.py:269
  75.4 13.2 %all_to_all.20 = f32[32,8,128]{2,1,0:T(8,128)S(1)} all-to-all(f32[32,8,128]{2,1,0:T(8,128)S(1)} %bitcast.25), channel_id=1, replica_groups=mesh['x'=4,'core'=2,'y'=4,'zh'=4,'zl'=4] {'x','core','y'}, dimensions={0} | all-to-all | bytes 262144 | tf_op jit(solution)/shard_map/all_to_all | solution.py:388
  88.6 0.7 shard_map.81
  89.3 20.2 %all_to_all.21.parts_ref = f32[16,1,512]{2,1,0:T(1,128)S(1)} all-to-all(f32[16,1,512]{2,1,0:T(1,128)} %shard_map.81), channel_id=1, replica_groups=mesh['x'=4,'core'=2,'y'=4,'zh'=4,'zl'=4] {'zh','zl'}, dimensions={0} | all-to-all | bytes 65536 | tf_op jit(solution)/shard_map/all_to_all | solution.py:396
  109.5 2.1 %shard_map.82 = (bf16[256,256]{1,0:T(8,128)(2,1)}, f32[8,256]{1,0:T(8,128)}) custom-call(f32[16,1,512]{2,1,0:T(1,128)S(1)} %all_to_all.21.parts_ref, f32[64,256]{1,0:T(8,128)S(1)} %get-tuple-element.12.key_ref, f32[64,256]{1,0:T(8,128)S(1)} %get-tuple-element.13.probs_ref, s32[8,256]{1,0:T(8,128)S(1)} %bitcast.21, bf16[64,256]{1,0:T(8,128)(2,1)} %bitcast.27), custom_call_target="tpu_custom_call" | custom-call | tf_op jit(solution)/shard_map/pallas_call | solution.py:335
  (2 shorter events, 0.0 us)
Async XLA Ops:
  3.4 37.9 %all-to-all-start.1 = ((bf16[4,96,3072]{2,1,0:T(8,128)(2,1)}), bf16[4,96,3072]{2,1,0:T(8,128)(2,1)S(1)}, u32[]{:S(2)}, u32[]{:S(2)}) async-start(bf16[4,96,3072]{2,1,0:T(8,128)(2,1)} %get-tuple-element.10), calls=%async_computation.1 | async-start | bytes 4718592 | tf_op jit(solution)/shard_map/all_to_all | solution.py:365
  41.3 32.2 %all-to-all-start = ((bf16[16,160,256]{2,1,0:T(8,128)(2,1)}), bf16[16,160,256]{2,1,0:T(8,128)(2,1)}, u32[]{:S(2)}, u32[]{:S(2)}) async-start(bf16[16,160,256]{2,1,0:T(8,128)(2,1)} %shard_map.78), calls=%async_computation | async-start | bytes 2621440 | tf_op jit(solution)/shard_map/all_to_all | solution.py:377
  51.0 6.3 %copy-start = (s32[256,8]{0,1:T(8,128)S(1)}, s32[256,8]{0,1:T(8,128)}, u32[]{:S(2)}) copy-start(s32[256,8]{0,1:T(8,128)} %param.7) | copy-start | bytes 24580
  51.0 6.3 %copy-start.1 = (f32[256,8]{0,1:T(8,128)S(1)}, f32[256,8]{0,1:T(8,128)}, u32[]{:S(2)}) copy-start(f32[256,8]{0,1:T(8,128)} %param.8) | copy-start | bytes 24580
  51.2 6.2 %collective-permute-start = (bf16[384,2816]{1,0:T(8,128)(2,1)S(1)}, bf16[384,2816]{1,0:T(8,128)(2,1)S(1)}, u32[]{:S(2)}, u32[]{:S(2)}) collective-permute-start(bf16[384,2816]{1,0:T(8,128)(2,1)S(1)} %pad_maximum_fusion), channel_id=1, source_target_pairs={{0,64},{64,0},{1,65},{65,1},{2,66},{66,2},{3,67},{67,3},{4,68},{68... | collective-permute-start | bytes 6488072 | tf_op jit(solution)/shard_map/ppermute | solution.py:368

commit v10 on v9

--- a/solution.py
+++ b/solution.py
@@ -31,13 +31,14 @@
     return pltpu.with_memory_space_constraint(array, pltpu.HBM)
 
 
-def select_kernel(base_ref, blocks_ref, out_hbm, picked, rows_out, sems):
+def select_kernel(base_ref, block0, block1, block2, block3, out_hbm, picked, rows_out, sems):
     base = base_ref[0]
+    blocks = (block0, block1, block2, block3)
     j = lax.broadcasted_iota(jnp.int32, (NEAR, TOK), 0)
     expert = ((j // ZL) * (ZH * ZL) + ((base + j % ZL) & (ZH * ZL - 1))).astype(F32)
     hits = []
     for b in range(ZH):
-        ids = blocks_ref[b, TOK : TOK + 16, :].astype(F32)
+        ids = blocks[b][TOK : TOK + 16, :].astype(F32)
         hit = jnp.zeros((NEAR, TOK), F32)
         for k in range(TOPK):
             hit = hit + (ids[k : k + 1, :] == expert).astype(F32)
@@ -57,7 +58,7 @@
                 [(key[e : e + 1, :] == slot).astype(F32) for e in range(first, first + ZL)], axis=0
             )
             picked[b] = jnp.dot(
-                pick.astype(BF16), blocks_ref[b, 0:TOK, :], preferred_element_type=F32
+                pick.astype(BF16), blocks[b][0:TOK, :], preferred_element_type=F32
             )
         for e in range(ZL):
             rows = [picked[b, e * CAP : (e + 1) * CAP, :] for b in range(ZH)]
@@ -75,8 +76,8 @@
         out_shape=pltpu.HBM((NEAR, ZH * CAP, DS), BF16),
         in_specs=[
             pl.BlockSpec(memory_space=pltpu.SMEM),
-            pl.BlockSpec(memory_space=pltpu.VMEM),
-        ],
+        ]
+        + [pl.BlockSpec(memory_space=pltpu.VMEM)] * ZH,
         out_specs=pl.BlockSpec(memory_space=pltpu.HBM),
         scratch_shapes=[
             pltpu.VMEM((ZH, ZL * CAP, DS), F32),
@@ -84,7 +85,7 @@
             pltpu.SemaphoreType.DMA((Y,)),
         ],
         compiler_params=pltpu.CompilerParams(vmem_limit_bytes=16 << 20),
-    )(base, blocks)
+    )(base, *blocks)
 
 
 def exchange_kernel(
@@ -165,7 +166,7 @@
 ):
     plan(ids_ref[...], logits_ref[...], key_ref, probs_ref)
     slots = EXPERTS * CAP
-    core = core_ref[0]
+    core, base = core_ref[0], core_ref[1]
     weight = jnp.where(
         core == 0, mine_ref[:, slots : slots + DS], mine_ref[:, slots + DS : slots + 2 * DS]
     )
@@ -181,9 +182,11 @@
         )
         for zl in range(ZL):
             place = zl ^ (2 * core)
+            node = ((base + place) & (ZH * ZL - 1)) >> 2
             for zh in range(ZH):
                 src = (zh * ZL + zl) * CAP
-                dst = pl.multiple_of(y * group + (place * ZH + zh) * CAP, 8)
+                back = (node - zh) & (ZH - 1)
+                dst = pl.multiple_of(y * group + (place * ZH + back) * CAP, 8)
                 out_ref[pl.ds(dst, CAP), :] = mixed[src : src + CAP, :]
         rows = pl.ds(y * group, group)
         rounded[rows, :] = out_ref[rows, :].astype(BF16)
@@ -261,7 +264,9 @@
                 lanes = jnp.where(own_lane[0], sums[0][slots, :], 0.0) + jnp.where(
                     own_lane[1], sums[1][slots, :], 0.0
                 )
-                place = (e // ZL * ZH + b) * 2 + ((e % ZL // 2) ^ core_ref[0])
+                pair = (e % ZL // 2) ^ core_ref[0]
+                node = ((core_ref[1] + e % ZL) & (ZH * ZL - 1)) >> 2
+                place = (e // ZL * ZH + ((node - b) & (ZH - 1))) * 2 + pair
                 out_ref[place] = jnp.sum(lanes, axis=0, keepdims=True)
 
 
@@ -368,11 +373,13 @@
     theirs = lax.ppermute(
         jnp.concatenate([mine[:, :slots], weight_other], axis=1), "core", [(0, 1), (1, 0)]
     )
-    core_scalar = core.reshape(1).astype(jnp.int32)
-    mixed, key, probs = mix(core_scalar, mine, theirs, ids, logits)
-    blocks = lax.all_gather(block, "zh", axis=0, tiled=False)
     z = lax.axis_index("zh") * ZL + lax.axis_index("zl")
     base = ((z - 2 * core) & (ZH * ZL - ZL)) + 2 * core
+    place = jnp.stack([core, base]).astype(jnp.int32)
+    mixed, key, probs = mix(place, mine, theirs, ids, logits)
+    blocks = [block] + [
+        lax.ppermute(block, "zh", [(i, (i + k) % ZH) for i in range(ZH)]) for k in range(1, ZH)
+    ]
     outgoing = select_rows(base.reshape(1).astype(jnp.int32), blocks)
     received = lax.all_to_all(
         outgoing,
@@ -382,7 +389,7 @@
         tiled=True,
         axis_index_groups=NEAR_GROUPS,
     )
-    part = slot_sums(core_scalar, received, mixed)
+    part = slot_sums(place, received, mixed)
     rows = ZH * ZL // 2
     part = jnp.broadcast_to(part.reshape(1, Y, rows, 128), (X * CORES, Y, rows, 128))
     part = lax.all_to_all(

time: 112 us -> 126 us (1.12)
  blocking collectives: 64.9 us -> 34.4 us
  starting transfers between devices: 16.6 us -> 38.9 us
  waiting for transfers between devices: 17.4 us -> 38.7 us
    all_gather x1 -> x0, blocking collectives: 31.5 us -> none  [body(): blocks = lax.all_gather(block, 'zh', axis=0, tiled=False)]
    ppermute x0 -> x3, starting transfers between devices: none -> 24.6 us  [body(): lax.ppermute(block, 'zh', [(i, (i + k) % ZH) for i in range(ZH)])]
    ppermute x0 -> x3, waiting for transfers between devices: none -> 20.3 us  [body(): lax.ppermute(block, 'zh', [(i, (i + k) % ZH) for i in range(ZH)])]
    all_to_all x1, starting transfers between devices: 9.5 us -> 7.51 us  [body(): lax.all_to_all(outgoing, ('core', 'y', 'zh', 'zl'), split_axis=0, concat_...]
    all_to_all x1, blocking collectives: 20.2 us -> 21.5 us  [body(): lax.all_to_all(part, ('zh', 'zl'), split_axis=0, concat_axis=0, tiled=True)]
  transfers between devices with their start and end apart: 3 -> 6, of which waited for: 2 -> 4; matrix products, arithmetic and copies ran while one was open for 0% -> 0% of each run, Pallas kernels for 4% -> 4%
where the time goes in v10:
time: 126 us
  starting transfers between devices  38.9 us (31%)
  waiting for transfers between devices  38.7 us (31%)
  blocking collectives  34.4 us (27%)
  Pallas kernels  12.6 us (10%)
    ppermute x3, starting transfers between devices, body(): lax.ppermute(block, 'zh', [(i, (i + k) % ZH) for i in range(ZH)])  24.6 us
    all_to_all x1, blocking collectives, body(): lax.all_to_all(part, ('zh', 'zl'), split_axis=0, concat_axis=0, tiled=True)  21.5 us
    ppermute x3, waiting for transfers between devices, body(): lax.ppermute(block, 'zh', [(i, (i + k) % ZH) for i in range(ZH)])  20.3 us
    all_to_all x1, waiting for transfers between devices, body(): lax.all_to_all(outgoing, ('core', 'y', 'zh', 'zl'), split_axis=0, concat_...  14.3 us
    all_to_all x1, blocking collectives, body(): lax.all_to_all(part.reshape(X * CORES * Y, rows, 128), ('x', 'core', 'y')...  12.9 us
    all_to_all x1, starting transfers between devices, body(): lax.all_to_all(outgoing, ('core', 'y', 'zh', 'zl'), split_axis=0, concat_...  7.51 us
    all_to_all x1, starting transfers between devices, body(): along = lax.all_to_all(along, 'x', split_axis=0, concat_axis=0, tiled=True)  4.85 us
    ppermute x1, waiting for transfers between devices, body(): lax.ppermute(jnp.concatenate([mine[:, :slots], weight_other], axis=1), 'c...  4.14 us
  transfers between devices with their start and end apart: 6, of which 4 were waited for; matrix products, arithmetic and copies ran while one was open for 0% of the time, Pallas kernels for 4%

profile of v10, /device:TPU:1, one launch (start us, length us, event | category | flops | bytes accessed | tf_op | source)
XLA Modules:
  0.0 125.8 jit_solution(11661886302496461745)
XLA Ops:
  0.6 2.8 %shard_map.77 = (bf16[4,96,3072]{2,1,0:T(8,128)(2,1)}, bf16[272,256]{1,0:T(8,128)(2,1)S(1)}) custom-call(s32[1]{0:T(128)} %bitcast.2.head_ref, s32[8,256]{1,0:T(8,128)} %bitcast.17, bf16[256,2048]{1,0:T(8,128)(2,1)} %grad_hbm.1, bf16[2560,96]{1,0:T(8,128)(2,1)} %bitcast.22, bf16[96,2048]{1,0:T(8,128)(2,1)} %bitcast.24), custom_call_target="tpu_custom_call" | custom-call | tf_op jit(solution)/shard_map/pallas_call | solution.py:139
  3.4 4.9 %all-to-all-start.1 = ((bf16[4,96,3072]{2,1,0:T(8,128)(2,1)}), bf16[4,96,3072]{2,1,0:T(8,128)(2,1)S(1)}, u32[]{:S(2)}, u32[]{:S(2)}) async-start(bf16[4,96,3072]{2,1,0:T(8,128)(2,1)} %get-tuple-element.10), calls=%async_computation.1 | async-start | bytes 4718592 | tf_op jit(solution)/shard_map/all_to_all | solution.py:370
  8.3 8.8 %collective-permute-start = (bf16[272,256]{1,0:T(8,128)(2,1)S(1)}, bf16[272,256]{1,0:T(8,128)(2,1)S(1)}, u32[]{:S(2)}, u32[]{:S(2)}) collective-permute-start(bf16[272,256]{1,0:T(8,128)(2,1)S(1)} %get-tuple-element.9.block0), channel_id=1, source_target_pairs={{0,4},{4,8},{8,12},{12,0},{1,5},{5,9},{9,13},{13,1},{2,6},{6,10},{... | collective-permute-start | bytes 417800 | tf_op jit(solution)/shard_map/ppermute | solution.py:381
  17.1 10.6 %collective-permute-start.1 = (bf16[272,256]{1,0:T(8,128)(2,1)S(1)}, bf16[272,256]{1,0:T(8,128)(2,1)S(1)}, u32[]{:S(2)}, u32[]{:S(2)}) collective-permute-start(bf16[272,256]{1,0:T(8,128)(2,1)S(1)} %get-tuple-element.9.block0), channel_id=1, source_target_pairs={{0,8},{4,12},{8,0},{12,4},{1,9},{5,13},{9,1},{13,5},{2,10},{6,14},... | collective-permute-start | bytes 417800 | tf_op jit(solution)/shard_map/ppermute | solution.py:381
  27.7 5.2 %collective-permute-start.2 = (bf16[272,256]{1,0:T(8,128)(2,1)S(1)}, bf16[272,256]{1,0:T(8,128)(2,1)S(1)}, u32[]{:S(2)}, u32[]{:S(2)}) collective-permute-start(bf16[272,256]{1,0:T(8,128)(2,1)S(1)} %get-tuple-element.9.block0), channel_id=1, source_target_pairs={{0,12},{4,0},{8,4},{12,8},{1,13},{5,1},{9,5},{13,9},{2,14},{6,2},{... | collective-permute-start | bytes 417800 | tf_op jit(solution)/shard_map/ppermute | solution.py:381
  32.9 0.0 collective-permute-done.block1
  32.9 13.1 %collective-permute-done.1.block2 = bf16[272,256]{1,0:T(8,128)(2,1)S(1)} collective-permute-done((bf16[272,256]{1,0:T(8,128)(2,1)S(1)}, bf16[272,256]{1,0:T(8,128)(2,1)S(1)}, u32[]{:S(2)}, u32[]{:S(2)}) %collective-permute-start.1) | collective-permute-done | bytes 139296 | tf_op jit(solution)/shard_map/ppermute | solution.py:381
  46.0 7.2 %collective-permute-done.2.block3 = bf16[272,256]{1,0:T(8,128)(2,1)S(1)} collective-permute-done((bf16[272,256]{1,0:T(8,128)(2,1)S(1)}, bf16[272,256]{1,0:T(8,128)(2,1)S(1)}, u32[]{:S(2)}, u32[]{:S(2)}) %collective-permute-start.2) | collective-permute-done | bytes 139296 | tf_op jit(solution)/shard_map/ppermute | solution.py:381
  53.2 1.5 %shard_map.78 = bf16[16,160,256]{2,1,0:T(8,128)(2,1)} custom-call(s32[1]{0:T(128)} %bitcast.1.base_ref, bf16[272,256]{1,0:T(8,128)(2,1)S(1)} %get-tuple-element.9.block0, bf16[272,256]{1,0:T(8,128)(2,1)S(1)} %collective-permute-done.block1, bf16[272,256]{1,0:T(8,128)(2,1)S(1)} %collective-permute-done.1.block2, ...), custom_call_target="tpu_custom_call" | custom-call | tf_op jit(solution)/shard_map/pallas_call | solution.py:74
  54.7 0.0 all-to-all-done.1
  54.7 7.5 %all-to-all-start = ((bf16[16,160,256]{2,1,0:T(8,128)(2,1)}), bf16[16,160,256]{2,1,0:T(8,128)(2,1)}, u32[]{:S(2)}, u32[]{:S(2)}) async-start(bf16[16,160,256]{2,1,0:T(8,128)(2,1)} %shard_map.78), calls=%async_computation | async-start | bytes 2621440 | tf_op jit(solution)/shard_map/all_to_all | solution.py:384
  62.2 0.1 slice.4
  62.4 0.0 copy-start
  62.4 0.0 copy-start.1
  62.4 0.1 pad_maximum_fusion
  62.6 1.9 %collective-permute-start.3 = (bf16[384,2816]{1,0:T(8,128)(2,1)S(1)}, bf16[384,2816]{1,0:T(8,128)(2,1)S(1)}, u32[]{:S(2)}, u32[]{:S(2)}) collective-permute-start(bf16[384,2816]{1,0:T(8,128)(2,1)S(1)} %pad_maximum_fusion), channel_id=1, source_target_pairs={{0,64},{64,0},{1,65},{65,1},{2,66},{66,2},{3,67},{67,3},{4,68},{68... | collective-permute-start | bytes 6488072 | tf_op jit(solution)/shard_map/ppermute | solution.py:373
  64.5 0.1 pad_add_fusion.core_ref
  64.6 4.1 %collective-permute-done.3.theirs_ref = bf16[384,2816]{1,0:T(8,128)(2,1)S(1)} collective-permute-done((bf16[384,2816]{1,0:T(8,128)(2,1)S(1)}, bf16[384,2816]{1,0:T(8,128)(2,1)S(1)}, u32[]{:S(2)}, u32[]{:S(2)}) %collective-permute-start.3) | collective-permute-done | bytes 2162720 | tf_op jit(solution)/shard_map/ppermute | solution.py:373
  68.7 0.0 copy-done
  68.7 0.0 copy-done.1
  68.7 3.1 %shard_map.79 = (bf16[2560,256]{1,0:T(8,128)(2,1)}, f32[64,256]{1,0:T(8,128)S(1)}, f32[64,256]{1,0:T(8,128)S(1)}) custom-call(s32[2]{0:T(128)S(1)} %pad_add_fusion.core_ref, bf16[384,3072]{1,0:T(8,128)(2,1)S(1)} %bitcast.15, bf16[384,2816]{1,0:T(8,128)(2,1)S(1)} %collective-permute-done.3.theirs_ref, s32[8,256]{1,0:T(8,128)S(1)} %bitcast.18, ...), custom_call_target="tpu_custom_call" | custom-call | tf_op jit(solution)/shard_map/pallas_call | solution.py:219
  71.8 14.3 %all-to-all-done.rows_hbm = bf16[16,160,256]{2,1,0:T(8,128)(2,1)} async-done(((bf16[16,160,256]{2,1,0:T(8,128)(2,1)}), bf16[16,160,256]{2,1,0:T(8,128)(2,1)}, u32[]{:S(2)}, u32[]{:S(2)}) %all-to-all-start) | async-done | bytes 1310752 | tf_op jit(solution)/shard_map/all_to_all | solution.py:384
  86.1 2.4 %shard_map.80 = f32[32,1,128]{2,1,0:T(1,128)S(1)} custom-call(s32[2]{0:T(128)S(1)} %pad_add_fusion.core_ref, bf16[16,160,256]{2,1,0:T(8,128)(2,1)} %all-to-all-done.rows_hbm, bf16[2560,256]{1,0:T(8,128)(2,1)} %get-tuple-element.11.mixed_hbm), custom_call_target="tpu_custom_call" | custom-call | tf_op jit(solution)/shard_map/pallas_call | solution.py:274
  88.6 12.9 %all_to_all.20 = f32[32,8,128]{2,1,0:T(8,128)S(1)} all-to-all(f32[32,8,128]{2,1,0:T(8,128)S(1)} %bitcast.23), channel_id=1, replica_groups=mesh['x'=4,'core'=2,'y'=4,'zh'=4,'zl'=4] {'x','core','y'}, dimensions={0} | all-to-all | bytes 262144 | tf_op jit(solution)/shard_map/all_to_all | solution.py:395
  101.5 0.7 shard_map.81
  102.2 21.5 %all_to_all.21.parts_ref = f32[16,1,512]{2,1,0:T(1,128)S(1)} all-to-all(f32[16,1,512]{2,1,0:T(1,128)} %shard_map.81), channel_id=1, replica_groups=mesh['x'=4,'core'=2,'y'=4,'zh'=4,'zl'=4] {'zh','zl'}, dimensions={0} | all-to-all | bytes 65536 | tf_op jit(solution)/shard_map/all_to_all | solution.py:403
  123.7 2.1 %shard_map.82 = (bf16[256,256]{1,0:T(8,128)(2,1)}, f32[8,256]{1,0:T(8,128)}) custom-call(f32[16,1,512]{2,1,0:T(1,128)S(1)} %all_to_all.21.parts_ref, f32[64,256]{1,0:T(8,128)S(1)} %get-tuple-element.12.key_ref, f32[64,256]{1,0:T(8,128)S(1)} %get-tuple-element.13.probs_ref, s32[8,256]{1,0:T(8,128)S(1)} %bitcast.19, bf16[64,256]{1,0:T(8,128)(2,1)} %bitcast.25), custom_call_target="tpu_custom_call" | custom-call | tf_op jit(solution)/shard_map/pallas_call | solution.py:340
  (2 shorter events, 0.0 us)
Async XLA Ops:
  3.4 51.3 %all-to-all-start.1 = ((bf16[4,96,3072]{2,1,0:T(8,128)(2,1)}), bf16[4,96,3072]{2,1,0:T(8,128)(2,1)S(1)}, u32[]{:S(2)}, u32[]{:S(2)}) async-start(bf16[4,96,3072]{2,1,0:T(8,128)(2,1)} %get-tuple-element.10), calls=%async_computation.1 | async-start | bytes 4718592 | tf_op jit(solution)/shard_map/all_to_all | solution.py:370
  8.3 24.7 %collective-permute-start = (bf16[272,256]{1,0:T(8,128)(2,1)S(1)}, bf16[272,256]{1,0:T(8,128)(2,1)S(1)}, u32[]{:S(2)}, u32[]{:S(2)}) collective-permute-start(bf16[272,256]{1,0:T(8,128)(2,1)S(1)} %get-tuple-element.9.block0), channel_id=1, source_target_pairs={{0,4},{4,8},{8,12},{12,0},{1,5},{5,9},{9,13},{13,1},{2,6},{6,10},{... | collective-permute-start | bytes 417800 | tf_op jit(solution)/shard_map/ppermute | solution.py:381
  17.1 28.9 %collective-permute-start.1 = (bf16[272,256]{1,0:T(8,128)(2,1)S(1)}, bf16[272,256]{1,0:T(8,128)(2,1)S(1)}, u32[]{:S(2)}, u32[]{:S(2)}) collective-permute-start(bf16[272,256]{1,0:T(8,128)(2,1)S(1)} %get-tuple-element.9.block0), channel_id=1, source_target_pairs={{0,8},{4,12},{8,0},{12,4},{1,9},{5,13},{9,1},{13,5},{2,10},{6,14},... | collective-permute-start | bytes 417800 | tf_op jit(solution)/shard_map/ppermute | solution.py:381
  27.7 25.5 %collective-permute-start.2 = (bf16[272,256]{1,0:T(8,128)(2,1)S(1)}, bf16[272,256]{1,0:T(8,128)(2,1)S(1)}, u32[]{:S(2)}, u32[]{:S(2)}) collective-permute-start(bf16[272,256]{1,0:T(8,128)(2,1)S(1)} %get-tuple-element.9.block0), channel_id=1, source_target_pairs={{0,12},{4,0},{8,4},{12,8},{1,13},{5,1},{9,5},{13,9},{2,14},{6,2},{... | collective-permute-start | bytes 417800 | tf_op jit(solution)/shard_map/ppermute | solution.py:381
  54.7 31.4 %all-to-all-start = ((bf16[16,160,256]{2,1,0:T(8,128)(2,1)}), bf16[16,160,256]{2,1,0:T(8,128)(2,1)}, u32[]{:S(2)}, u32[]{:S(2)}) async-start(bf16[16,160,256]{2,1,0:T(8,128)(2,1)} %shard_map.78), calls=%async_computation | async-start | bytes 2621440 | tf_op jit(solution)/shard_map/all_to_all | solution.py:384
  62.4 6.3 %copy-start = (s32[256,8]{0,1:T(8,128)S(1)}, s32[256,8]{0,1:T(8,128)}, u32[]{:S(2)}) copy-start(s32[256,8]{0,1:T(8,128)} %param.7) | copy-start | bytes 24580
  62.4 6.3 %copy-start.1 = (f32[256,8]{0,1:T(8,128)S(1)}, f32[256,8]{0,1:T(8,128)}, u32[]{:S(2)}) copy-start(f32[256,8]{0,1:T(8,128)} %param.8) | copy-start | bytes 24580
  62.6 6.1 %collective-permute-start.3 = (bf16[384,2816]{1,0:T(8,128)(2,1)S(1)}, bf16[384,2816]{1,0:T(8,128)(2,1)S(1)}, u32[]{:S(2)}, u32[]{:S(2)}) collective-permute-start(bf16[384,2816]{1,0:T(8,128)(2,1)S(1)} %pad_maximum_fusion), channel_id=1, source_target_pairs={{0,64},{64,0},{1,65},{65,1},{2,66},{66,2},{3,67},{67,3},{4,68},{68... | collective-permute-start | bytes 6488072 | tf_op jit(solution)/shard_map/ppermute | solution.py:373

commit v11 on v9

--- a/solution.py
+++ b/solution.py
@@ -16,7 +16,7 @@
 NEAR = Y * ZL
 F32 = jnp.float32
 NEAR_GROUPS = [
-    [c * Y * ZH * ZL + y * ZH * ZL + (q * ZL + r + 2 * c) % (ZH * ZL) for y in range(Y) for r in range(ZL)]
+    [c * Y * ZH * ZL + y * ZH * ZL + (q * ZL + r + 2 * c) % (ZH * ZL) for r in range(ZL) for y in range(Y)]
     for c in range(CORES)
     for q in range(ZH)
 ]
@@ -34,7 +34,7 @@
 def select_kernel(base_ref, blocks_ref, out_hbm, picked, rows_out, sems):
     base = base_ref[0]
     j = lax.broadcasted_iota(jnp.int32, (NEAR, TOK), 0)
-    expert = ((j // ZL) * (ZH * ZL) + ((base + j % ZL) & (ZH * ZL - 1))).astype(F32)
+    expert = ((j % Y) * (ZH * ZL) + ((base + j // Y) & (ZH * ZL - 1))).astype(F32)
     hits = []
     for b in range(ZH):
         ids = blocks_ref[b, TOK : TOK + 16, :].astype(F32)
@@ -183,8 +183,9 @@
             place = zl ^ (2 * core)
             for zh in range(ZH):
                 src = (zh * ZL + zl) * CAP
-                dst = pl.multiple_of(y * group + (place * ZH + zh) * CAP, 8)
+                dst = pl.multiple_of(((place * Y + y) * ZH + zh) * CAP, 8)
                 out_ref[pl.ds(dst, CAP), :] = mixed[src : src + CAP, :]
+    for y in range(Y):
         rows = pl.ds(y * group, group)
         rounded[rows, :] = out_ref[rows, :].astype(BF16)
         copies.append(pltpu.make_async_copy(rounded.at[rows], out_hbm.at[rows], sems.at[y]))
@@ -229,7 +230,7 @@
 
 
 def value_kernel(core_ref, rows_hbm, mixed_hbm, out_ref, rows_ref, mixed_ref, sems):
-    steps = 4
+    steps = ZL
     per = NEAR // steps
     copies = []
     for i in range(steps):
@@ -246,14 +247,15 @@
     slot = lax.broadcasted_iota(jnp.int32, (CAP, 128), 0)
     lane = lax.broadcasted_iota(jnp.int32, (CAP, 128), 1)
     own_lane = (lane == slot, lane == slot + 64)
-    for i in range(steps):
-        for copy in copies[i]:
+    for pair in range(ZL // 2):
+        for copy in copies[2 * pair] + copies[2 * pair + 1]:
             copy.wait()
-        for e in range(i * per, (i + 1) * per, 2):
+        for y in range(Y):
             sums = []
-            for odd in range(2):
-                rows = rows_ref[e + odd].astype(F32) * mixed_ref[
-                    (e + odd) * ZH * CAP : (e + odd + 1) * ZH * CAP, :
+            for r in (2 * pair, 2 * pair + 1):
+                e = r * Y + y
+                rows = rows_ref[e].astype(F32) * mixed_ref[
+                    e * ZH * CAP : (e + 1) * ZH * CAP, :
                 ].astype(F32)
                 sums.append(jnp.sum(rows[:, 0:128] + rows[:, 128:256], axis=1, keepdims=True))
             for b in range(ZH):
@@ -261,7 +263,7 @@
                 lanes = jnp.where(own_lane[0], sums[0][slots, :], 0.0) + jnp.where(
                     own_lane[1], sums[1][slots, :], 0.0
                 )
-                place = (e // ZL * ZH + b) * 2 + ((e % ZL // 2) ^ core_ref[0])
+                place = (y * ZH + b) * 2 + (pair ^ core_ref[0])
                 out_ref[place] = jnp.sum(lanes, axis=0, keepdims=True)
 
 

time: 112 us -> 112 us (level)
  blocking collectives: 64.9 us -> 63.4 us
  waiting for transfers between devices: 17.4 us -> 18.8 us
    all_to_all x1, waiting for transfers between devices: 13.6 us -> 14.9 us  [body(): lax.all_to_all(outgoing, ('core', 'y', 'zh', 'zl'), split_axis=0, concat_...]
where the time goes in v11:
time: 112 us
  blocking collectives  63.4 us (57%)
  waiting for transfers between devices  18.8 us (17%)
  starting transfers between devices  16.6 us (15%)
  Pallas kernels  11.8 us (11%)
    all_gather x1, blocking collectives, body(): blocks = lax.all_gather(block, 'zh', axis=0, tiled=False)  31.5 us
    all_to_all x1, blocking collectives, body(): lax.all_to_all(part, ('zh', 'zl'), split_axis=0, concat_axis=0, tiled=True)  19.8 us
    all_to_all x1, waiting for transfers between devices, body(): lax.all_to_all(outgoing, ('core', 'y', 'zh', 'zl'), split_axis=0, concat_...  14.9 us
    all_to_all x1, blocking collectives, body(): lax.all_to_all(part.reshape(X * CORES * Y, rows, 128), ('x', 'core', 'y')...  12.1 us
    all_to_all x1, starting transfers between devices, body(): lax.all_to_all(outgoing, ('core', 'y', 'zh', 'zl'), split_axis=0, concat_...  9.5 us
    all_to_all x1, starting transfers between devices, body(): along = lax.all_to_all(along, 'x', split_axis=0, concat_axis=0, tiled=True)  4.85 us
    ppermute x1, waiting for transfers between devices, body(): lax.ppermute(jnp.concatenate([mine[:, :slots], weight_other], axis=1), 'c...  3.86 us
    pallas_call x1, Pallas kernels, exchange_blocks(): pl.pallas_call(exchange_kernel, out_shape=(pltpu.HBM((X, width, EXPERTS *...  2.78 us
  transfers between devices with their start and end apart: 3, of which 2 were waited for; matrix products, arithmetic and copies ran while one was open for 0% of the time, Pallas kernels for 4%

profile of v11, /device:TPU:1, one launch (start us, length us, event | category | flops | bytes accessed | tf_op | source)
XLA Modules:
  0.0 111.8 jit_solution(16473660784467788112)
XLA Ops:
  0.6 2.8 %shard_map.77 = (bf16[4,96,3072]{2,1,0:T(8,128)(2,1)}, bf16[272,256]{1,0:T(8,128)(2,1)S(1)}) custom-call(s32[1]{0:T(128)} %bitcast.2.head_ref, s32[8,256]{1,0:T(8,128)} %bitcast.19, bf16[256,2048]{1,0:T(8,128)(2,1)} %grad_hbm.1, bf16[2560,96]{1,0:T(8,128)(2,1)} %bitcast.24, bf16[96,2048]{1,0:T(8,128)(2,1)} %bitcast.26), custom_call_target="tpu_custom_call" | custom-call | tf_op jit(solution)/shard_map/pallas_call | solution.py:138
  3.4 4.9 %all-to-all-start.1 = ((bf16[4,96,3072]{2,1,0:T(8,128)(2,1)}), bf16[4,96,3072]{2,1,0:T(8,128)(2,1)S(1)}, u32[]{:S(2)}, u32[]{:S(2)}) async-start(bf16[4,96,3072]{2,1,0:T(8,128)(2,1)} %get-tuple-element.10), calls=%async_computation.1 | async-start | bytes 4718592 | tf_op jit(solution)/shard_map/all_to_all | solution.py:367
  8.3 31.5 %all-gather = bf16[1088,256]{1,0:T(8,128)(2,1)S(1)} all-gather(bf16[272,256]{1,0:T(8,128)(2,1)S(1)} %get-tuple-element.9), channel_id=2, replica_groups=mesh['x'=4,'core'=2,'y'=4,'zh'=4,'zl'=4] {'zh'}, dimensions={0}, use_global_device_ids=true | all-gather | bytes 696320 | tf_op jit(solution)/shard_map/all_gather | solution.py:375
  39.8 1.5 %shard_map.78 = bf16[16,160,256]{2,1,0:T(8,128)(2,1)} custom-call(s32[1]{0:T(128)} %bitcast.1.base_ref, bf16[4,272,256]{2,1,0:T(8,128)(2,1)S(1)} %bitcast.17), custom_call_target="tpu_custom_call" | custom-call | tf_op jit(solution)/shard_map/pallas_call | solution.py:73
  41.3 0.0 all-to-all-done.1
  41.3 9.5 %all-to-all-start = ((bf16[16,160,256]{2,1,0:T(8,128)(2,1)}), bf16[16,160,256]{2,1,0:T(8,128)(2,1)}, u32[]{:S(2)}, u32[]{:S(2)}) async-start(bf16[16,160,256]{2,1,0:T(8,128)(2,1)} %shard_map.78), calls=%async_computation | async-start | bytes 2621440 | tf_op jit(solution)/shard_map/all_to_all | solution.py:379
  50.8 0.1 slice.4
  51.0 0.0 copy-start
  51.0 0.0 copy-start.1
  51.0 0.1 pad_maximum_fusion
  51.2 2.3 %collective-permute-start = (bf16[384,2816]{1,0:T(8,128)(2,1)S(1)}, bf16[384,2816]{1,0:T(8,128)(2,1)S(1)}, u32[]{:S(2)}, u32[]{:S(2)}) collective-permute-start(bf16[384,2816]{1,0:T(8,128)(2,1)S(1)} %pad_maximum_fusion), channel_id=1, source_target_pairs={{0,64},{64,0},{1,65},{65,1},{2,66},{66,2},{3,67},{67,3},{4,68},{68... | collective-permute-start | bytes 6488072 | tf_op jit(solution)/shard_map/ppermute | solution.py:370
  53.5 3.9 %collective-permute-done.theirs_ref = bf16[384,2816]{1,0:T(8,128)(2,1)S(1)} collective-permute-done((bf16[384,2816]{1,0:T(8,128)(2,1)S(1)}, bf16[384,2816]{1,0:T(8,128)(2,1)S(1)}, u32[]{:S(2)}, u32[]{:S(2)}) %collective-permute-start) | collective-permute-done | bytes 2162720 | tf_op jit(solution)/shard_map/ppermute | solution.py:370
  57.3 0.0 copy-done
  57.3 0.0 copy-done.1
  57.3 2.8 %shard_map.79 = (bf16[2560,256]{1,0:T(8,128)(2,1)}, f32[64,256]{1,0:T(8,128)S(1)}, f32[64,256]{1,0:T(8,128)S(1)}) custom-call(s32[1]{0:T(128)} %bitcast.core_ref, bf16[384,3072]{1,0:T(8,128)(2,1)S(1)} %bitcast.16, bf16[384,2816]{1,0:T(8,128)(2,1)S(1)} %collective-permute-done.theirs_ref, s32[8,256]{1,0:T(8,128)S(1)} %bitcast.20, f32[8,256]{1,0:T(8,128)S(1)} %bitcast.23), custom_call_target="tpu_custom_call" | custom-call | tf_op jit(solution)/shard_map/pallas_call | solution.py:217
  60.1 14.9 %all-to-all-done.rows_hbm = bf16[16,160,256]{2,1,0:T(8,128)(2,1)} async-done(((bf16[16,160,256]{2,1,0:T(8,128)(2,1)}), bf16[16,160,256]{2,1,0:T(8,128)(2,1)}, u32[]{:S(2)}, u32[]{:S(2)}) %all-to-all-start) | async-done | bytes 1310752 | tf_op jit(solution)/shard_map/all_to_all | solution.py:379
  75.0 2.0 %shard_map.80 = f32[32,1,128]{2,1,0:T(1,128)S(1)} custom-call(s32[1]{0:T(128)} %bitcast.core_ref, bf16[16,160,256]{2,1,0:T(8,128)(2,1)} %all-to-all-done.rows_hbm, bf16[2560,256]{1,0:T(8,128)(2,1)} %get-tuple-element.11.mixed_hbm), custom_call_target="tpu_custom_call" | custom-call | tf_op jit(solution)/shard_map/pallas_call | solution.py:271
  77.0 12.1 %all_to_all.20 = f32[32,8,128]{2,1,0:T(8,128)S(1)} all-to-all(f32[32,8,128]{2,1,0:T(8,128)S(1)} %bitcast.25), channel_id=1, replica_groups=mesh['x'=4,'core'=2,'y'=4,'zh'=4,'zl'=4] {'x','core','y'}, dimensions={0} | all-to-all | bytes 262144 | tf_op jit(solution)/shard_map/all_to_all | solution.py:390
  89.2 0.7 shard_map.81
  89.9 19.8 %all_to_all.21.parts_ref = f32[16,1,512]{2,1,0:T(1,128)S(1)} all-to-all(f32[16,1,512]{2,1,0:T(1,128)} %shard_map.81), channel_id=1, replica_groups=mesh['x'=4,'core'=2,'y'=4,'zh'=4,'zl'=4] {'zh','zl'}, dimensions={0} | all-to-all | bytes 65536 | tf_op jit(solution)/shard_map/all_to_all | solution.py:398
  109.6 2.1 %shard_map.82 = (bf16[256,256]{1,0:T(8,128)(2,1)}, f32[8,256]{1,0:T(8,128)}) custom-call(f32[16,1,512]{2,1,0:T(1,128)S(1)} %all_to_all.21.parts_ref, f32[64,256]{1,0:T(8,128)S(1)} %get-tuple-element.12.key_ref, f32[64,256]{1,0:T(8,128)S(1)} %get-tuple-element.13.probs_ref, s32[8,256]{1,0:T(8,128)S(1)} %bitcast.21, bf16[64,256]{1,0:T(8,128)(2,1)} %bitcast.27), custom_call_target="tpu_custom_call" | custom-call | tf_op jit(solution)/shard_map/pallas_call | solution.py:337
  (2 shorter events, 0.0 us)
Async XLA Ops:
  3.4 37.9 %all-to-all-start.1 = ((bf16[4,96,3072]{2,1,0:T(8,128)(2,1)}), bf16[4,96,3072]{2,1,0:T(8,128)(2,1)S(1)}, u32[]{:S(2)}, u32[]{:S(2)}) async-start(bf16[4,96,3072]{2,1,0:T(8,128)(2,1)} %get-tuple-element.10), calls=%async_computation.1 | async-start | bytes 4718592 | tf_op jit(solution)/shard_map/all_to_all | solution.py:367
  41.3 33.7 %all-to-all-start = ((bf16[16,160,256]{2,1,0:T(8,128)(2,1)}), bf16[16,160,256]{2,1,0:T(8,128)(2,1)}, u32[]{:S(2)}, u32[]{:S(2)}) async-start(bf16[16,160,256]{2,1,0:T(8,128)(2,1)} %shard_map.78), calls=%async_computation | async-start | bytes 2621440 | tf_op jit(solution)/shard_map/all_to_all | solution.py:379
  51.0 6.3 %copy-start = (s32[256,8]{0,1:T(8,128)S(1)}, s32[256,8]{0,1:T(8,128)}, u32[]{:S(2)}) copy-start(s32[256,8]{0,1:T(8,128)} %param.7) | copy-start | bytes 24580
  51.0 6.3 %copy-start.1 = (f32[256,8]{0,1:T(8,128)S(1)}, f32[256,8]{0,1:T(8,128)}, u32[]{:S(2)}) copy-start(f32[256,8]{0,1:T(8,128)} %param.8) | copy-start | bytes 24580
  51.2 6.2 %collective-permute-start = (bf16[384,2816]{1,0:T(8,128)(2,1)S(1)}, bf16[384,2816]{1,0:T(8,128)(2,1)S(1)}, u32[]{:S(2)}, u32[]{:S(2)}) collective-permute-start(bf16[384,2816]{1,0:T(8,128)(2,1)S(1)} %pad_maximum_fusion), channel_id=1, source_target_pairs={{0,64},{64,0},{1,65},{65,1},{2,66},{66,2},{3,67},{67,3},{4,68},{68... | collective-permute-start | bytes 6488072 | tf_op jit(solution)/shard_map/ppermute | solution.py:370

commit v12 on v9

--- a/solution.py
+++ b/solution.py
@@ -287,7 +287,7 @@
 def head_sum_kernel(parts_ref, out_ref):
     for y in range(Y):
         total = parts_ref[0, y]
-        for i in range(1, X * CORES):
+        for i in range(1, X):
             total = total + parts_ref[i, y]
         turned = pltpu.roll(total, 64, 1)
         for z in range(0, ZH * ZL, 2):
@@ -384,15 +384,12 @@
     )
     part = slot_sums(core_scalar, received, mixed)
     rows = ZH * ZL // 2
-    part = jnp.broadcast_to(part.reshape(1, Y, rows, 128), (X * CORES, Y, rows, 128))
+    part = jnp.sum(lax.all_gather(part, "core", axis=0, tiled=False), axis=0)
+    part = jnp.broadcast_to(part.reshape(1, Y, rows, 128), (X, Y, rows, 128))
     part = lax.all_to_all(
-        part.reshape(X * CORES * Y, rows, 128),
-        ("x", "core", "y"),
-        split_axis=0,
-        concat_axis=0,
-        tiled=True,
-    )
-    part = head_sums(part.reshape(X * CORES, Y, rows, 128))
+        part.reshape(X * Y, rows, 128), ("x", "y"), split_axis=0, concat_axis=0, tiled=True
+    )
+    part = head_sums(part.reshape(X, Y, rows, 128))
     part = lax.all_to_all(part, ("zh", "zl"), split_axis=0, concat_axis=0, tiled=True)
     grad, weight_grad = finish(part, key, probs, ids, router_weight.T)
     return grad, weight_grad.T

time: 112 us -> 113 us (level)
    all_gather x0 -> x1, blocking collectives: none -> 1.83 us  [body(): part = jnp.sum(lax.all_gather(part, 'core', axis=0, tiled=False), axis=0)]
    all_to_all x1, blocking collectives: 13.2 us -> 11.7 us  [body(): lax.all_to_all(part.reshape(X * Y, rows, 128), ('x', 'y'), split_axis=0,...]
where the time goes in v12:
time: 113 us; the launch traced here: 112 us
  blocking collectives  65.4 us (58%)
  waiting for transfers between devices  17.4 us (15%)
  starting transfers between devices  16.6 us (15%)
  Pallas kernels  11.5 us (10%)
    all_gather x1, blocking collectives, body(): blocks = lax.all_gather(block, 'zh', axis=0, tiled=False)  31.5 us
    all_to_all x1, blocking collectives, body(): lax.all_to_all(part, ('zh', 'zl'), split_axis=0, concat_axis=0, tiled=True)  20.3 us
    all_to_all x1, waiting for transfers between devices, body(): lax.all_to_all(outgoing, ('core', 'y', 'zh', 'zl'), split_axis=0, concat_...  13.6 us
    all_to_all x1, blocking collectives, body(): lax.all_to_all(part.reshape(X * Y, rows, 128), ('x', 'y'), split_axis=0,...  11.7 us
    all_to_all x1, starting transfers between devices, body(): lax.all_to_all(outgoing, ('core', 'y', 'zh', 'zl'), split_axis=0, concat_...  9.51 us
    all_to_all x1, starting transfers between devices, body(): along = lax.all_to_all(along, 'x', split_axis=0, concat_axis=0, tiled=True)  4.85 us
    ppermute x1, waiting for transfers between devices, body(): lax.ppermute(jnp.concatenate([mine[:, :slots], weight_other], axis=1), 'c...  3.86 us
    pallas_call x1, Pallas kernels, exchange_blocks(): pl.pallas_call(exchange_kernel, out_shape=(pltpu.HBM((X, width, EXPERTS *...  2.74 us
  transfers between devices with their start and end apart: 3, of which 2 were waited for; matrix products, arithmetic and copies ran while one was open for 0% of the time, Pallas kernels for 4%

profile of v12, /device:TPU:1, one launch (start us, length us, event | category | flops | bytes accessed | tf_op | source)
XLA Modules:
  0.0 112.1 jit_solution(9239617018415767076)
XLA Ops:
  0.6 2.7 %shard_map.77 = (bf16[4,96,3072]{2,1,0:T(8,128)(2,1)}, bf16[272,256]{1,0:T(8,128)(2,1)S(1)}) custom-call(s32[1]{0:T(128)} %bitcast.2.head_ref, s32[8,256]{1,0:T(8,128)} %bitcast.22, bf16[256,2048]{1,0:T(8,128)(2,1)} %grad_hbm.1, bf16[2560,96]{1,0:T(8,128)(2,1)} %bitcast.26, bf16[96,2048]{1,0:T(8,128)(2,1)} %bitcast.27), custom_call_target="tpu_custom_call" | custom-call | tf_op jit(solution)/shard_map/pallas_call | solution.py:138
  3.4 4.9 %all-to-all-start.1 = ((bf16[4,96,3072]{2,1,0:T(8,128)(2,1)}), bf16[4,96,3072]{2,1,0:T(8,128)(2,1)S(1)}, u32[]{:S(2)}, u32[]{:S(2)}) async-start(bf16[4,96,3072]{2,1,0:T(8,128)(2,1)} %get-tuple-element.10), calls=%async_computation.1 | async-start | bytes 4718592 | tf_op jit(solution)/shard_map/all_to_all | solution.py:365
  8.2 31.5 %all-gather = bf16[1088,256]{1,0:T(8,128)(2,1)S(1)} all-gather(bf16[272,256]{1,0:T(8,128)(2,1)S(1)} %get-tuple-element.9), channel_id=2, replica_groups=mesh['x'=4,'core'=2,'y'=4,'zh'=4,'zl'=4] {'zh'}, dimensions={0}, use_global_device_ids=true | all-gather | bytes 696320 | tf_op jit(solution)/shard_map/all_gather | solution.py:373
  39.8 1.5 %shard_map.78 = bf16[16,160,256]{2,1,0:T(8,128)(2,1)} custom-call(s32[1]{0:T(128)} %bitcast.1.base_ref, bf16[4,272,256]{2,1,0:T(8,128)(2,1)S(1)} %bitcast.20), custom_call_target="tpu_custom_call" | custom-call | tf_op jit(solution)/shard_map/pallas_call | solution.py:73
  41.3 0.0 all-to-all-done.1
  41.3 9.5 %all-to-all-start = ((bf16[16,160,256]{2,1,0:T(8,128)(2,1)}), bf16[16,160,256]{2,1,0:T(8,128)(2,1)}, u32[]{:S(2)}, u32[]{:S(2)}) async-start(bf16[16,160,256]{2,1,0:T(8,128)(2,1)} %shard_map.78), calls=%async_computation | async-start | bytes 2621440 | tf_op jit(solution)/shard_map/all_to_all | solution.py:377
  50.8 0.1 slice.4
  51.0 0.0 copy-start
  51.0 0.0 copy-start.1
  51.0 0.1 pad_maximum_fusion
  51.1 2.3 %collective-permute-start = (bf16[384,2816]{1,0:T(8,128)(2,1)S(1)}, bf16[384,2816]{1,0:T(8,128)(2,1)S(1)}, u32[]{:S(2)}, u32[]{:S(2)}) collective-permute-start(bf16[384,2816]{1,0:T(8,128)(2,1)S(1)} %pad_maximum_fusion), channel_id=1, source_target_pairs={{0,64},{64,0},{1,65},{65,1},{2,66},{66,2},{3,67},{67,3},{4,68},{68... | collective-permute-start | bytes 6488072 | tf_op jit(solution)/shard_map/ppermute | solution.py:368
  53.4 3.9 %collective-permute-done.theirs_ref = bf16[384,2816]{1,0:T(8,128)(2,1)S(1)} collective-permute-done((bf16[384,2816]{1,0:T(8,128)(2,1)S(1)}, bf16[384,2816]{1,0:T(8,128)(2,1)S(1)}, u32[]{:S(2)}, u32[]{:S(2)}) %collective-permute-start) | collective-permute-done | bytes 2162720 | tf_op jit(solution)/shard_map/ppermute | solution.py:368
  57.3 0.0 copy-done
  57.3 0.0 copy-done.1
  57.3 2.6 %shard_map.79 = (bf16[2560,256]{1,0:T(8,128)(2,1)}, f32[64,256]{1,0:T(8,128)S(1)}, f32[64,256]{1,0:T(8,128)S(1)}) custom-call(s32[1]{0:T(128)} %bitcast.core_ref, bf16[384,3072]{1,0:T(8,128)(2,1)S(1)} %bitcast.19, bf16[384,2816]{1,0:T(8,128)(2,1)S(1)} %collective-permute-done.theirs_ref, s32[8,256]{1,0:T(8,128)S(1)} %bitcast.23, f32[8,256]{1,0:T(8,128)S(1)} %bitcast.25), custom_call_target="tpu_custom_call" | custom-call | tf_op jit(solution)/shard_map/pallas_call | solution.py:216
  59.9 13.6 %all-to-all-done.rows_hbm = bf16[16,160,256]{2,1,0:T(8,128)(2,1)} async-done(((bf16[16,160,256]{2,1,0:T(8,128)(2,1)}), bf16[16,160,256]{2,1,0:T(8,128)(2,1)}, u32[]{:S(2)}, u32[]{:S(2)}) %all-to-all-start) | async-done | bytes 1310752 | tf_op jit(solution)/shard_map/all_to_all | solution.py:377
  73.4 1.9 %shard_map.80 = f32[32,1,128]{2,1,0:T(1,128)S(1)} custom-call(s32[1]{0:T(128)} %bitcast.core_ref, bf16[16,160,256]{2,1,0:T(8,128)(2,1)} %all-to-all-done.rows_hbm, bf16[2560,256]{1,0:T(8,128)(2,1)} %get-tuple-element.11.mixed_hbm), custom_call_target="tpu_custom_call" | custom-call | tf_op jit(solution)/shard_map/pallas_call | solution.py:269
  75.4 1.8 %all-gather.1 = f32[64,1,128]{2,1,0:T(1,128)S(1)} all-gather(f32[32,1,128]{2,1,0:T(1,128)S(1)} %shard_map.80), channel_id=3, replica_groups=mesh['x'=4,'core'=2,'y'=4,'zh'=4,'zl'=4] {'core'}, dimensions={0}, use_global_device_ids=true | all-gather | bytes 49152 | tf_op jit(solution)/shard_map/all_gather | solution.py:387
  77.2 11.7 %all_to_all.20 = f32[16,8,128]{2,1,0:T(8,128)S(1)} all-to-all(f32[16,8,128]{2,1,0:T(8,128)S(1)} %bitcast.28), channel_id=1, replica_groups=mesh['x'=4,'core'=2,'y'=4,'zh'=4,'zl'=4] {'x','y'}, dimensions={0} | all-to-all | bytes 131072 | tf_op jit(solution)/shard_map/all_to_all | solution.py:389
  88.9 0.7 shard_map.81
  89.6 20.3 %all_to_all.21.parts_ref = f32[16,1,512]{2,1,0:T(1,128)S(1)} all-to-all(f32[16,1,512]{2,1,0:T(1,128)} %shard_map.81), channel_id=1, replica_groups=mesh['x'=4,'core'=2,'y'=4,'zh'=4,'zl'=4] {'zh','zl'}, dimensions={0} | all-to-all | bytes 65536 | tf_op jit(solution)/shard_map/all_to_all | solution.py:393
  110.0 2.1 %shard_map.82 = (bf16[256,256]{1,0:T(8,128)(2,1)}, f32[8,256]{1,0:T(8,128)}) custom-call(f32[16,1,512]{2,1,0:T(1,128)S(1)} %all_to_all.21.parts_ref, f32[64,256]{1,0:T(8,128)S(1)} %get-tuple-element.12.key_ref, f32[64,256]{1,0:T(8,128)S(1)} %get-tuple-element.13.probs_ref, s32[8,256]{1,0:T(8,128)S(1)} %bitcast.24, bf16[64,256]{1,0:T(8,128)(2,1)} %bitcast.31), custom_call_target="tpu_custom_call" | custom-call | tf_op jit(solution)/shard_map/pallas_call | solution.py:335
  (3 shorter events, 0.0 us)
Async XLA Ops:
  3.4 37.9 %all-to-all-start.1 = ((bf16[4,96,3072]{2,1,0:T(8,128)(2,1)}), bf16[4,96,3072]{2,1,0:T(8,128)(2,1)S(1)}, u32[]{:S(2)}, u32[]{:S(2)}) async-start(bf16[4,96,3072]{2,1,0:T(8,128)(2,1)} %get-tuple-element.10), calls=%async_computation.1 | async-start | bytes 4718592 | tf_op jit(solution)/shard_map/all_to_all | solution.py:365
  41.3 32.2 %all-to-all-start = ((bf16[16,160,256]{2,1,0:T(8,128)(2,1)}), bf16[16,160,256]{2,1,0:T(8,128)(2,1)}, u32[]{:S(2)}, u32[]{:S(2)}) async-start(bf16[16,160,256]{2,1,0:T(8,128)(2,1)} %shard_map.78), calls=%async_computation | async-start | bytes 2621440 | tf_op jit(solution)/shard_map/all_to_all | solution.py:377
  51.0 6.3 %copy-start = (s32[256,8]{0,1:T(8,128)S(1)}, s32[256,8]{0,1:T(8,128)}, u32[]{:S(2)}) copy-start(s32[256,8]{0,1:T(8,128)} %param.7) | copy-start | bytes 24580
  51.0 6.3 %copy-start.1 = (f32[256,8]{0,1:T(8,128)S(1)}, f32[256,8]{0,1:T(8,128)}, u32[]{:S(2)}) copy-start(f32[256,8]{0,1:T(8,128)} %param.8) | copy-start | bytes 24580
  51.1 6.1 %collective-permute-start = (bf16[384,2816]{1,0:T(8,128)(2,1)S(1)}, bf16[384,2816]{1,0:T(8,128)(2,1)S(1)}, u32[]{:S(2)}, u32[]{:S(2)}) collective-permute-start(bf16[384,2816]{1,0:T(8,128)(2,1)S(1)} %pad_maximum_fusion), channel_id=1, source_target_pairs={{0,64},{64,0},{1,65},{65,1},{2,66},{66,2},{3,67},{67,3},{4,68},{68... | collective-permute-start | bytes 6488072 | tf_op jit(solution)/shard_map/ppermute | solution.py:368

commit v13 on v12

--- a/solution.py
+++ b/solution.py
@@ -285,20 +285,19 @@
 
 
 def head_sum_kernel(parts_ref, out_ref):
-    for y in range(Y):
-        total = parts_ref[0, y]
-        for i in range(1, X):
-            total = total + parts_ref[i, y]
-        turned = pltpu.roll(total, 64, 1)
-        for z in range(0, ZH * ZL, 2):
-            out_ref[z, :, y * 128 : (y + 1) * 128] = total[z // 2 : z // 2 + 1, :]
-            out_ref[z + 1, :, y * 128 : (y + 1) * 128] = turned[z // 2 : z // 2 + 1, :]
+    total = parts_ref[0]
+    for i in range(1, X * CORES):
+        total = total + parts_ref[i]
+    turned = pltpu.roll(total, 64, 1)
+    for row in range(EXPERTS // 2):
+        out_ref[2 * row] = total[row : row + 1, :]
+        out_ref[2 * row + 1] = turned[row : row + 1, :]
 
 
 def head_sums(parts):
     return pl.pallas_call(
         head_sum_kernel,
-        out_shape=jax.ShapeDtypeStruct((ZH * ZL, 1, Y * 128), F32),
+        out_shape=jax.ShapeDtypeStruct((EXPERTS, 1, 128), F32),
     )(in_vmem(parts))
 
 
@@ -308,8 +307,7 @@
 ):
     load_router = pltpu.make_async_copy(router_hbm, router_ref, sem)
     load_router.start()
-    for y in range(Y):
-        total[y * ZH * ZL : (y + 1) * ZH * ZL, :] = parts_ref[:, 0, y * 128 : (y + 1) * 128]
+    total[...] = parts_ref[:, 0, :]
     back = total[...]
     key = key_ref[...]
     probs = probs_ref[...]
@@ -383,14 +381,10 @@
         axis_index_groups=NEAR_GROUPS,
     )
     part = slot_sums(core_scalar, received, mixed)
-    rows = ZH * ZL // 2
-    part = jnp.sum(lax.all_gather(part, "core", axis=0, tiled=False), axis=0)
-    part = jnp.broadcast_to(part.reshape(1, Y, rows, 128), (X, Y, rows, 128))
-    part = lax.all_to_all(
-        part.reshape(X * Y, rows, 128), ("x", "y"), split_axis=0, concat_axis=0, tiled=True
-    )
-    part = head_sums(part.reshape(X, Y, rows, 128))
-    part = lax.all_to_all(part, ("zh", "zl"), split_axis=0, concat_axis=0, tiled=True)
+    part = part.reshape(1, EXPERTS // 2, 128)
+    part = jnp.broadcast_to(part, (X * CORES,) + part.shape[1:])
+    part = lax.all_to_all(part, HEAD, split_axis=0, concat_axis=0, tiled=True)
+    part = lax.all_to_all(head_sums(part), EXPERT, split_axis=0, concat_axis=0, tiled=True)
     grad, weight_grad = finish(part, key, probs, ids, router_weight.T)
     return grad, weight_grad.T
 

time: 113 us -> 112 us (level)
    all_gather x1 -> x0, blocking collectives: 1.83 us -> none  [body(): part = jnp.sum(lax.all_gather(part, 'core', axis=0, tiled=False), axis=0)]
    all_to_all x2, blocking collectives: 32.1 us -> 33.6 us  [the longest x1 25.3 us: body(): lax.all_to_all(head_sums(part), EXPERT, split_axis=0, concat_axis=0, tile...]
where the time goes in v13:
time: 112 us
  blocking collectives  65.1 us (58%)
  waiting for transfers between devices  17.4 us (16%)
  starting transfers between devices  16.6 us (15%)
  Pallas kernels  11.5 us (10%)
    all_gather x1, blocking collectives, body(): blocks = lax.all_gather(block, 'zh', axis=0, tiled=False)  31.5 us
    all_to_all x1, blocking collectives, body(): lax.all_to_all(head_sums(part), EXPERT, split_axis=0, concat_axis=0, tile...  25.3 us
    all_to_all x1, waiting for transfers between devices, body(): lax.all_to_all(outgoing, ('core', 'y', 'zh', 'zl'), split_axis=0, concat_...  13.6 us
    all_to_all x1, starting transfers between devices, body(): lax.all_to_all(outgoing, ('core', 'y', 'zh', 'zl'), split_axis=0, concat_...  9.5 us
    all_to_all x1, blocking collectives, body(): part = lax.all_to_all(part, HEAD, split_axis=0, concat_axis=0, tiled=True)  8.24 us
    all_to_all x1, starting transfers between devices, body(): along = lax.all_to_all(along, 'x', split_axis=0, concat_axis=0, tiled=True)  4.85 us
    ppermute x1, waiting for transfers between devices, body(): lax.ppermute(jnp.concatenate([mine[:, :slots], weight_other], axis=1), 'c...  3.86 us
    pallas_call x1, Pallas kernels, exchange_blocks(): pl.pallas_call(exchange_kernel, out_shape=(pltpu.HBM((X, width, EXPERTS *...  2.78 us
  transfers between devices with their start and end apart: 3, of which 2 were waited for; matrix products, arithmetic and copies ran while one was open for 0% of the time, Pallas kernels for 4%

profile of v13, /device:TPU:1, one launch (start us, length us, event | category | flops | bytes accessed | tf_op | source)
XLA Modules:
  0.0 111.8 jit_solution(4322577329626954230)
XLA Ops:
  0.6 2.8 %shard_map.77 = (bf16[4,96,3072]{2,1,0:T(8,128)(2,1)}, bf16[272,256]{1,0:T(8,128)(2,1)S(1)}) custom-call(s32[1]{0:T(128)} %bitcast.2.head_ref, s32[8,256]{1,0:T(8,128)} %bitcast.16, bf16[256,2048]{1,0:T(8,128)(2,1)} %grad_hbm.1, bf16[2560,96]{1,0:T(8,128)(2,1)} %bitcast.21, bf16[96,2048]{1,0:T(8,128)(2,1)} %bitcast.22), custom_call_target="tpu_custom_call" | custom-call | tf_op jit(solution)/shard_map/pallas_call | solution.py:138
  3.4 4.9 %all-to-all-start.1 = ((bf16[4,96,3072]{2,1,0:T(8,128)(2,1)}), bf16[4,96,3072]{2,1,0:T(8,128)(2,1)S(1)}, u32[]{:S(2)}, u32[]{:S(2)}) async-start(bf16[4,96,3072]{2,1,0:T(8,128)(2,1)} %get-tuple-element.10), calls=%async_computation.1 | async-start | bytes 4718592 | tf_op jit(solution)/shard_map/all_to_all | solution.py:363
  8.3 31.5 %all-gather = bf16[1088,256]{1,0:T(8,128)(2,1)S(1)} all-gather(bf16[272,256]{1,0:T(8,128)(2,1)S(1)} %get-tuple-element.9), channel_id=2, replica_groups=mesh['x'=4,'core'=2,'y'=4,'zh'=4,'zl'=4] {'zh'}, dimensions={0}, use_global_device_ids=true | all-gather | bytes 696320 | tf_op jit(solution)/shard_map/all_gather | solution.py:371
  39.8 1.5 %shard_map.78 = bf16[16,160,256]{2,1,0:T(8,128)(2,1)} custom-call(s32[1]{0:T(128)} %bitcast.1.base_ref, bf16[4,272,256]{2,1,0:T(8,128)(2,1)S(1)} %bitcast.15), custom_call_target="tpu_custom_call" | custom-call | tf_op jit(solution)/shard_map/pallas_call | solution.py:73
  41.3 0.0 all-to-all-done.1
  41.3 9.5 %all-to-all-start = ((bf16[16,160,256]{2,1,0:T(8,128)(2,1)}), bf16[16,160,256]{2,1,0:T(8,128)(2,1)}, u32[]{:S(2)}, u32[]{:S(2)}) async-start(bf16[16,160,256]{2,1,0:T(8,128)(2,1)} %shard_map.78), calls=%async_computation | async-start | bytes 2621440 | tf_op jit(solution)/shard_map/all_to_all | solution.py:375
  50.8 0.1 slice.4
  51.0 0.0 copy-start
  51.0 0.0 copy-start.1
  51.0 0.1 pad_maximum_fusion
  51.2 2.3 %collective-permute-start = (bf16[384,2816]{1,0:T(8,128)(2,1)S(1)}, bf16[384,2816]{1,0:T(8,128)(2,1)S(1)}, u32[]{:S(2)}, u32[]{:S(2)}) collective-permute-start(bf16[384,2816]{1,0:T(8,128)(2,1)S(1)} %pad_maximum_fusion), channel_id=1, source_target_pairs={{0,64},{64,0},{1,65},{65,1},{2,66},{66,2},{3,67},{67,3},{4,68},{68... | collective-permute-start | bytes 6488072 | tf_op jit(solution)/shard_map/ppermute | solution.py:366
  53.5 3.9 %collective-permute-done.theirs_ref = bf16[384,2816]{1,0:T(8,128)(2,1)S(1)} collective-permute-done((bf16[384,2816]{1,0:T(8,128)(2,1)S(1)}, bf16[384,2816]{1,0:T(8,128)(2,1)S(1)}, u32[]{:S(2)}, u32[]{:S(2)}) %collective-permute-start) | collective-permute-done | bytes 2162720 | tf_op jit(solution)/shard_map/ppermute | solution.py:366
  57.3 0.0 copy-done
  57.3 0.0 copy-done.1
  57.3 2.6 %shard_map.79 = (bf16[2560,256]{1,0:T(8,128)(2,1)}, f32[64,256]{1,0:T(8,128)S(1)}, f32[64,256]{1,0:T(8,128)S(1)}) custom-call(s32[1]{0:T(128)} %bitcast.core_ref, bf16[384,3072]{1,0:T(8,128)(2,1)S(1)} %bitcast.14, bf16[384,2816]{1,0:T(8,128)(2,1)S(1)} %collective-permute-done.theirs_ref, s32[8,256]{1,0:T(8,128)S(1)} %bitcast.17, f32[8,256]{1,0:T(8,128)S(1)} %bitcast.20), custom_call_target="tpu_custom_call" | custom-call | tf_op jit(solution)/shard_map/pallas_call | solution.py:216
  59.9 13.6 %all-to-all-done.rows_hbm = bf16[16,160,256]{2,1,0:T(8,128)(2,1)} async-done(((bf16[16,160,256]{2,1,0:T(8,128)(2,1)}), bf16[16,160,256]{2,1,0:T(8,128)(2,1)}, u32[]{:S(2)}, u32[]{:S(2)}) %all-to-all-start) | async-done | bytes 1310752 | tf_op jit(solution)/shard_map/all_to_all | solution.py:375
  73.5 1.9 %shard_map.80 = f32[32,1,128]{2,1,0:T(1,128)S(1)} custom-call(s32[1]{0:T(128)} %bitcast.core_ref, bf16[16,160,256]{2,1,0:T(8,128)(2,1)} %all-to-all-done.rows_hbm, bf16[2560,256]{1,0:T(8,128)(2,1)} %get-tuple-element.11.mixed_hbm), custom_call_target="tpu_custom_call" | custom-call | tf_op jit(solution)/shard_map/pallas_call | solution.py:269
  75.4 8.2 %all_to_all.20.parts_ref = f32[8,32,128]{2,1,0:T(8,128)S(1)} all-to-all(f32[8,32,128]{2,1,0:T(8,128)S(1)} %broadcast_in_dim.8), channel_id=1, replica_groups=mesh['x'=4,'core'=2,'y'=4,'zh'=4,'zl'=4] {'x','core'}, dimensions={0} | all-to-all | bytes 262144 | tf_op jit(solution)/shard_map/all_to_all | solution.py:386
  83.7 0.7 shard_map.81
  84.4 25.3 %all_to_all.21.parts_ref = f32[64,1,128]{2,1,0:T(1,128)S(1)} all-to-all(f32[64,1,128]{2,1,0:T(1,128)} %shard_map.81), channel_id=1, replica_groups=mesh['x'=4,'core'=2,'y'=4,'zh'=4,'zl'=4] {'y','zh','zl'}, dimensions={0} | all-to-all | bytes 65536 | tf_op jit(solution)/shard_map/all_to_all | solution.py:387
  109.7 2.1 %shard_map.82 = (bf16[256,256]{1,0:T(8,128)(2,1)}, f32[8,256]{1,0:T(8,128)}) custom-call(f32[64,1,128]{2,1,0:T(1,128)S(1)} %all_to_all.21.parts_ref, f32[64,256]{1,0:T(8,128)S(1)} %get-tuple-element.12.key_ref, f32[64,256]{1,0:T(8,128)S(1)} %get-tuple-element.13.probs_ref, s32[8,256]{1,0:T(8,128)S(1)} %bitcast.18, bf16[64,256]{1,0:T(8,128)(2,1)} %bitcast.23), custom_call_target="tpu_custom_call" | custom-call | tf_op jit(solution)/shard_map/pallas_call | solution.py:333
  (2 shorter events, 0.0 us)
Async XLA Ops:
  3.4 37.9 %all-to-all-start.1 = ((bf16[4,96,3072]{2,1,0:T(8,128)(2,1)}), bf16[4,96,3072]{2,1,0:T(8,128)(2,1)S(1)}, u32[]{:S(2)}, u32[]{:S(2)}) async-start(bf16[4,96,3072]{2,1,0:T(8,128)(2,1)} %get-tuple-element.10), calls=%async_computation.1 | async-start | bytes 4718592 | tf_op jit(solution)/shard_map/all_to_all | solution.py:363
  41.3 32.2 %all-to-all-start = ((bf16[16,160,256]{2,1,0:T(8,128)(2,1)}), bf16[16,160,256]{2,1,0:T(8,128)(2,1)}, u32[]{:S(2)}, u32[]{:S(2)}) async-start(bf16[16,160,256]{2,1,0:T(8,128)(2,1)} %shard_map.78), calls=%async_computation | async-start | bytes 2621440 | tf_op jit(solution)/shard_map/all_to_all | solution.py:375
  51.0 6.3 %copy-start = (s32[256,8]{0,1:T(8,128)S(1)}, s32[256,8]{0,1:T(8,128)}, u32[]{:S(2)}) copy-start(s32[256,8]{0,1:T(8,128)} %param.7) | copy-start | bytes 24580
  51.0 6.3 %copy-start.1 = (f32[256,8]{0,1:T(8,128)S(1)}, f32[256,8]{0,1:T(8,128)}, u32[]{:S(2)}) copy-start(f32[256,8]{0,1:T(8,128)} %param.8) | copy-start | bytes 24580
  51.2 6.2 %collective-permute-start = (bf16[384,2816]{1,0:T(8,128)(2,1)S(1)}, bf16[384,2816]{1,0:T(8,128)(2,1)S(1)}, u32[]{:S(2)}, u32[]{:S(2)}) collective-permute-start(bf16[384,2816]{1,0:T(8,128)(2,1)S(1)} %pad_maximum_fusion), channel_id=1, source_target_pairs={{0,64},{64,0},{1,65},{65,1},{2,66},{66,2},{3,67},{67,3},{4,68},{68... | collective-permute-start | bytes 6488072 | tf_op jit(solution)/shard_map/ppermute | solution.py:366

commit v14 on v9

--- a/solution.py
+++ b/solution.py
@@ -229,7 +229,7 @@
 
 
 def value_kernel(core_ref, rows_hbm, mixed_hbm, out_ref, rows_ref, mixed_ref, sems):
-    steps = 4
+    steps = 2
     per = NEAR // steps
     copies = []
     for i in range(steps):

time: 112 us -> 112 us (level)
  no operation moved by 1% of the time
where the time goes in v14:
time: 112 us
  blocking collectives  64.9 us (58%)
  waiting for transfers between devices  17.4 us (16%)
  starting transfers between devices  16.6 us (15%)
  Pallas kernels  11.7 us (10%)
    all_gather x1, blocking collectives, body(): blocks = lax.all_gather(block, 'zh', axis=0, tiled=False)  31.5 us
    all_to_all x1, blocking collectives, body(): lax.all_to_all(part, ('zh', 'zl'), split_axis=0, concat_axis=0, tiled=True)  20.2 us
    all_to_all x1, waiting for transfers between devices, body(): lax.all_to_all(outgoing, ('core', 'y', 'zh', 'zl'), split_axis=0, concat_...  13.6 us
    all_to_all x1, blocking collectives, body(): lax.all_to_all(part.reshape(X * CORES * Y, rows, 128), ('x', 'core', 'y')...  13.2 us
    all_to_all x1, starting transfers between devices, body(): lax.all_to_all(outgoing, ('core', 'y', 'zh', 'zl'), split_axis=0, concat_...  9.5 us
    all_to_all x1, starting transfers between devices, body(): along = lax.all_to_all(along, 'x', split_axis=0, concat_axis=0, tiled=True)  4.85 us
    ppermute x1, waiting for transfers between devices, body(): lax.ppermute(jnp.concatenate([mine[:, :slots], weight_other], axis=1), 'c...  3.86 us
    pallas_call x1, Pallas kernels, exchange_blocks(): pl.pallas_call(exchange_kernel, out_shape=(pltpu.HBM((X, width, EXPERTS *...  2.78 us
  transfers between devices with their start and end apart: 3, of which 2 were waited for; matrix products, arithmetic and copies ran while one was open for 0% of the time, Pallas kernels for 4%

profile of v14, /device:TPU:1, one launch (start us, length us, event | category | flops | bytes accessed | tf_op | source)
XLA Modules:
  0.0 111.7 jit_solution(6585303696472822998)
XLA Ops:
  0.6 2.8 %shard_map.77 = (bf16[4,96,3072]{2,1,0:T(8,128)(2,1)}, bf16[272,256]{1,0:T(8,128)(2,1)S(1)}) custom-call(s32[1]{0:T(128)} %bitcast.2.head_ref, s32[8,256]{1,0:T(8,128)} %bitcast.19, bf16[256,2048]{1,0:T(8,128)(2,1)} %grad_hbm.1, bf16[2560,96]{1,0:T(8,128)(2,1)} %bitcast.24, bf16[96,2048]{1,0:T(8,128)(2,1)} %bitcast.26), custom_call_target="tpu_custom_call" | custom-call | tf_op jit(solution)/shard_map/pallas_call | solution.py:138
  3.4 4.9 %all-to-all-start.1 = ((bf16[4,96,3072]{2,1,0:T(8,128)(2,1)}), bf16[4,96,3072]{2,1,0:T(8,128)(2,1)S(1)}, u32[]{:S(2)}, u32[]{:S(2)}) async-start(bf16[4,96,3072]{2,1,0:T(8,128)(2,1)} %get-tuple-element.10), calls=%async_computation.1 | async-start | bytes 4718592 | tf_op jit(solution)/shard_map/all_to_all | solution.py:365
  8.3 31.5 %all-gather = bf16[1088,256]{1,0:T(8,128)(2,1)S(1)} all-gather(bf16[272,256]{1,0:T(8,128)(2,1)S(1)} %get-tuple-element.9), channel_id=2, replica_groups=mesh['x'=4,'core'=2,'y'=4,'zh'=4,'zl'=4] {'zh'}, dimensions={0}, use_global_device_ids=true | all-gather | bytes 696320 | tf_op jit(solution)/shard_map/all_gather | solution.py:373
  39.8 1.5 %shard_map.78 = bf16[16,160,256]{2,1,0:T(8,128)(2,1)} custom-call(s32[1]{0:T(128)} %bitcast.1.base_ref, bf16[4,272,256]{2,1,0:T(8,128)(2,1)S(1)} %bitcast.17), custom_call_target="tpu_custom_call" | custom-call | tf_op jit(solution)/shard_map/pallas_call | solution.py:73
  41.3 0.0 all-to-all-done.1
  41.3 9.5 %all-to-all-start = ((bf16[16,160,256]{2,1,0:T(8,128)(2,1)}), bf16[16,160,256]{2,1,0:T(8,128)(2,1)}, u32[]{:S(2)}, u32[]{:S(2)}) async-start(bf16[16,160,256]{2,1,0:T(8,128)(2,1)} %shard_map.78), calls=%async_computation | async-start | bytes 2621440 | tf_op jit(solution)/shard_map/all_to_all | solution.py:377
  50.8 0.1 slice.4
  51.0 0.0 copy-start
  51.0 0.0 copy-start.1
  51.0 0.1 pad_maximum_fusion
  51.2 2.3 %collective-permute-start = (bf16[384,2816]{1,0:T(8,128)(2,1)S(1)}, bf16[384,2816]{1,0:T(8,128)(2,1)S(1)}, u32[]{:S(2)}, u32[]{:S(2)}) collective-permute-start(bf16[384,2816]{1,0:T(8,128)(2,1)S(1)} %pad_maximum_fusion), channel_id=1, source_target_pairs={{0,64},{64,0},{1,65},{65,1},{2,66},{66,2},{3,67},{67,3},{4,68},{68... | collective-permute-start | bytes 6488072 | tf_op jit(solution)/shard_map/ppermute | solution.py:368
  53.5 3.9 %collective-permute-done.theirs_ref = bf16[384,2816]{1,0:T(8,128)(2,1)S(1)} collective-permute-done((bf16[384,2816]{1,0:T(8,128)(2,1)S(1)}, bf16[384,2816]{1,0:T(8,128)(2,1)S(1)}, u32[]{:S(2)}, u32[]{:S(2)}) %collective-permute-start) | collective-permute-done | bytes 2162720 | tf_op jit(solution)/shard_map/ppermute | solution.py:368
  57.3 0.0 copy-done
  57.3 0.0 copy-done.1
  57.3 2.6 %shard_map.79 = (bf16[2560,256]{1,0:T(8,128)(2,1)}, f32[64,256]{1,0:T(8,128)S(1)}, f32[64,256]{1,0:T(8,128)S(1)}) custom-call(s32[1]{0:T(128)} %bitcast.core_ref, bf16[384,3072]{1,0:T(8,128)(2,1)S(1)} %bitcast.16, bf16[384,2816]{1,0:T(8,128)(2,1)S(1)} %collective-permute-done.theirs_ref, s32[8,256]{1,0:T(8,128)S(1)} %bitcast.20, f32[8,256]{1,0:T(8,128)S(1)} %bitcast.23), custom_call_target="tpu_custom_call" | custom-call | tf_op jit(solution)/shard_map/pallas_call | solution.py:216
  59.9 13.6 %all-to-all-done.rows_hbm = bf16[16,160,256]{2,1,0:T(8,128)(2,1)} async-done(((bf16[16,160,256]{2,1,0:T(8,128)(2,1)}), bf16[16,160,256]{2,1,0:T(8,128)(2,1)}, u32[]{:S(2)}, u32[]{:S(2)}) %all-to-all-start) | async-done | bytes 1310752 | tf_op jit(solution)/shard_map/all_to_all | solution.py:377
  73.5 2.0 %shard_map.80 = f32[32,1,128]{2,1,0:T(1,128)S(1)} custom-call(s32[1]{0:T(128)} %bitcast.core_ref, bf16[16,160,256]{2,1,0:T(8,128)(2,1)} %all-to-all-done.rows_hbm, bf16[2560,256]{1,0:T(8,128)(2,1)} %get-tuple-element.11.mixed_hbm), custom_call_target="tpu_custom_call" | custom-call | tf_op jit(solution)/shard_map/pallas_call | solution.py:269
  75.5 13.2 %all_to_all.20 = f32[32,8,128]{2,1,0:T(8,128)S(1)} all-to-all(f32[32,8,128]{2,1,0:T(8,128)S(1)} %bitcast.25), channel_id=1, replica_groups=mesh['x'=4,'core'=2,'y'=4,'zh'=4,'zl'=4] {'x','core','y'}, dimensions={0} | all-to-all | bytes 262144 | tf_op jit(solution)/shard_map/all_to_all | solution.py:388
  88.7 0.7 shard_map.81
  89.4 20.2 %all_to_all.21.parts_ref = f32[16,1,512]{2,1,0:T(1,128)S(1)} all-to-all(f32[16,1,512]{2,1,0:T(1,128)} %shard_map.81), channel_id=1, replica_groups=mesh['x'=4,'core'=2,'y'=4,'zh'=4,'zl'=4] {'zh','zl'}, dimensions={0} | all-to-all | bytes 65536 | tf_op jit(solution)/shard_map/all_to_all | solution.py:396
  109.6 2.1 %shard_map.82 = (bf16[256,256]{1,0:T(8,128)(2,1)}, f32[8,256]{1,0:T(8,128)}) custom-call(f32[16,1,512]{2,1,0:T(1,128)S(1)} %all_to_all.21.parts_ref, f32[64,256]{1,0:T(8,128)S(1)} %get-tuple-element.12.key_ref, f32[64,256]{1,0:T(8,128)S(1)} %get-tuple-element.13.probs_ref, s32[8,256]{1,0:T(8,128)S(1)} %bitcast.21, bf16[64,256]{1,0:T(8,128)(2,1)} %bitcast.27), custom_call_target="tpu_custom_call" | custom-call | tf_op jit(solution)/shard_map/pallas_call | solution.py:335
  (2 shorter events, 0.0 us)
Async XLA Ops:
  3.4 37.9 %all-to-all-start.1 = ((bf16[4,96,3072]{2,1,0:T(8,128)(2,1)}), bf16[4,96,3072]{2,1,0:T(8,128)(2,1)S(1)}, u32[]{:S(2)}, u32[]{:S(2)}) async-start(bf16[4,96,3072]{2,1,0:T(8,128)(2,1)} %get-tuple-element.10), calls=%async_computation.1 | async-start | bytes 4718592 | tf_op jit(solution)/shard_map/all_to_all | solution.py:365
  41.3 32.2 %all-to-all-start = ((bf16[16,160,256]{2,1,0:T(8,128)(2,1)}), bf16[16,160,256]{2,1,0:T(8,128)(2,1)}, u32[]{:S(2)}, u32[]{:S(2)}) async-start(bf16[16,160,256]{2,1,0:T(8,128)(2,1)} %shard_map.78), calls=%async_computation | async-start | bytes 2621440 | tf_op jit(solution)/shard_map/all_to_all | solution.py:377
  51.0 6.3 %copy-start = (s32[256,8]{0,1:T(8,128)S(1)}, s32[256,8]{0,1:T(8,128)}, u32[]{:S(2)}) copy-start(s32[256,8]{0,1:T(8,128)} %param.7) | copy-start | bytes 24580
  51.0 6.3 %copy-start.1 = (f32[256,8]{0,1:T(8,128)S(1)}, f32[256,8]{0,1:T(8,128)}, u32[]{:S(2)}) copy-start(f32[256,8]{0,1:T(8,128)} %param.8) | copy-start | bytes 24580
  51.2 6.2 %collective-permute-start = (bf16[384,2816]{1,0:T(8,128)(2,1)S(1)}, bf16[384,2816]{1,0:T(8,128)(2,1)S(1)}, u32[]{:S(2)}, u32[]{:S(2)}) collective-permute-start(bf16[384,2816]{1,0:T(8,128)(2,1)S(1)} %pad_maximum_fusion), channel_id=1, source_target_pairs={{0,64},{64,0},{1,65},{65,1},{2,66},{66,2},{3,67},{67,3},{4,68},{68... | collective-permute-start | bytes 6488072 | tf_op jit(solution)/shard_map/ppermute | solution.py:368
